TPU v7x, 256 devices: a whole 4x4x8 slice. The times are simulated.
256 devices in a mesh: context: 32 (over z_hi, x, core), tensor: 8 (over z_lo, y).
Axes of the slice: x: 4, y: 4, z: 8 (z_hi: 4, z_lo: 2; z = z_hi * 2 + z_lo), core: 2. Of those that a mesh axis runs over, the one named last changes fastest.
Arguments:
- grad_out: bfloat16 [4096, 8192], P('context'), may hold values from -6 to 6
- out_weight: bfloat16 [8192, 8192], P('tensor', 'context'), may hold values from -0.0625 to 0.0625
- query_proj: bfloat16 [4096, 8192], P('context', 'tensor'), may hold values from -6 to 6
- key_proj: bfloat16 [4096, 8192], P('context', 'tensor'), may hold values from -6 to 6
- value_proj: bfloat16 [4096, 8192], P('context', 'tensor'), may hold values from -6 to 6
- filter_taps: bfloat16 [4096, 8192], P('context', 'tensor')
- skip_gain: float32 [8192], P('tensor'), may hold values from 0.5 to 1.5
Outputs:
- grad_query: bfloat16 [4096, 8192], P('context', 'tensor')
- grad_key: bfloat16 [4096, 8192], P('context', 'tensor')
- grad_value: bfloat16 [4096, 8192], P('context', 'tensor')
- grad_filter: bfloat16 [4096, 8192], P('context', 'tensor')
- grad_weight: bfloat16 [8192, 8192], P('tensor', 'context')
All inputs are finite; a program needn't handle non-finite values.
Results may differ from a plain program's by a relative error of at most 0.0049.
Values may be sent and summed in bfloat16 or wider, within the bound.
No kernel may reach another device: no remote copies, remote signals or barrier semaphores. Data moves between devices by JAX's collectives and lax.ppermute only.
A program may use at most 128 MiB of HBM per device.

v0:
```python
import math

import jax
import jax.numpy as jnp
from jax import lax
from jax.sharding import PartitionSpec as P

highest = lax.Precision.HIGHEST


def angles(modulus, row_count, col_count):
    row_ids = jnp.arange(row_count)[:, None]
    col_ids = jnp.arange(col_count)[None, :]
    turns = row_ids * col_ids % modulus
    phase = turns.astype(jnp.float32) * (2.0 * math.pi / modulus)
    return (jnp.cos(phase), jnp.sin(phase))


def forward_dft(field):
    channels, length = field.shape
    inner = length // 64
    blocks = field.reshape(channels, 64, inner)
    outer_cos, outer_sin = angles(64, 64, 64)
    section_re = jnp.einsum("nab,ak->nkb", blocks, outer_cos, precision=highest)
    section_im = -jnp.einsum("nab,ak->nkb", blocks, outer_sin, precision=highest)
    twist_cos, twist_sin = angles(length, 64, inner)
    turned_re = section_re * twist_cos + section_im * twist_sin
    turned_im = section_im * twist_cos - section_re * twist_sin
    inner_cos, inner_sin = angles(inner, inner, inner)
    spec_re = jnp.einsum("nkb,bd->nkd", turned_re, inner_cos, precision=highest) + jnp.einsum(
        "nkb,bd->nkd", turned_im, inner_sin, precision=highest
    )
    spec_im = jnp.einsum("nkb,bd->nkd", turned_im, inner_cos, precision=highest) - jnp.einsum(
        "nkb,bd->nkd", turned_re, inner_sin, precision=highest
    )
    return (spec_re, spec_im)


def inverse_dft(spec_re, spec_im, keep):
    channels, outer, inner = spec_re.shape
    length = outer * inner
    inner_cos, inner_sin = angles(inner, inner, inner)
    back_re = jnp.einsum("nkd,db->nkb", spec_re, inner_cos, precision=highest) - jnp.einsum(
        "nkd,db->nkb", spec_im, inner_sin, precision=highest
    )
    back_im = jnp.einsum("nkd,db->nkb", spec_re, inner_sin, precision=highest) + jnp.einsum(
        "nkd,db->nkb", spec_im, inner_cos, precision=highest
    )
    twist_cos, twist_sin = angles(length, outer, inner)
    turned_re = back_re * twist_cos - back_im * twist_sin
    turned_im = back_re * twist_sin + back_im * twist_cos
    outer_cos, outer_sin = angles(outer, outer, outer)
    result = (
        jnp.einsum("nkb,ka->nab", turned_re, outer_cos, precision=highest)
        - jnp.einsum("nkb,ka->nab", turned_im, outer_sin, precision=highest)
    ) / length
    return result.reshape(channels, length)[:, :keep]


def shards(grad_out, out_weight, query_proj, key_proj, value_proj, filter_taps, skip_gain):
    tok_rows = grad_out.shape[0]
    context_size = lax.axis_size("context")
    seq_len = tok_rows * context_size
    group_width = out_weight.shape[0]
    owned = group_width // context_size
    norm_scale = 1.0 / math.sqrt(seq_len)
    contract_last = (((1,), (1,)), ((), ()))
    grad_cols = lax.all_to_all(grad_out, "context", split_axis=1, concat_axis=0, tiled=True)
    moved = (
        lax.all_to_all(query_proj, "context", split_axis=1, concat_axis=0, tiled=True),
        lax.all_to_all(key_proj, "context", split_axis=1, concat_axis=0, tiled=True),
        lax.all_to_all(value_proj, "context", split_axis=1, concat_axis=0, tiled=True),
        lax.all_to_all(filter_taps, "context", split_axis=1, concat_axis=0, tiled=True),
    )
    query_vals, key_vals, value_vals, taps_vals = [item.T.astype(jnp.float32) for item in moved]
    local_mix = lax.psum_scatter(
        lax.dot_general(grad_cols, out_weight, contract_last, preferred_element_type=jnp.float32),
        "context",
        scatter_dimension=0,
        tiled=True,
    )
    grad_mix = lax.all_to_all(local_mix, "context", split_axis=1, concat_axis=0, tiled=True).T
    skip_part = lax.dynamic_slice_in_dim(skip_gain, lax.axis_index("context") * owned, owned, 0)[
        :, None
    ]
    filt = taps_vals * norm_scale
    gated = key_vals * value_vals
    padding = ((0, 0), (0, seq_len))
    both_re, both_im = forward_dft(jnp.pad(jnp.concatenate([gated, filt], 0), padding))
    gated_re, filt_re = (both_re[:owned], both_re[owned:])
    gated_im, filt_im = (both_im[:owned], both_im[owned:])
    conv = inverse_dft(
        filt_re * gated_re - filt_im * gated_im, filt_re * gated_im + filt_im * gated_re, seq_len
    )
    total = conv + skip_part * gated
    mixed = (query_vals * total).astype(jnp.bfloat16)
    grad_query = (grad_mix * total).astype(jnp.bfloat16)
    gsig = grad_mix * query_vals
    gsig_re, gsig_im = forward_dft(jnp.pad(gsig, padding))
    corr_re = jnp.concatenate(
        [filt_re * gsig_re + filt_im * gsig_im, gated_re * gsig_re + gated_im * gsig_im], 0
    )
    corr_im = jnp.concatenate(
        [filt_re * gsig_im - filt_im * gsig_re, gated_re * gsig_im - gated_im * gsig_re], 0
    )
    corr = inverse_dft(corr_re, corr_im, seq_len)
    grad_gated = corr[:owned] + skip_part * gsig
    grad_taps = corr[owned:] * norm_scale
    outgoing = (
        grad_query.T,
        (grad_gated * value_vals).astype(jnp.bfloat16).T,
        (grad_gated * key_vals).astype(jnp.bfloat16).T,
        grad_taps.astype(jnp.bfloat16).T,
    )
    grad_q_out, grad_k_out, grad_v_out, grad_f_out = (
        lax.all_to_all(outgoing[0], "context", split_axis=0, concat_axis=1, tiled=True),
        lax.all_to_all(outgoing[1], "context", split_axis=0, concat_axis=1, tiled=True),
        lax.all_to_all(outgoing[2], "context", split_axis=0, concat_axis=1, tiled=True),
        lax.all_to_all(outgoing[3], "context", split_axis=0, concat_axis=1, tiled=True),
    )
    product = jnp.dot(
        lax.all_gather(mixed, "context", axis=0, tiled=True),
        grad_cols,
        preferred_element_type=jnp.float32,
    )
    grad_weight = (product * norm_scale).astype(jnp.bfloat16)
    return (grad_q_out, grad_k_out, grad_v_out, grad_f_out, grad_weight)


def solution(mesh):
    in_specs = (
        P("context", None),
        P("tensor", "context"),
        P("context", "tensor"),
        P("context", "tensor"),
        P("context", "tensor"),
        P("context", "tensor"),
        P("tensor"),
    )
    out_specs = (
        P("context", "tensor"),
        P("context", "tensor"),
        P("context", "tensor"),
        P("context", "tensor"),
        P("tensor", "context"),
    )
    return jax.shard_map(shards, mesh=mesh, in_specs=in_specs, out_specs=out_specs, check_vma=False)
```

profile of v0, /device:TPU:1, one launch (start us, length us, event | category | flops | bytes accessed | tf_op | source)
XLA Modules:
  0.0 421.9 jit_solution(12540600754884265640)
XLA Ops:
  7.2 3.3 copy.38
  10.5 62.7 %all_to_all.166 = bf16[128,32,256]{0,2,1:T(8,128)(2,1)} all-to-all(bf16[128,32,256]{0,2,1:T(8,128)(2,1)S(1)} %bitcast.264), channel_id=1, replica_groups=mesh['context'=32,'tensor'=8] {'context'}, dimensions={1} | all-to-all | bytes 4194304 | tf_op jit(solution)/shard_map/all_to_all | solution.py:68
  73.2 3.3 copy.39
  76.5 8.1 %fusion.246 = f32[4096,1024]{1,0:T(8,128)} fusion(bf16[4096,256]{1,0:T(8,128)(2,1)S(1)} %bitcast.261, bf16[1024,256]{1,0:T(8,128)(2,1)S(1)} %copy-done), kind=kOutput, calls=%fused_computation.266 | convolution fusion | flops 2147483648 | bytes 19398656 | tf_op jit(solution)/shard_map/dot_general | solution.py:77
  84.6 0.9 copy-done.15
  85.5 0.8 copy.46
  86.4 6.4 %all-to-all-start.4 = ((bf16[128,32,32]{0,2,1:T(8,128)(2,1)}), bf16[128,32,32]{0,2,1:T(8,128)(2,1)S(1)}, u32[]{:S(2)}, u32[]{:S(2)}) async-start(bf16[128,32,32]{0,2,1:T(8,128)(2,1)} %bitcast.13), calls=%async_computation.5 | async-start | bytes 524288 | tf_op jit(solution)/shard_map/all_to_all | solution.py:73
  92.8 0.8 copy.44
  93.6 12.3 %all-to-all-done.4 = bf16[128,32,32]{0,2,1:T(8,128)(2,1)S(1)} async-done(((bf16[128,32,32]{0,2,1:T(8,128)(2,1)}), bf16[128,32,32]{0,2,1:T(8,128)(2,1)S(1)}, u32[]{:S(2)}, u32[]{:S(2)}) %all-to-all-start.4) | async-done | bytes 262176 | tf_op jit(solution)/shard_map/all_to_all | solution.py:73
  105.9 4.4 %all-to-all-start.3 = ((bf16[128,32,32]{0,2,1:T(8,128)(2,1)}), bf16[128,32,32]{0,2,1:T(8,128)(2,1)S(1)}, u32[]{:S(2)}, u32[]{:S(2)}) async-start(bf16[128,32,32]{0,2,1:T(8,128)(2,1)} %bitcast.10), calls=%async_computation.4 | async-start | bytes 524288 | tf_op jit(solution)/shard_map/all_to_all | solution.py:72
  110.3 0.8 copy.49
  111.2 0.8 copy.42
  112.0 0.8 dynamic_slice.3
  112.9 10.2 %all-to-all-done.3 = bf16[128,32,32]{0,2,1:T(8,128)(2,1)S(1)} async-done(((bf16[128,32,32]{0,2,1:T(8,128)(2,1)}), bf16[128,32,32]{0,2,1:T(8,128)(2,1)S(1)}, u32[]{:S(2)}, u32[]{:S(2)}) %all-to-all-start.3) | async-done | bytes 262176 | tf_op jit(solution)/shard_map/all_to_all | solution.py:72
  123.2 4.3 %all-to-all-start.2 = ((bf16[128,32,32]{0,2,1:T(8,128)(2,1)}), bf16[128,32,32]{0,2,1:T(8,128)(2,1)S(1)}, u32[]{:S(2)}, u32[]{:S(2)}) async-start(bf16[128,32,32]{0,2,1:T(8,128)(2,1)} %bitcast.7), calls=%async_computation.3 | async-start | bytes 524288 | tf_op jit(solution)/shard_map/all_to_all | solution.py:71
  127.5 12.7 %all-to-all-done.2 = bf16[128,32,32]{0,2,1:T(8,128)(2,1)S(1)} async-done(((bf16[128,32,32]{0,2,1:T(8,128)(2,1)}), bf16[128,32,32]{0,2,1:T(8,128)(2,1)S(1)}, u32[]{:S(2)}, u32[]{:S(2)}) %all-to-all-start.2) | async-done | bytes 262176 | tf_op jit(solution)/shard_map/all_to_all | solution.py:71
  140.3 4.6 %all-to-all-start.6 = ((bf16[128,32,32]{0,2,1:T(8,128)(2,1)}), bf16[128,32,32]{0,2,1:T(8,128)(2,1)S(1)}, u32[]{:S(2)}, u32[]{:S(2)}) async-start(bf16[128,32,32]{0,2,1:T(8,128)(2,1)} %bitcast.25), calls=%async_computation.7 | async-start | bytes 524288 | tf_op jit(solution)/shard_map/all_to_all | solution.py:70
  144.9 0.8 copy-done.9
  146.3 2.1 fusion.108
  148.4 2.1 fusion.102
  150.5 1.4 copy-done.2
  151.9 3.5 fusion.1
  155.4 99.4 %reduce-scatter.2.cloned.1.call-done = f32[128,1024]{1,0:T(8,128)} async-done(((f32[4096,1024]{1,0:T(8,128)}), f32[128,1024]{1,0:T(8,128)}) %reduce-scatter.2.cloned.1.call-update) | async-done | bytes 524304 | tf_op jit(solution)/shard_map/reduce_scatter | solution.py:76
  254.8 2.0 copy.40
  256.8 7.9 %all-to-all-start.1 = ((f32[128,32,32]{0,2,1:T(8,128)}), f32[128,32,32]{0,2,1:T(8,128)S(1)}, u32[]{:S(2)}, u32[]{:S(2)}) async-start(f32[128,32,32]{0,2,1:T(8,128)} %bitcast.269), calls=%async_computation.2 | async-start | bytes 1048576 | tf_op jit(solution)/shard_map/all_to_all | solution.py:82
  265.2 3.9 fusion.3
  269.1 3.6 fusion.26
  272.7 3.5 fusion.23
  276.2 6.9 %all-to-all-done.1 = f32[128,32,32]{0,2,1:T(8,128)S(1)} async-done(((f32[128,32,32]{0,2,1:T(8,128)}), f32[128,32,32]{0,2,1:T(8,128)S(1)}, u32[]{:S(2)}, u32[]{:S(2)}) %all-to-all-start.1) | async-done | bytes 524320 | tf_op jit(solution)/shard_map/all_to_all | solution.py:82
  283.4 1.2 convolution_negate_fusion
  284.6 1.2 fusion.105
  285.7 1.2 fusion.37
  287.0 1.2 fusion.33
  288.2 1.4 convolution_add_fusion
  290.4 1.8 multiply_add_fusion.2
  292.2 2.1 fusion.17
  294.3 2.1 fusion.18
  296.4 1.2 fusion.76
  297.7 1.2 fusion.86
  298.9 2.1 fusion.22
  301.0 2.3 fusion.21
  303.3 2.1 fusion.9
  305.4 2.2 subtract_multiply_fusion
  307.6 1.2 copy.92
  308.8 1.2 convolution_add_fusion.1
  310.0 1.2 convolution_subtract_fusion.2
  311.3 1.2 fusion.46
  312.4 1.5 fusion.31
  315.1 1.1 fusion.67
  317.0 4.6 %all-to-all-start.5 = ((bf16[32,128,32]{1,2,0:T(8,128)(2,1)}), bf16[32,128,32]{1,2,0:T(8,128)(2,1)S(1)}, u32[]{:S(2)}, u32[]{:S(2)}) async-start(bf16[32,128,32]{1,2,0:T(8,128)(2,1)} %bitcast.256), calls=%async_computation.6 | async-start | bytes 524288 | tf_op jit(solution)/shard_map/all_to_all | solution.py:116
  322.4 12.7 %all-to-all-done.5 = bf16[32,128,32]{1,2,0:T(8,128)(2,1)S(1)} async-done(((bf16[32,128,32]{1,2,0:T(8,128)(2,1)}), bf16[32,128,32]{1,2,0:T(8,128)(2,1)S(1)}, u32[]{:S(2)}, u32[]{:S(2)}) %all-to-all-start.5) | async-done | bytes 262176 | tf_op jit(solution)/shard_map/all_to_all | solution.py:116
  335.1 6.5 %all-to-all-start.7 = ((bf16[32,128,32]{1,2,0:T(8,128)(2,1)}), bf16[32,128,32]{1,2,0:T(8,128)(2,1)S(1)}, u32[]{:S(2)}, u32[]{:S(2)}) async-start(bf16[32,128,32]{1,2,0:T(8,128)(2,1)} %bitcast.255), calls=%async_computation.8 | async-start | bytes 524288 | tf_op jit(solution)/shard_map/all_to_all | solution.py:117
  342.3 11.9 %all-to-all-done.7 = bf16[32,128,32]{1,2,0:T(8,128)(2,1)S(1)} async-done(((bf16[32,128,32]{1,2,0:T(8,128)(2,1)}), bf16[32,128,32]{1,2,0:T(8,128)(2,1)S(1)}, u32[]{:S(2)}, u32[]{:S(2)}) %all-to-all-start.7) | async-done | bytes 262176 | tf_op jit(solution)/shard_map/all_to_all | solution.py:117
  354.2 3.7 all-to-all-start.8
  357.9 0.8 copy.94
  358.7 18.5 %all-to-all-done.8 = bf16[32,128,32]{1,2,0:T(8,128)(2,1)S(1)} async-done(((bf16[32,128,32]{1,2,0:T(8,128)(2,1)}), bf16[32,128,32]{1,2,0:T(8,128)(2,1)S(1)}, u32[]{:S(2)}, u32[]{:S(2)}) %all-to-all-start.8) | async-done | bytes 262176 | tf_op jit(solution)/shard_map/all_to_all | solution.py:118
  377.2 5.4 %all-to-all-start.9 = ((bf16[32,128,32]{1,2,0:T(8,128)(2,1)}), bf16[32,128,32]{1,2,0:T(8,128)(2,1)S(1)}, u32[]{:S(2)}, u32[]{:S(2)}) async-start(bf16[32,128,32]{1,2,0:T(8,128)(2,1)} %bitcast.253), calls=%async_computation.10 | async-start | bytes 524288 | tf_op jit(solution)/shard_map/all_to_all | solution.py:119
  382.5 0.8 copy.54
  383.4 0.8 copy.55
  384.2 0.8 copy.56
  385.1 19.0 %all-to-all-done.9 = bf16[32,128,32]{1,2,0:T(8,128)(2,1)S(1)} async-done(((bf16[32,128,32]{1,2,0:T(8,128)(2,1)}), bf16[32,128,32]{1,2,0:T(8,128)(2,1)S(1)}, u32[]{:S(2)}, u32[]{:S(2)}) %all-to-all-start.9) | async-done | bytes 262176 | tf_op jit(solution)/shard_map/all_to_all | solution.py:119
  404.1 0.8 copy.57
  404.9 3.1 all-gather.2.cloned.1.call-done
  408.1 6.6 %fusion.32 = bf16[1024,256]{1,0:T(8,128)(2,1)} fusion(bf16[1024,4096]{1,0:T(8,128)(2,1)} %all-gather.2.cloned.1.call-done, bf16[4096,256]{1,0:T(8,128)(2,1)S(1)} %bitcast.262), kind=kOutput, calls=%fused_computation.41 | convolution fusion | flops 2148007936 | bytes 11010048 | tf_op jit(solution)/shard_map/dot_general | solution.py:121
  (52 shorter events, 5.9 us)
Async XLA Ops:
  7.2 69.3 %copy-start = (bf16[1024,256]{1,0:T(8,128)(2,1)S(1)}, bf16[1024,256]{1,0:T(8,128)(2,1)}, u32[]{:S(2)}) copy-start(bf16[1024,256]{1,0:T(8,128)(2,1)} %param.8) | copy-start | bytes 1572868
  7.2 247.6 %reduce-scatter.2.cloned.1.call-start = ((), (), s32[]{:S(2)}) async-start(), calls=%async_computation.11 | async-start | bytes 17301504 | tf_op jit(solution)/shard_map/reduce_scatter | solution.py:76
  76.4 8.2 %copy-start.4 = (bf16[32,128,256]{2,1,0:T(8,128)(2,1)}, bf16[32,128,256]{2,1,0:T(8,128)(2,1)S(1)}, u32[]{:S(2)}) copy-start(bf16[32,128,256]{2,1,0:T(8,128)(2,1)S(1)} %copy.39) | copy-start | bytes 6291460
  84.6 1.0 copy-start.15
  84.6 8.2 %copy-start.16 = (bf16[128,1024]{1,0:T(8,128)(2,1)S(1)}, bf16[128,1024]{1,0:T(8,128)(2,1)}, u32[]{:S(2)}) copy-start(bf16[128,1024]{1,0:T(8,128)(2,1)} %param.11) | copy-start | bytes 786436
  85.5 24.8 %copy-start.17 = (bf16[128,1024]{1,0:T(8,128)(2,1)S(1)}, bf16[128,1024]{1,0:T(8,128)(2,1)}, u32[]{:S(2)}) copy-start(bf16[128,1024]{1,0:T(8,128)(2,1)} %param.9) | copy-start | bytes 786436
  85.5 25.6 %copy-start.18 = (bf16[128,1024]{1,0:T(8,128)(2,1)S(1)}, bf16[128,1024]{1,0:T(8,128)(2,1)}, u32[]{:S(2)}) copy-start(bf16[128,1024]{1,0:T(8,128)(2,1)} %param.10) | copy-start | bytes 786436
  86.4 19.5 %all-to-all-start.4 = ((bf16[128,32,32]{0,2,1:T(8,128)(2,1)}), bf16[128,32,32]{0,2,1:T(8,128)(2,1)S(1)}, u32[]{:S(2)}, u32[]{:S(2)}) async-start(bf16[128,32,32]{0,2,1:T(8,128)(2,1)} %bitcast.13), calls=%async_computation.5 | async-start | bytes 524288 | tf_op jit(solution)/shard_map/all_to_all | solution.py:73
  105.9 17.2 %all-to-all-start.3 = ((bf16[128,32,32]{0,2,1:T(8,128)(2,1)}), bf16[128,32,32]{0,2,1:T(8,128)(2,1)S(1)}, u32[]{:S(2)}, u32[]{:S(2)}) async-start(bf16[128,32,32]{0,2,1:T(8,128)(2,1)} %bitcast.10), calls=%async_computation.4 | async-start | bytes 524288 | tf_op jit(solution)/shard_map/all_to_all | solution.py:72
  123.1 22.7 %copy-start.11 = (bf16[128,32,32]{0,2,1:T(8,128)(2,1)}, bf16[128,32,32]{0,2,1:T(8,128)(2,1)S(1)}, u32[]{:S(2)}) copy-start(bf16[128,32,32]{0,2,1:T(8,128)(2,1)S(1)} %all-to-all-done.3) | copy-start | bytes 786436
  123.2 17.1 %all-to-all-start.2 = ((bf16[128,32,32]{0,2,1:T(8,128)(2,1)}), bf16[128,32,32]{0,2,1:T(8,128)(2,1)S(1)}, u32[]{:S(2)}, u32[]{:S(2)}) async-start(bf16[128,32,32]{0,2,1:T(8,128)(2,1)} %bitcast.7), calls=%async_computation.3 | async-start | bytes 524288 | tf_op jit(solution)/shard_map/all_to_all | solution.py:71
  140.3 5.6 %copy-start.13 = (bf16[128,32,32]{0,2,1:T(8,128)(2,1)}, bf16[128,32,32]{0,2,1:T(8,128)(2,1)S(1)}, u32[]{:S(2)}) copy-start(bf16[128,32,32]{0,2,1:T(8,128)(2,1)S(1)} %all-to-all-done.2) | copy-start | bytes 786436
  140.3 116.5 %all-to-all-start.6 = ((bf16[128,32,32]{0,2,1:T(8,128)(2,1)}), bf16[128,32,32]{0,2,1:T(8,128)(2,1)S(1)}, u32[]{:S(2)}, u32[]{:S(2)}) async-start(bf16[128,32,32]{0,2,1:T(8,128)(2,1)} %bitcast.25), calls=%async_computation.7 | async-start | bytes 524288 | tf_op jit(solution)/shard_map/all_to_all | solution.py:70
  144.9 0.8 copy-start.9
  150.5 1.4 copy-start.2
  256.8 26.3 %all-to-all-start.1 = ((f32[128,32,32]{0,2,1:T(8,128)}), f32[128,32,32]{0,2,1:T(8,128)S(1)}, u32[]{:S(2)}, u32[]{:S(2)}) async-start(f32[128,32,32]{0,2,1:T(8,128)} %bitcast.269), calls=%async_computation.2 | async-start | bytes 1048576 | tf_op jit(solution)/shard_map/all_to_all | solution.py:82
  264.7 143.4 %all-gather.2.cloned.1.call-start = ((), (), s32[]{:S(2)}) async-start(), calls=%async_computation.12 | async-start | bytes 8650752 | tf_op jit(solution)/shard_map/all_gather | solution.py:122
  265.2 4.0 copy-start.3
  265.2 4.0 copy-start.6
  288.2 1.6 copy-start.7
  288.2 2.2 copy-start.8
  313.9 1.0 copy-start.10
  313.9 1.1 copy-start.12
  314.0 1.2 copy-start.14
  317.0 18.1 %all-to-all-start.5 = ((bf16[32,128,32]{1,2,0:T(8,128)(2,1)}), bf16[32,128,32]{1,2,0:T(8,128)(2,1)S(1)}, u32[]{:S(2)}, u32[]{:S(2)}) async-start(bf16[32,128,32]{1,2,0:T(8,128)(2,1)} %bitcast.256), calls=%async_computation.6 | async-start | bytes 524288 | tf_op jit(solution)/shard_map/all_to_all | solution.py:116
  335.1 19.2 %all-to-all-start.7 = ((bf16[32,128,32]{1,2,0:T(8,128)(2,1)}), bf16[32,128,32]{1,2,0:T(8,128)(2,1)S(1)}, u32[]{:S(2)}, u32[]{:S(2)}) async-start(bf16[32,128,32]{1,2,0:T(8,128)(2,1)} %bitcast.255), calls=%async_computation.8 | async-start | bytes 524288 | tf_op jit(solution)/shard_map/all_to_all | solution.py:117
  341.5 66.5 %copy-start.5 = (bf16[32,128,256]{2,1,0:T(8,128)(2,1)S(1)}, bf16[32,128,256]{2,1,0:T(8,128)(2,1)}, u32[]{:S(2)}) copy-start(bf16[32,128,256]{2,1,0:T(8,128)(2,1)} %copy-done.4) | copy-start | bytes 6291460
  354.2 22.9 %all-to-all-start.8 = ((bf16[32,128,32]{1,2,0:T(8,128)(2,1)}), bf16[32,128,32]{1,2,0:T(8,128)(2,1)S(1)}, u32[]{:S(2)}, u32[]{:S(2)}) async-start(bf16[32,128,32]{1,2,0:T(8,128)(2,1)} %bitcast.254), calls=%async_computation.9 | async-start | bytes 524288 | tf_op jit(solution)/shard_map/all_to_all | solution.py:118
  377.2 26.9 %all-to-all-start.9 = ((bf16[32,128,32]{1,2,0:T(8,128)(2,1)}), bf16[32,128,32]{1,2,0:T(8,128)(2,1)S(1)}, u32[]{:S(2)}, u32[]{:S(2)}) async-start(bf16[32,128,32]{1,2,0:T(8,128)(2,1)} %bitcast.253), calls=%async_computation.10 | async-start | bytes 524288 | tf_op jit(solution)/shard_map/all_to_all | solution.py:119
  408.1 6.6 %copy-start.1 = (bf16[1024,256]{1,0:T(8,128)(2,1)S(1)}, bf16[1024,256]{1,0:T(8,128)(2,1)}, u32[]{:S(2)}) copy-start(bf16[1024,256]{1,0:T(8,128)(2,1)} %param.8) | copy-start | bytes 1572868
Sparse Core Ops, SparseCore 0:
  84.7 169.9 reduce-scatter.1
  316.4 91.6 all-gather.1
where the time goes:
time: 428 us; the launch traced here: 422 us
  waiting for transfers between devices  207 us (48%)
  blocking collectives  62.7 us (15%)
  matrix products  61.7 us (14%)
  starting transfers between devices  48.2 us (11%)
  local copies, waits for them, and re-layouts  26 us (6%)
  between operations  15 us (4%)
    reduce_scatter x1, waiting for transfers between devices, shards(): lax.psum_scatter(lax.dot_general(grad_cols, out_weight, contract_last, pr...  99.4 us
    all_to_all x1, blocking collectives, shards(): lax.all_to_all(grad_out, 'context', split_axis=1, concat_axis=0, tiled=True)  62.7 us
    all_to_all x1, waiting for transfers between devices, shards(): lax.all_to_all(outgoing[3], 'context', split_axis=0, concat_axis=1, tiled...  19 us
    all_to_all x1, waiting for transfers between devices, shards(): lax.all_to_all(outgoing[2], 'context', split_axis=0, concat_axis=1, tiled...  18.5 us
    unnamed x52, local copies, waits for them, and re-layouts  17 us
    all_to_all x1, waiting for transfers between devices, shards(): lax.all_to_all(key_proj, 'context', split_axis=1, concat_axis=0, tiled=True)  12.7 us
    all_to_all x1, waiting for transfers between devices, shards(): lax.all_to_all(outgoing[0], 'context', split_axis=0, concat_axis=1, tiled...  12.7 us
    all_to_all x1, waiting for transfers between devices, shards(): lax.all_to_all(filter_taps, 'context', split_axis=1, concat_axis=0, tiled...  12.3 us
  transfers between devices with their start and end apart: 11, of which 10 were waited for; matrix products, arithmetic and copies ran while one was open for 8% of the time, Pallas kernels for 0%

commit v1 on v0

v1 whole, which is shorter than its diff:
```python
import functools
import math

import jax
import jax.numpy as jnp
import numpy as np
from jax import lax
from jax.experimental import pallas as pl
from jax.experimental.pallas import tpu as pltpu
from jax.sharding import Mesh
from jax.sharding import PartitionSpec as P

bf16 = jnp.bfloat16
f32 = jnp.float32
CTX = ("zh", "x", "core")
TEN = ("zl", "y")
VMEM_LIMIT = 48 * 1024 * 1024

OUTER, INNER = 64, 128
KEPT = OUTER // 2 + 1
HALF = OUTER // 2
GROUP = 16


def split_const(value):
    high = value.astype(np.float32).astype(bf16)
    low = (value - high.astype(np.float64)).astype(np.float32).astype(bf16)
    return np.stack([np.asarray(high), np.asarray(low)])


@functools.cache
def tables(seq_len):
    length = 2 * seq_len
    i = np.arange(HALF)
    k = np.arange(KEPT)
    turn = 2.0 * np.pi * np.outer(k, i) / OUTER
    rows = np.concatenate([np.cos(turn), -np.sin(turn)[1:HALF]], 0)
    first = split_const(np.kron(rows, np.eye(8)))
    weight = np.where((k == 0) | (k == HALF), 1.0, 2.0)[:, None]
    back = np.concatenate([weight * np.cos(turn), -(weight * np.sin(turn))[1:HALF]], 0).T
    last = split_const(np.kron(back / (length * math.sqrt(seq_len)), np.eye(8)))
    b = np.arange(INNER)
    twist = 2.0 * np.pi * np.outer(k, b) / length
    twist = np.stack([np.cos(twist), np.sin(twist)]).astype(np.float32)
    inner = 2.0 * np.pi * np.outer(b, b) / INNER
    c, s = np.cos(inner), np.sin(inner)
    ahead = split_const(np.block([[c, -s], [s, c]]))
    behind = split_const(np.block([[c, s], [-s, c]]))
    return first, twist, ahead, behind, last


def dot(a, b):
    return jnp.dot(a, b, preferred_element_type=f32)


def split(x):
    high = x.astype(bf16)
    return high, (x - high.astype(f32)).astype(bf16)


def forward(field, first_ref, twist_ref, ahead_ref):
    packed = jnp.concatenate(
        [field[:, 8 * g : 8 * g + 8].reshape(8 * HALF, INNER) for g in range(2)], 1
    ).astype(bf16)
    mixed = dot(first_ref[0], packed) + dot(first_ref[1], packed)
    halves = [mixed[:, INNER * g : INNER * (g + 1)].reshape(OUTER, 8, INNER) for g in range(2)]
    both = jnp.concatenate(halves, 1)
    zero = jnp.zeros((1, GROUP, INNER), f32)
    re = both[:KEPT]
    im = jnp.concatenate([zero, both[KEPT:], zero], 0)
    cos, sin = twist_ref[0][:, None, :], twist_ref[1][:, None, :]
    turned = jnp.concatenate([re * cos + im * sin, im * cos - re * sin], 2)
    high, low = split(turned.reshape(KEPT * GROUP, 2 * INNER))
    spec = dot(high, ahead_ref[0]) + (dot(low, ahead_ref[0]) + dot(high, ahead_ref[1]))
    return spec[:, :INNER], spec[:, INNER:]


def backward(re, im, twist_ref, behind_ref, last_ref):
    high, low = split(jnp.concatenate([re, im], 1))
    turned = dot(high, behind_ref[0]) + (dot(low, behind_ref[0]) + dot(high, behind_ref[1]))
    re = turned[:, :INNER].reshape(KEPT, GROUP, INNER)
    im = turned[:, INNER:].reshape(KEPT, GROUP, INNER)
    cos, sin = twist_ref[0][:, None, :], twist_ref[1][:, None, :]
    rows = jnp.concatenate([re * cos - im * sin, (re * sin + im * cos)[1:HALF]], 0)
    packed = jnp.concatenate(
        [rows[:, 8 * g : 8 * g + 8].reshape(8 * OUTER, INNER) for g in range(2)], 1
    )
    high, low = split(packed)
    field = dot(last_ref[0], high) + (dot(last_ref[0], low) + dot(last_ref[1], high))
    return jnp.concatenate(
        [field[:, INNER * g : INNER * (g + 1)].reshape(HALF, 8, INNER) for g in range(2)], 1
    )


def conv_kernel(
    fields_ref, skip_ref, first_ref, twist_ref, ahead_ref, behind_ref, last_ref, total_ref, spec_ref
):
    gated = fields_ref[:, 0].astype(f32)
    taps = fields_ref[:, 1].astype(f32)
    gated_re, gated_im = forward(gated, first_ref, twist_ref, ahead_ref)
    taps_re, taps_im = forward(taps, first_ref, twist_ref, ahead_ref)
    for place, part in enumerate((gated_re, gated_im, taps_re, taps_im)):
        spec_ref[place, 0] = part
    conv = backward(
        taps_re * gated_re - taps_im * gated_im,
        taps_re * gated_im + taps_im * gated_re,
        twist_ref,
        behind_ref,
        last_ref,
    )
    total_ref[...] = (conv + skip_ref[...][None] * gated).astype(bf16)


def corr_kernel(
    gsig_ref, spec_ref, skip_ref, first_ref, twist_ref, ahead_ref, behind_ref, last_ref, out_ref
):
    gsig = gsig_ref[...].astype(f32)
    gsig_re, gsig_im = forward(gsig, first_ref, twist_ref, ahead_ref)
    gated_re, gated_im, taps_re, taps_im = [spec_ref[place, 0] for place in range(4)]
    grad_gated = backward(
        taps_re * gsig_re + taps_im * gsig_im,
        taps_re * gsig_im - taps_im * gsig_re,
        twist_ref,
        behind_ref,
        last_ref,
    )
    out_ref[:, 0] = (grad_gated + skip_ref[...][None] * gsig).astype(bf16)
    grad_taps = backward(
        gated_re * gsig_re + gated_im * gsig_im,
        gated_re * gsig_im - gated_im * gsig_re,
        twist_ref,
        behind_ref,
        last_ref,
    )
    out_ref[:, 1] = grad_taps.astype(bf16)


def whole(array):
    rank = array.ndim
    return pl.BlockSpec(array.shape, lambda g: (0,) * rank)


def conv_call(fields, skip_rows, consts):
    blocks, _, owned, inner = fields.shape
    steps = owned // GROUP
    spec_rows = KEPT * GROUP
    return pl.pallas_call(
        conv_kernel,
        grid=(steps,),
        in_specs=[
            pl.BlockSpec((blocks, 2, GROUP, inner), lambda g: (0, 0, g, 0)),
            pl.BlockSpec((GROUP, inner), lambda g: (g, 0)),
        ]
        + [whole(item) for item in consts],
        out_specs=[
            pl.BlockSpec((blocks, GROUP, inner), lambda g: (0, g, 0)),
            pl.BlockSpec((4, 1, spec_rows, inner), lambda g: (0, g, 0, 0)),
        ],
        out_shape=[
            jax.ShapeDtypeStruct((blocks, owned, inner), bf16),
            jax.ShapeDtypeStruct((4, steps, spec_rows, inner), f32),
        ],
        compiler_params=pltpu.CompilerParams(vmem_limit_bytes=VMEM_LIMIT),
        cost_estimate=pl.CostEstimate(flops=10**9, bytes_accessed=6 * 2**20, transcendentals=0),
        name="conv",
    )(fields, skip_rows, *consts)


def corr_call(gsig, spec, skip_rows, consts):
    blocks, owned, inner = gsig.shape
    steps = owned // GROUP
    spec_rows = KEPT * GROUP
    return pl.pallas_call(
        corr_kernel,
        grid=(steps,),
        in_specs=[
            pl.BlockSpec((blocks, GROUP, inner), lambda g: (0, g, 0)),
            pl.BlockSpec((4, 1, spec_rows, inner), lambda g: (0, g, 0, 0)),
            pl.BlockSpec((GROUP, inner), lambda g: (g, 0)),
        ]
        + [whole(item) for item in consts],
        out_specs=pl.BlockSpec((blocks, 2, GROUP, inner), lambda g: (0, 0, g, 0)),
        out_shape=jax.ShapeDtypeStruct((blocks, 2, owned, inner), bf16),
        compiler_params=pltpu.CompilerParams(vmem_limit_bytes=VMEM_LIMIT),
        cost_estimate=pl.CostEstimate(flops=10**9, bytes_accessed=6 * 2**20, transcendentals=0),
        name="corr",
    )(gsig, spec, skip_rows, *consts)


def pick_kernel(place_ref, in_ref, out_ref):
    out_ref[0] = in_ref[...]


def pick_blocks(grad_out, places, width):
    rows = grad_out.shape[0]
    count = places.shape[0]
    return pl.pallas_call(
        pick_kernel,
        grid_spec=pltpu.PrefetchScalarGridSpec(
            num_scalar_prefetch=1,
            grid=(count,),
            in_specs=[pl.BlockSpec((rows, width), lambda n, place_ref: (0, place_ref[n]))],
            out_specs=pl.BlockSpec((1, rows, width), lambda n, place_ref: (n, 0, 0)),
        ),
        out_shape=jax.ShapeDtypeStruct((count, rows, width), grad_out.dtype),
        cost_estimate=pl.CostEstimate(flops=0, bytes_accessed=2**20, transcendentals=0),
        name="pick",
    )(places, grad_out)


def mix_kernel(*refs):
    weights, grads, outs = refs[:8], refs[8:12], refs[12:]
    step = 256
    for pair in range(2):
        lines = [
            jnp.concatenate([grads[2 * pair + n][r] for r in range(8)], 1) for n in range(2)
        ]
        grad = jnp.concatenate(lines, 0)

        def body(m, _, grad=grad, pair=pair):
            here = pl.ds(pl.multiple_of(m * step, step), step)
            weight = jnp.concatenate([w[here, :] for w in weights], 1)
            part = lax.dot_general(
                weight, grad, (((1,), (1,)), ((), ())), preferred_element_type=f32
            )
            for n in range(2):
                out = outs[2 * pair + n]
                out[here, :] = part[:, INNER * n : INNER * (n + 1)].astype(out.dtype)
            return 0

        lax.fori_loop(0, weights[0].shape[0] // step, body, 0)


def mix_call(weights, grads):
    rows = weights[0].shape[0]
    toks = grads[0].shape[1]
    kinds = (f32, bf16, bf16, bf16)
    return pl.pallas_call(
        mix_kernel,
        out_shape=[jax.ShapeDtypeStruct((rows, toks), kind) for kind in kinds],
        compiler_params=pltpu.CompilerParams(vmem_limit_bytes=VMEM_LIMIT),
        cost_estimate=pl.CostEstimate(
            flops=2 * rows * toks * 4 * 2048, bytes_accessed=8 * 2**20, transcendentals=0
        ),
        name="mix",
    )(*weights, *grads)


def ring(size, shift):
    return [(n, (n + shift) % size) for n in range(size)]


def shards(grad_out, out_weight, query_proj, key_proj, value_proj, filter_taps, skip_gain):
    tok_rows = grad_out.shape[0]
    context_size = lax.axis_size(CTX)
    size_z, size_x = lax.axis_size("zh"), lax.axis_size("x")
    seq_len = tok_rows * context_size
    group_width, width = out_weight.shape
    owned = group_width // context_size
    norm_scale = 1.0 / math.sqrt(seq_len)
    my_z, my_x, my_core = (lax.axis_index(name) for name in CTX)
    consts = [jnp.asarray(item) for item in tables(seq_len)]

    def swap(item):
        return lax.ppermute(item, "core", [(0, 1), (1, 0)])

    def shift_z(item, by):
        return lax.ppermute(item, "zh", ring(size_z, by % size_z)) if by % size_z else item

    def shift_x(item, by):
        return lax.ppermute(item, "x", ring(size_x, by % size_x)) if by % size_x else item

    def to_all(item):
        return lax.all_to_all(item, CTX, split_axis=0, concat_axis=0, tiled=True)

    gated = (key_proj.astype(f32) * value_proj.astype(f32)).astype(bf16)
    fields = jnp.stack(
        [
            gated.T.reshape(context_size, owned, tok_rows),
            filter_taps.T.reshape(context_size, owned, tok_rows),
        ],
        1,
    )
    fields = to_all(fields)

    order = (0, 1, 3, 2)
    grads = {}
    for s in order:
        places = jnp.stack(
            [
                ((my_z - r) % size_z * size_x + (my_x + s) % size_x) * 2 + (my_core + rc) % 2
                for rc in range(2)
                for r in range(size_z)
            ]
        ).astype(jnp.int32)
        grads[s] = shift_x(pick_blocks(grad_out, places, width), s)
    weights = {r: shift_z(out_weight, r) for r in order}
    weights_far = {r: swap(weights[r]) for r in order}

    skip_rows = lax.dynamic_slice_in_dim(
        skip_gain, lax.axis_index(CTX) * owned, owned, 0
    )
    skip_rows = jnp.broadcast_to(skip_rows[:, None], (owned, tok_rows))
    total, spec = conv_call(fields, skip_rows, consts)
    total = to_all(total).reshape(group_width, tok_rows)
    query_t = query_proj.T
    mixed = (query_t.astype(f32) * total.astype(f32)).astype(bf16)

    parts = mix_call(
        [weights[r] for r in range(size_z)] + [weights_far[r] for r in range(size_z)],
        [grads[s] for s in range(size_x)],
    )
    grad_mix = parts[0]
    for s in order[1:]:
        grad_mix = grad_mix + shift_x(parts[s], -s).astype(f32)
    gsig = (grad_mix * query_t.astype(f32)).astype(bf16)
    grad_query = (grad_mix * total.astype(f32)).astype(bf16).T
    gsig = to_all(gsig.reshape(context_size, owned, tok_rows))
    corr = to_all(corr_call(gsig, spec, skip_rows, consts))
    grad_gated = corr[:, 0].reshape(group_width, tok_rows).T
    grad_filter = corr[:, 1].reshape(group_width, tok_rows).T
    grad_key = (grad_gated.astype(f32) * value_proj.astype(f32)).astype(bf16)
    grad_value = (grad_gated.astype(f32) * key_proj.astype(f32)).astype(bf16)

    lines = [shift_x(mixed, s) for s in range(size_x)]
    lines = jnp.concatenate(lines, 1)
    lines = jnp.concatenate([lines, swap(lines)], 1)
    far = [swap(grads[s][size_z:]) for s in range(size_x)]
    grad_weight = None
    for r in order[::-1]:
        columns = jnp.concatenate(
            [grads[s][r] for s in range(size_x)] + [far[s][r] for s in range(size_x)], 0
        )
        product = dot(lines, columns)
        if r:
            product = shift_z(product.astype(bf16), -r).astype(f32)
        grad_weight = product if grad_weight is None else grad_weight + product
    grad_weight = (grad_weight * norm_scale).astype(bf16)
    return (grad_query, grad_key, grad_value, grad_filter, grad_weight)


def solution(mesh):
    fine = Mesh(mesh.devices.reshape(4, 4, 2, 2, 4), CTX + TEN)
    rows_cols = P(CTX, TEN)
    in_specs = (P(CTX, None), P(TEN, CTX)) + (rows_cols,) * 4 + (P(TEN),)
    out_specs = (rows_cols,) * 4 + (P(TEN, CTX),)
    return jax.shard_map(
        shards, mesh=fine, in_specs=in_specs, out_specs=out_specs, check_vma=False
    )
```

time: 428 us -> 261 us (0.61)
  waiting for transfers between devices: 207 us -> 77.8 us
  blocking collectives: 62.7 us -> 0 us
  matrix products: 61.7 us -> 12.6 us
  Pallas kernels: 0 us -> 38.6 us
  starting transfers between devices: 48.2 us -> 81.4 us
  local copies, waits for them, and re-layouts: 26 us -> 40.2 us
  between operations: 15 us -> 1 us
  other arithmetic: 1.58 us -> 6.39 us
    all_to_all x9 -> x4, waiting for transfers between devices: 104 us -> 2.63 us  [to_all(): return lax.all_to_all(item, CTX, split_axis=0, concat_axis=0, tiled=True)]
    reduce_scatter x1 -> x0, waiting for transfers between devices: 99.4 us -> none  [shards(): lax.psum_scatter(lax.dot_general(grad_cols, out_weight, contract_last, pr...]
    ppermute x0 -> x24, waiting for transfers between devices: none -> 75.1 us  [the longest x6 59.8 us: shift_z(): lax.ppermute(item, 'zh', ring(size_z, by % size_z))]
    all_to_all x1 -> x0, blocking collectives: 62.7 us -> none  [shards(): lax.all_to_all(grad_out, 'context', split_axis=1, concat_axis=0, tiled=True)]
    dot_general x26 -> x4, matrix products: 61.7 us -> 12.6 us  [dot(): return jnp.dot(a, b, preferred_element_type=f32)]
    ppermute x0 -> x24, starting transfers between devices: none -> 40.2 us  [the longest x6 16.3 us: shift_z(): lax.ppermute(item, 'zh', ring(size_z, by % size_z))]
    pallas_call x0 -> x7, Pallas kernels: none -> 38.6 us  [the longest x4 21.8 us: pick_blocks(): pl.pallas_call(pick_kernel, grid_spec=pltpu.PrefetchScalarGridSpec(num_sc...]
    unnamed x52 -> x67, local copies, waits for them, and re-layouts: 17 us -> 25.6 us
  transfers between devices with their start and end apart: 11 -> 28, of which waited for: 10 -> 10; matrix products, arithmetic and copies ran while one was open for 8% -> 18% of each run, Pallas kernels for 0% -> 15%
where the time goes in v1:
time: 261 us; the launch traced here: 258 us
  starting transfers between devices  81.4 us (31%)
  waiting for transfers between devices  77.8 us (30%)
  local copies, waits for them, and re-layouts  40.2 us (15%)
  Pallas kernels  38.6 us (15%)
  matrix products  12.6 us (5%)
  other arithmetic  6.39 us (2%)
    ppermute x6, waiting for transfers between devices, shift_z(): lax.ppermute(item, 'zh', ring(size_z, by % size_z))  59.8 us
    all_to_all x4, starting transfers between devices, to_all(): return lax.all_to_all(item, CTX, split_axis=0, concat_axis=0, tiled=True)  41.2 us
    unnamed x67, local copies, waits for them, and re-layouts  25.6 us
    pallas_call x4, Pallas kernels, pick_blocks(): pl.pallas_call(pick_kernel, grid_spec=pltpu.PrefetchScalarGridSpec(num_sc...  21.8 us
    ppermute x6, starting transfers between devices, shift_z(): lax.ppermute(item, 'zh', ring(size_z, by % size_z))  16.3 us
    ppermute x9, waiting for transfers between devices, shift_x(): lax.ppermute(item, 'x', ring(size_x, by % size_x))  15.3 us
    dot_general x4, matrix products, dot(): return jnp.dot(a, b, preferred_element_type=f32)  12.6 us
    ppermute x9, starting transfers between devices, shift_x(): lax.ppermute(item, 'x', ring(size_x, by % size_x))  12.4 us
  transfers between devices with their start and end apart: 28, of which 10 were waited for; matrix products, arithmetic and copies ran while one was open for 18% of the time, Pallas kernels for 15%

profile of v1, /device:TPU:1, one launch (start us, length us, event | category | flops | bytes accessed | tf_op | source)
XLA Modules:
  0.0 258.0 jit_solution(11519571551953962381)
XLA Ops:
  0.6 1.1 copy.18
  1.8 1.1 fusion.7
  3.9 12.6 %all-to-all-start = ((bf16[32,2,32,128]{3,2,1,0:T(8,128)(2,1)}), bf16[32,2,32,128]{3,2,1,0:T(8,128)(2,1)S(1)}, u32[]{:S(2)}, u32[]{:S(2)}) async-start(bf16[32,2,32,128]{3,2,1,0:T(8,128)(2,1)} %pad_maximum_fusion.1), calls=%async_computation | async-start | bytes 1048576 | tf_op jit(solution)/shard_map/all_to_all | solution.py:274
  17.2 5.4 %pick.6 = bf16[8,128,256]{2,1,0:T(8,128)(2,1)} custom-call(s32[8]{0:T(128)} %stack.137.place_ref, bf16[128,8192]{1,0:T(8,128)(2,1)} %in_ref.7), custom_call_target="tpu_custom_call" | custom-call | bytes 1048576 | tf_op jit(solution)/shard_map/pick/pallas_call | solution.py:197
  22.6 2.9 %collective-permute-start.8 = (bf16[8,128,256]{2,1,0:T(8,128)(2,1)}, bf16[8,128,256]{2,1,0:T(8,128)(2,1)S(1)}, u32[]{:S(2)}, u32[]{:S(2)}) collective-permute-start(bf16[8,128,256]{2,1,0:T(8,128)(2,1)} %pick.6), channel_id=1, source_target_pairs={{0,32},{16,48},{32,0},{48,16},{1,33},{17,49},{33,1},{49,17},{2,34}... | collective-permute-start | bytes 1572872 | tf_op jit(solution)/shard_map/ppermute | solution.py:271
  26.1 5.5 %pick.7 = bf16[8,128,256]{2,1,0:T(8,128)(2,1)} custom-call(s32[8]{0:T(128)} %stack.146.place_ref, bf16[128,8192]{1,0:T(8,128)(2,1)} %in_ref.7), custom_call_target="tpu_custom_call" | custom-call | bytes 1048576 | tf_op jit(solution)/shard_map/pick/pallas_call | solution.py:197
  32.5 3.4 %collective-permute-start.2 = (bf16[1024,256]{1,0:T(8,128)(2,1)}, bf16[1024,256]{1,0:T(8,128)(2,1)}, u32[]{:S(2)}, u32[]{:S(2)}) collective-permute-start(bf16[1024,256]{1,0:T(8,128)(2,1)} %refs_0_.1), channel_id=1, source_target_pairs={{0,192},{64,0},{128,64},{192,128},{1,193},{65,1},{129,65},{193,129... | collective-permute-start | bytes 1572872 | tf_op jit(solution)/shard_map/ppermute | solution.py:268
  35.9 2.0 collective-permute-start.1
  37.9 2.1 collective-permute-start
  40.6 5.4 %pick.5 = bf16[8,128,256]{2,1,0:T(8,128)(2,1)} custom-call(s32[8]{0:T(128)} %stack.128.place_ref, bf16[128,8192]{1,0:T(8,128)(2,1)} %in_ref.7), custom_call_target="tpu_custom_call" | custom-call | bytes 1048576 | tf_op jit(solution)/shard_map/pick/pallas_call | solution.py:197
  46.0 1.8 collective-permute-start.3
  47.8 3.6 %collective-permute-done.9.refs_11_ = bf16[8,128,256]{2,1,0:T(8,128)(2,1)S(1)} collective-permute-done((bf16[8,128,256]{2,1,0:T(8,128)(2,1)}, bf16[8,128,256]{2,1,0:T(8,128)(2,1)S(1)}, u32[]{:S(2)}, u32[]{:S(2)}) %collective-permute-start.9) | collective-permute-done | bytes 524320 | tf_op jit(solution)/shard_map/ppermute | solution.py:271
  51.4 1.8 collective-permute-start.7
  53.2 16.1 %collective-permute-done.2.refs_3_ = bf16[1024,256]{1,0:T(8,128)(2,1)} collective-permute-done((bf16[1024,256]{1,0:T(8,128)(2,1)}, bf16[1024,256]{1,0:T(8,128)(2,1)}, u32[]{:S(2)}, u32[]{:S(2)}) %collective-permute-start.2) | collective-permute-done | bytes 524320 | tf_op jit(solution)/shard_map/ppermute | solution.py:268
  69.3 1.0 collective-permute-start.6
  70.3 3.7 %collective-permute-done.refs_1_ = bf16[1024,256]{1,0:T(8,128)(2,1)} collective-permute-done((bf16[1024,256]{1,0:T(8,128)(2,1)}, bf16[1024,256]{1,0:T(8,128)(2,1)}, u32[]{:S(2)}, u32[]{:S(2)}) %collective-permute-start) | collective-permute-done | bytes 524320 | tf_op jit(solution)/shard_map/ppermute | solution.py:268
  74.0 1.6 collective-permute-start.4
  77.1 5.5 %pick.4.refs_8_ = bf16[8,128,256]{2,1,0:T(8,128)(2,1)} custom-call(s32[8]{0:T(128)} %stack.119.place_ref, bf16[128,8192]{1,0:T(8,128)(2,1)} %in_ref.7), custom_call_target="tpu_custom_call" | custom-call | bytes 1048576 | tf_op jit(solution)/shard_map/pick/pallas_call | solution.py:197
  82.6 1.7 slice.158
  85.0 1.6 constant_dynamic-update-slice_fusion.12
  88.3 1.0 copy-done.2
  89.3 1.0 copy-done.6
  90.4 0.9 copy-done.8
  91.3 4.9 %conv.1 = (bf16[32,32,128]{2,1,0:T(8,128)(2,1)S(1)}, f32[4,2,528,128]{3,2,1,0:T(8,128)S(1)}) custom-call(bf16[32,2,32,128]{3,2,1,0:T(8,128)(2,1)S(1)} %copy-done.6, f32[32,128]{1,0:T(8,128)S(1)} %broadcast_in_dim.2.skip_ref, bf16[2,512,256]{2,1,0:T(8,128)(2,1)S(1)} %copy-done.2, f32[2,33,128]{2,1,0:T(8,128)S(1)} %copy-done.11, ...), custom_call_target="tpu_custom_call" | custom-call | flops 1000000000 | bytes 6291456 | tf_op jit(solution)/shard_map/conv/pallas_call | solution.py:147
  96.9 14.0 %all-to-all-start.1 = ((bf16[32,32,128]{2,1,0:T(8,128)(2,1)}), bf16[32,32,128]{2,1,0:T(8,128)(2,1)}, u32[]{:S(2)}, u32[]{:S(2)}) async-start(bf16[32,32,128]{2,1,0:T(8,128)(2,1)} %copy-done.10), calls=%async_computation.1 | async-start | bytes 524288 | tf_op jit(solution)/shard_map/all_to_all | solution.py:274
  111.6 6.4 %mix.1 = (f32[1024,128]{1,0:T(8,128)S(1)}, bf16[1024,128]{1,0:T(8,128)(2,1)S(1)}, bf16[1024,128]{1,0:T(8,128)(2,1)S(1)}, bf16[1024,128]{1,0:T(8,128)(2,1)S(1)}) custom-call(bf16[1024,256]{1,0:T(8,128)(2,1)} %refs_0_.1, bf16[1024,256]{1,0:T(8,128)(2,1)} %collective-permute-done.refs_1_, bf16[1024,256]{1,0:T(8,128)(2,1)} %collective-permute-done.1.refs_2_, ...), custom_call_target="tpu_custom_call" | custom-call | flops 2147483648 | bytes 8388608 | tf_op jit(solution)/shard_map/mix/pallas_call | solution.py:238
  118.9 2.6 %collective-permute-start.10 = (bf16[1024,128]{1,0:T(8,128)(2,1)S(1)}, bf16[1024,128]{1,0:T(8,128)(2,1)S(1)}, u32[]{:S(2)}, u32[]{:S(2)}) collective-permute-start(bf16[1024,128]{1,0:T(8,128)(2,1)S(1)} %get-tuple-element.12), channel_id=1, source_target_pairs={{0,48},{16,0},{32,16},{48,32},{1,49},{17,1},{33,17},{49,33},{2,50}... | collective-permute-start | bytes 786440 | tf_op jit(solution)/shard_map/ppermute | solution.py:271
  121.5 1.7 collective-permute-start.12
  123.2 1.6 constant_dynamic-update-slice_fusion.11
  125.6 6.7 %collective-permute-done.10 = bf16[1024,128]{1,0:T(8,128)(2,1)S(1)} collective-permute-done((bf16[1024,128]{1,0:T(8,128)(2,1)S(1)}, bf16[1024,128]{1,0:T(8,128)(2,1)S(1)}, u32[]{:S(2)}, u32[]{:S(2)}) %collective-permute-start.10) | collective-permute-done | bytes 262176 | tf_op jit(solution)/shard_map/ppermute | solution.py:271
  132.3 2.4 collective-permute-done.12
  134.8 2.4 fusion.5
  137.1 1.8 collective-permute-start.15
  139.6 1.6 constant_dynamic-update-slice_fusion.9
  141.3 1.7 slice.164
  142.9 1.0 slice.160
  143.9 2.6 %collective-permute-start.18 = (bf16[4,128,256]{2,1,0:T(8,128)(2,1)S(1)}, bf16[4,128,256]{2,1,0:T(8,128)(2,1)S(1)}, u32[]{:S(2)}, u32[]{:S(2)}) collective-permute-start(bf16[4,128,256]{2,1,0:T(8,128)(2,1)S(1)} %slice.160), channel_id=1, source_target_pairs={{0,8},{8,0},{1,9},{9,1},{2,10},{10,2},{3,11},{11,3},{4,12},{12,4},... | collective-permute-start | bytes 786440 | tf_op jit(solution)/shard_map/ppermute | solution.py:265
  146.5 1.6 constant_dynamic-update-slice_fusion.8
  148.2 3.0 %collective-permute-start.20 = (bf16[4,128,256]{2,1,0:T(8,128)(2,1)}, bf16[4,128,256]{2,1,0:T(8,128)(2,1)}, u32[]{:S(2)}, u32[]{:S(2)}) collective-permute-start(bf16[4,128,256]{2,1,0:T(8,128)(2,1)} %slice.164), channel_id=1, source_target_pairs={{0,8},{8,0},{1,9},{9,1},{2,10},{10,2},{3,11},{11,3},{4,12},{12,4},... | collective-permute-start | bytes 786440 | tf_op jit(solution)/shard_map/ppermute | solution.py:265
  151.2 2.5 collective-permute-done.13
  153.7 1.1 pad_maximum_fusion
  156.4 1.7 constant_dynamic-update-slice_fusion.6
  158.1 7.2 %all-to-all-start.2 = ((bf16[32,32,128]{2,1,0:T(8,128)(2,1)}), bf16[32,32,128]{2,1,0:T(8,128)(2,1)S(1)}, u32[]{:S(2)}, u32[]{:S(2)}) async-start(bf16[32,32,128]{2,1,0:T(8,128)(2,1)} %bitcast.193), calls=%async_computation.2 | async-start | bytes 524288 | tf_op jit(solution)/shard_map/all_to_all | solution.py:274
  165.3 1.6 constant_dynamic-update-slice_fusion.5
  167.0 1.8 copy.22
  168.8 1.7 constant_dynamic-update-slice_fusion.4
  170.5 1.7 constant_dynamic-update-slice_fusion.3
  172.2 1.7 constant_dynamic-update-slice_fusion.2
  173.9 1.7 constant_dynamic-update-slice_fusion.1
  175.6 2.6 %all-to-all-done.2.gsig_ref = bf16[32,32,128]{2,1,0:T(8,128)(2,1)S(1)} async-done(((bf16[32,32,128]{2,1,0:T(8,128)(2,1)}), bf16[32,32,128]{2,1,0:T(8,128)(2,1)S(1)}, u32[]{:S(2)}, u32[]{:S(2)}) %all-to-all-start.2) | async-done | bytes 262176 | tf_op jit(solution)/shard_map/all_to_all | solution.py:274
  178.2 1.0 copy-done.3
  179.2 5.4 %corr.1 = bf16[32,2,32,128]{3,2,1,0:T(8,128)(2,1)} custom-call(bf16[32,32,128]{2,1,0:T(8,128)(2,1)S(1)} %all-to-all-done.2.gsig_ref, f32[4,2,528,128]{3,2,1,0:T(8,128)S(1)} %get-tuple-element.16.spec_ref, f32[32,128]{1,0:T(8,128)S(1)} %broadcast_in_dim.2.skip_ref, bf16[2,512,256]{2,1,0:T(8,128)(2,1)S(1)} %copy-done.3, f32[2,33,128]{2,1,0:T(8,128)S(1)} %copy-done.11, ...), custom_call_target="tpu_custom_call" | custom-call | flops 1000000000 | bytes 6291456 | tf_op jit(solution)/shard_map/corr/pallas_call | solution.py:173
  184.7 7.3 %all-to-all-start.3 = ((bf16[32,2,32,128]{3,2,1,0:T(8,128)(2,1)}), bf16[32,2,32,128]{3,2,1,0:T(8,128)(2,1)S(1)}, u32[]{:S(2)}, u32[]{:S(2)}) async-start(bf16[32,2,32,128]{3,2,1,0:T(8,128)(2,1)} %corr.1), calls=%async_computation.3 | async-start | bytes 1048576 | tf_op jit(solution)/shard_map/all_to_all | solution.py:274
  192.0 2.3 constant_dynamic-update-slice_fusion
  194.3 3.1 %convolution_convert_fusion.2 = bf16[1024,256]{1,0:T(8,128)(2,1)} fusion(bf16[1024,1024]{1,0:T(8,128)(2,1)} %constant_dynamic-update-slice_fusion, bf16[1024,256]{1,0:T(8,128)(2,1)S(1)} %copy-done.23), kind=kOutput, calls=%fused_computation.2 | convolution fusion | flops 537133056 | bytes 3145728 | tf_op jit(solution)/shard_map/dot_general | solution.py:53
  197.5 5.3 %collective-permute-start.21 = (bf16[1024,256]{1,0:T(8,128)(2,1)}, bf16[1024,256]{1,0:T(8,128)(2,1)S(1)}, u32[]{:S(2)}, u32[]{:S(2)}) collective-permute-start(bf16[1024,256]{1,0:T(8,128)(2,1)} %convolution_convert_fusion.2), channel_id=1, source_target_pairs={{0,128},{64,192},{128,0},{192,64},{1,129},{65,193},{129,1},{193,65... | collective-permute-start | bytes 1572872 | tf_op jit(solution)/shard_map/ppermute | solution.py:268
  202.8 3.2 %convolution_convert_fusion.1 = bf16[1024,256]{1,0:T(8,128)(2,1)} fusion(bf16[1024,1024]{1,0:T(8,128)(2,1)} %constant_dynamic-update-slice_fusion, bf16[1024,256]{1,0:T(8,128)(2,1)S(1)} %copy-done.26), kind=kOutput, calls=%fused_computation.1 | convolution fusion | flops 537133056 | bytes 3145728 | tf_op jit(solution)/shard_map/dot_general | solution.py:53
  206.3 3.1 %convolution_convert_fusion = bf16[1024,256]{1,0:T(8,128)(2,1)} fusion(bf16[1024,1024]{1,0:T(8,128)(2,1)} %constant_dynamic-update-slice_fusion, bf16[1024,256]{1,0:T(8,128)(2,1)S(1)} %copy-done.25), kind=kOutput, calls=%fused_computation | convolution fusion | flops 537133056 | bytes 3145728 | tf_op jit(solution)/shard_map/dot_general | solution.py:53
  209.4 3.3 %collective-permute-start.23 = (bf16[1024,256]{1,0:T(8,128)(2,1)}, bf16[1024,256]{1,0:T(8,128)(2,1)}, u32[]{:S(2)}, u32[]{:S(2)}) collective-permute-start(bf16[1024,256]{1,0:T(8,128)(2,1)} %convolution_convert_fusion), channel_id=1, source_target_pairs={{0,192},{64,0},{128,64},{192,128},{1,193},{65,1},{129,65},{193,129... | collective-permute-start | bytes 1572872 | tf_op jit(solution)/shard_map/ppermute | solution.py:268
  213.8 0.9 fusion
  214.7 17.2 %collective-permute-done.21 = bf16[1024,256]{1,0:T(8,128)(2,1)S(1)} collective-permute-done((bf16[1024,256]{1,0:T(8,128)(2,1)}, bf16[1024,256]{1,0:T(8,128)(2,1)S(1)}, u32[]{:S(2)}, u32[]{:S(2)}) %collective-permute-start.21) | collective-permute-done | bytes 524320 | tf_op jit(solution)/shard_map/ppermute | solution.py:268
  231.9 9.3 %collective-permute-done.22 = bf16[1024,256]{1,0:T(8,128)(2,1)S(1)} collective-permute-done((bf16[1024,256]{1,0:T(8,128)(2,1)}, bf16[1024,256]{1,0:T(8,128)(2,1)S(1)}, u32[]{:S(2)}, u32[]{:S(2)}) %collective-permute-start.22) | collective-permute-done | bytes 524320 | tf_op jit(solution)/shard_map/ppermute | solution.py:268
  241.3 13.5 %collective-permute-done.23 = bf16[1024,256]{1,0:T(8,128)(2,1)} collective-permute-done((bf16[1024,256]{1,0:T(8,128)(2,1)}, bf16[1024,256]{1,0:T(8,128)(2,1)}, u32[]{:S(2)}, u32[]{:S(2)}) %collective-permute-start.23) | collective-permute-done | bytes 524320 | tf_op jit(solution)/shard_map/ppermute | solution.py:268
  254.8 3.2 %multiply_convert_fusion = bf16[1024,256]{1,0:T(8,128)(2,1)} fusion(bf16[1024,256]{1,0:T(8,128)(2,1)} %collective-permute-done.23, bf16[1024,256]{1,0:T(8,128)(2,1)S(1)} %collective-permute-done.22, bf16[1024,256]{1,0:T(8,128)(2,1)S(1)} %collective-permute-done.21, bf16[1024,1024]{1,0:T(8,128)(2,1)} %constant_dynamic-update-slice_fusion, ...), kind=kOutput, calls=%fused_computation.4 | convolution fusion | flops 538968064 | bytes 4718592 | tf_op jit(solution)/shard_map/dot_general | solution.py:53
  (93 shorter events, 14.2 us)
Async XLA Ops:
  3.9 83.5 %all-to-all-start = ((bf16[32,2,32,128]{3,2,1,0:T(8,128)(2,1)}), bf16[32,2,32,128]{3,2,1,0:T(8,128)(2,1)S(1)}, u32[]{:S(2)}, u32[]{:S(2)}) async-start(bf16[32,2,32,128]{3,2,1,0:T(8,128)(2,1)} %pad_maximum_fusion.1), calls=%async_computation | async-start | bytes 1048576 | tf_op jit(solution)/shard_map/all_to_all | solution.py:274
  22.6 23.4 %collective-permute-start.8 = (bf16[8,128,256]{2,1,0:T(8,128)(2,1)}, bf16[8,128,256]{2,1,0:T(8,128)(2,1)S(1)}, u32[]{:S(2)}, u32[]{:S(2)}) collective-permute-start(bf16[8,128,256]{2,1,0:T(8,128)(2,1)} %pick.6), channel_id=1, source_target_pairs={{0,32},{16,48},{32,0},{48,16},{1,33},{17,49},{33,1},{49,17},{2,34}... | collective-permute-start | bytes 1572872 | tf_op jit(solution)/shard_map/ppermute | solution.py:271
  26.1 49.5 %copy-start.22 = (bf16[128,1024]{1,0:T(8,128)(2,1)S(1)}, bf16[128,1024]{1,0:T(8,128)(2,1)}, u32[]{:S(2)}) copy-start(bf16[128,1024]{1,0:T(8,128)(2,1)} %param.14) | copy-start | bytes 786436
  31.7 19.7 %collective-permute-start.9 = (bf16[8,128,256]{2,1,0:T(8,128)(2,1)}, bf16[8,128,256]{2,1,0:T(8,128)(2,1)S(1)}, u32[]{:S(2)}, u32[]{:S(2)}) collective-permute-start(bf16[8,128,256]{2,1,0:T(8,128)(2,1)} %pick.7), channel_id=1, source_target_pairs={{0,48},{16,0},{32,16},{48,32},{1,49},{17,1},{33,17},{49,33},{2,50}... | collective-permute-start | bytes 1572872 | tf_op jit(solution)/shard_map/ppermute | solution.py:271
  32.5 36.8 %collective-permute-start.2 = (bf16[1024,256]{1,0:T(8,128)(2,1)}, bf16[1024,256]{1,0:T(8,128)(2,1)}, u32[]{:S(2)}, u32[]{:S(2)}) collective-permute-start(bf16[1024,256]{1,0:T(8,128)(2,1)} %refs_0_.1), channel_id=1, source_target_pairs={{0,192},{64,0},{128,64},{192,128},{1,193},{65,1},{129,65},{193,129... | collective-permute-start | bytes 1572872 | tf_op jit(solution)/shard_map/ppermute | solution.py:268
  35.9 34.4 %collective-permute-start.1 = (bf16[1024,256]{1,0:T(8,128)(2,1)}, bf16[1024,256]{1,0:T(8,128)(2,1)}, u32[]{:S(2)}, u32[]{:S(2)}) collective-permute-start(bf16[1024,256]{1,0:T(8,128)(2,1)} %refs_0_.1), channel_id=1, source_target_pairs={{0,128},{64,192},{128,0},{192,64},{1,129},{65,193},{129,1},{193,65... | collective-permute-start | bytes 1572872 | tf_op jit(solution)/shard_map/ppermute | solution.py:268
  37.9 36.1 %collective-permute-start = (bf16[1024,256]{1,0:T(8,128)(2,1)}, bf16[1024,256]{1,0:T(8,128)(2,1)}, u32[]{:S(2)}, u32[]{:S(2)}) collective-permute-start(bf16[1024,256]{1,0:T(8,128)(2,1)} %refs_0_.1), channel_id=1, source_target_pairs={{0,64},{64,128},{128,192},{192,0},{1,65},{65,129},{129,193},{193,1... | collective-permute-start | bytes 1572872 | tf_op jit(solution)/shard_map/ppermute | solution.py:268
  46.0 40.7 %copy-start.18 = (bf16[8,128,256]{2,1,0:T(8,128)(2,1)}, bf16[8,128,256]{2,1,0:T(8,128)(2,1)S(1)}, u32[]{:S(2)}) copy-start(bf16[8,128,256]{2,1,0:T(8,128)(2,1)S(1)} %collective-permute-done.8.refs_10_) | copy-start | bytes 1572868
  46.0 65.4 %collective-permute-start.3 = (bf16[1024,256]{1,0:T(8,128)(2,1)}, bf16[1024,256]{1,0:T(8,128)(2,1)}, u32[]{:S(2)}, u32[]{:S(2)}) collective-permute-start(bf16[1024,256]{1,0:T(8,128)(2,1)} %refs_0_.1), channel_id=1, source_target_pairs={{0,8},{8,0},{1,9},{9,1},{2,10},{10,2},{3,11},{11,3},{4,12},{12,4},... | collective-permute-start | bytes 1572872 | tf_op jit(solution)/shard_map/ppermute | solution.py:265
  51.4 25.1 %copy-start.20 = (bf16[8,128,256]{2,1,0:T(8,128)(2,1)}, bf16[8,128,256]{2,1,0:T(8,128)(2,1)S(1)}, u32[]{:S(2)}) copy-start(bf16[8,128,256]{2,1,0:T(8,128)(2,1)S(1)} %collective-permute-done.9.refs_11_) | copy-start | bytes 1572868
  51.4 59.6 %collective-permute-start.7 = (bf16[8,128,256]{2,1,0:T(8,128)(2,1)}, bf16[8,128,256]{2,1,0:T(8,128)(2,1)}, u32[]{:S(2)}, u32[]{:S(2)}) collective-permute-start(bf16[8,128,256]{2,1,0:T(8,128)(2,1)} %pick.5), channel_id=1, source_target_pairs={{0,16},{16,32},{32,48},{48,0},{1,17},{17,33},{33,49},{49,1},{2,18}... | collective-permute-start | bytes 1572872 | tf_op jit(solution)/shard_map/ppermute | solution.py:271
  69.3 42.3 %collective-permute-start.6 = (bf16[1024,256]{1,0:T(8,128)(2,1)}, bf16[1024,256]{1,0:T(8,128)(2,1)}, u32[]{:S(2)}, u32[]{:S(2)}) collective-permute-start(bf16[1024,256]{1,0:T(8,128)(2,1)} %collective-permute-done.2.refs_3_), channel_id=1, source_target_pairs={{0,8},{8,0},{1,9},{9,1},{2,10},{10,2},{3,11},{11,3},{4,12},{12,4},... | collective-permute-start | bytes 1572872 | tf_op jit(solution)/shard_map/ppermute | solution.py:265
  70.3 41.3 %collective-permute-start.5 = (bf16[1024,256]{1,0:T(8,128)(2,1)}, bf16[1024,256]{1,0:T(8,128)(2,1)}, u32[]{:S(2)}, u32[]{:S(2)}) collective-permute-start(bf16[1024,256]{1,0:T(8,128)(2,1)} %collective-permute-done.1.refs_2_), channel_id=1, source_target_pairs={{0,8},{8,0},{1,9},{9,1},{2,10},{10,2},{3,11},{11,3},{4,12},{12,4},... | collective-permute-start | bytes 1572872 | tf_op jit(solution)/shard_map/ppermute | solution.py:265
  74.0 37.6 %collective-permute-start.4 = (bf16[1024,256]{1,0:T(8,128)(2,1)}, bf16[1024,256]{1,0:T(8,128)(2,1)}, u32[]{:S(2)}, u32[]{:S(2)}) collective-permute-start(bf16[1024,256]{1,0:T(8,128)(2,1)} %collective-permute-done.refs_1_), channel_id=1, source_target_pairs={{0,8},{8,0},{1,9},{9,1},{2,10},{10,2},{3,11},{11,3},{4,12},{12,4},... | collective-permute-start | bytes 1572872 | tf_op jit(solution)/shard_map/ppermute | solution.py:265
  77.1 11.2 %copy-start.1 = (bf16[2,256,512]{2,1,0:T(8,128)(2,1)S(1)}, bf16[2,256,512]{2,1,0:T(8,128)(2,1)}, u32[]{:S(2)}) copy-start(bf16[2,256,512]{2,1,0:T(8,128)(2,1)} %constant.273.clone.last_ref) | copy-start | bytes 1572868
  77.1 11.2 %copy-start.7 = (bf16[2,256,256]{2,1,0:T(8,128)(2,1)S(1)}, bf16[2,256,256]{2,1,0:T(8,128)(2,1)}, u32[]{:S(2)}) copy-start(bf16[2,256,256]{2,1,0:T(8,128)(2,1)} %constant.272.clone.behind_ref) | copy-start | bytes 786436
  77.1 11.2 %copy-start.11 = (f32[2,33,128]{2,1,0:T(8,128)S(1)}, f32[2,33,128]{2,1,0:T(8,128)}, u32[]{:S(2)}) copy-start(f32[2,33,128]{2,1,0:T(8,128)} %constant.270.clone.twist_ref) | copy-start | bytes 101380
  87.4 0.8 copy-start.5
  88.3 1.0 copy-start.2
  89.3 1.0 copy-start.6
  90.4 0.9 copy-start.8
  91.3 20.3 %copy-start = (bf16[8,128,256]{2,1,0:T(8,128)(2,1)S(1)}, bf16[8,128,256]{2,1,0:T(8,128)(2,1)}, u32[]{:S(2)}) copy-start(bf16[8,128,256]{2,1,0:T(8,128)(2,1)} %pick.4.refs_8_) | copy-start | bytes 1572868
  96.2 0.7 copy-start.10
  96.9 37.8 %all-to-all-start.1 = ((bf16[32,32,128]{2,1,0:T(8,128)(2,1)}), bf16[32,32,128]{2,1,0:T(8,128)(2,1)}, u32[]{:S(2)}, u32[]{:S(2)}) async-start(bf16[32,32,128]{2,1,0:T(8,128)(2,1)} %copy-done.10), calls=%async_computation.1 | async-start | bytes 524288 | tf_op jit(solution)/shard_map/all_to_all | solution.py:274
  111.0 13.9 %copy-start.19 = (bf16[8,128,256]{2,1,0:T(8,128)(2,1)S(1)}, bf16[8,128,256]{2,1,0:T(8,128)(2,1)}, u32[]{:S(2)}) copy-start(bf16[8,128,256]{2,1,0:T(8,128)(2,1)} %copy-done.18) | copy-start | bytes 1572868
  111.0 32.9 %collective-permute-start.17 = (bf16[4,128,256]{2,1,0:T(8,128)(2,1)}, bf16[4,128,256]{2,1,0:T(8,128)(2,1)}, u32[]{:S(2)}, u32[]{:S(2)}) collective-permute-start(bf16[4,128,256]{2,1,0:T(8,128)(2,1)} %slice.158), channel_id=1, source_target_pairs={{0,8},{8,0},{1,9},{9,1},{2,10},{10,2},{3,11},{11,3},{4,12},{12,4},... | collective-permute-start | bytes 786440 | tf_op jit(solution)/shard_map/ppermute | solution.py:265
  111.4 45.0 %collective-permute-start.19 = (bf16[4,128,256]{2,1,0:T(8,128)(2,1)}, bf16[4,128,256]{2,1,0:T(8,128)(2,1)}, u32[]{:S(2)}, u32[]{:S(2)}) collective-permute-start(bf16[4,128,256]{2,1,0:T(8,128)(2,1)} %slice.162), channel_id=1, source_target_pairs={{0,8},{8,0},{1,9},{9,1},{2,10},{10,2},{3,11},{11,3},{4,12},{12,4},... | collective-permute-start | bytes 786440 | tf_op jit(solution)/shard_map/ppermute | solution.py:265
  118.1 0.8 copy-start.4
  118.9 13.5 %collective-permute-start.10 = (bf16[1024,128]{1,0:T(8,128)(2,1)S(1)}, bf16[1024,128]{1,0:T(8,128)(2,1)S(1)}, u32[]{:S(2)}, u32[]{:S(2)}) collective-permute-start(bf16[1024,128]{1,0:T(8,128)(2,1)S(1)} %get-tuple-element.12), channel_id=1, source_target_pairs={{0,48},{16,0},{32,16},{48,32},{1,49},{17,1},{33,17},{49,33},{2,50}... | collective-permute-start | bytes 786440 | tf_op jit(solution)/shard_map/ppermute | solution.py:271
  121.5 10.9 %collective-permute-start.11 = (bf16[1024,128]{1,0:T(8,128)(2,1)S(1)}, bf16[1024,128]{1,0:T(8,128)(2,1)S(1)}, u32[]{:S(2)}, u32[]{:S(2)}) collective-permute-start(bf16[1024,128]{1,0:T(8,128)(2,1)S(1)} %get-tuple-element.13), channel_id=1, source_target_pairs={{0,16},{16,32},{32,48},{48,0},{1,17},{17,33},{33,49},{49,1},{2,18}... | collective-permute-start | bytes 786440 | tf_op jit(solution)/shard_map/ppermute | solution.py:271
  121.5 13.3 %collective-permute-start.12 = (bf16[1024,128]{1,0:T(8,128)(2,1)S(1)}, bf16[1024,128]{1,0:T(8,128)(2,1)}, u32[]{:S(2)}, u32[]{:S(2)}) collective-permute-start(bf16[1024,128]{1,0:T(8,128)(2,1)S(1)} %get-tuple-element.14), channel_id=1, source_target_pairs={{0,32},{16,48},{32,0},{48,16},{1,33},{17,49},{33,1},{49,17},{2,34}... | collective-permute-start | bytes 786440 | tf_op jit(solution)/shard_map/ppermute | solution.py:271
  132.3 2.4 copy-start.21
  137.1 19.2 %copy-start.12 = (bf16[1024,128]{1,0:T(8,128)(2,1)}, bf16[1024,128]{1,0:T(8,128)(2,1)S(1)}, u32[]{:S(2)}) copy-start(bf16[1024,128]{1,0:T(8,128)(2,1)S(1)} %get-tuple-element.24) | copy-start | bytes 786436
  137.1 11.0 %collective-permute-start.15 = (bf16[1024,128]{1,0:T(8,128)(2,1)S(1)}, bf16[1024,128]{1,0:T(8,128)(2,1)S(1)}, u32[]{:S(2)}, u32[]{:S(2)}) collective-permute-start(bf16[1024,128]{1,0:T(8,128)(2,1)S(1)} %get-tuple-element.24), channel_id=1, source_target_pairs={{0,48},{16,0},{32,16},{48,32},{1,49},{17,1},{33,17},{49,33},{2,50}... | collective-permute-start | bytes 786440 | tf_op jit(solution)/shard_map/ppermute | solution.py:271
  139.0 12.2 %collective-permute-start.14 = (bf16[1024,128]{1,0:T(8,128)(2,1)S(1)}, bf16[1024,128]{1,0:T(8,128)(2,1)S(1)}, u32[]{:S(2)}, u32[]{:S(2)}) collective-permute-start(bf16[1024,128]{1,0:T(8,128)(2,1)S(1)} %get-tuple-element.24), channel_id=1, source_target_pairs={{0,32},{16,48},{32,0},{48,16},{1,33},{17,49},{33,1},{49,17},{2,34}... | collective-permute-start | bytes 786440 | tf_op jit(solution)/shard_map/ppermute | solution.py:271
  139.0 14.7 %collective-permute-start.13 = (bf16[1024,128]{1,0:T(8,128)(2,1)S(1)}, bf16[1024,128]{1,0:T(8,128)(2,1)S(1)}, u32[]{:S(2)}, u32[]{:S(2)}) collective-permute-start(bf16[1024,128]{1,0:T(8,128)(2,1)S(1)} %get-tuple-element.24), channel_id=1, source_target_pairs={{0,16},{16,32},{32,48},{48,0},{1,17},{17,33},{33,49},{49,1},{2,18}... | collective-permute-start | bytes 786440 | tf_op jit(solution)/shard_map/ppermute | solution.py:271
  143.9 11.7 %collective-permute-start.18 = (bf16[4,128,256]{2,1,0:T(8,128)(2,1)S(1)}, bf16[4,128,256]{2,1,0:T(8,128)(2,1)S(1)}, u32[]{:S(2)}, u32[]{:S(2)}) collective-permute-start(bf16[4,128,256]{2,1,0:T(8,128)(2,1)S(1)} %slice.160), channel_id=1, source_target_pairs={{0,8},{8,0},{1,9},{9,1},{2,10},{10,2},{3,11},{11,3},{4,12},{12,4},... | collective-permute-start | bytes 786440 | tf_op jit(solution)/shard_map/ppermute | solution.py:265
  148.2 9.9 %copy-start.15 = (bf16[1024,128]{1,0:T(8,128)(2,1)}, bf16[1024,128]{1,0:T(8,128)(2,1)S(1)}, u32[]{:S(2)}) copy-start(bf16[1024,128]{1,0:T(8,128)(2,1)S(1)} %collective-permute-done.15) | copy-start | bytes 786436
  148.2 17.1 %collective-permute-start.20 = (bf16[4,128,256]{2,1,0:T(8,128)(2,1)}, bf16[4,128,256]{2,1,0:T(8,128)(2,1)}, u32[]{:S(2)}, u32[]{:S(2)}) collective-permute-start(bf16[4,128,256]{2,1,0:T(8,128)(2,1)} %slice.164), channel_id=1, source_target_pairs={{0,8},{8,0},{1,9},{9,1},{2,10},{10,2},{3,11},{11,3},{4,12},{12,4},... | collective-permute-start | bytes 786440 | tf_op jit(solution)/shard_map/ppermute | solution.py:265
  151.2 5.2 %copy-start.16 = (bf16[1024,128]{1,0:T(8,128)(2,1)}, bf16[1024,128]{1,0:T(8,128)(2,1)S(1)}, u32[]{:S(2)}) copy-start(bf16[1024,128]{1,0:T(8,128)(2,1)S(1)} %collective-permute-done.14) | copy-start | bytes 786436
  153.7 4.4 %copy-start.17 = (bf16[1024,128]{1,0:T(8,128)(2,1)}, bf16[1024,128]{1,0:T(8,128)(2,1)S(1)}, u32[]{:S(2)}) copy-start(bf16[1024,128]{1,0:T(8,128)(2,1)S(1)} %collective-permute-done.13) | copy-start | bytes 786436
  154.8 37.2 %collective-permute-start.16 = (bf16[1024,512]{1,0:T(8,128)(2,1)}, bf16[1024,512]{1,0:T(8,128)(2,1)}, u32[]{:S(2)}, u32[]{:S(2)}) collective-permute-start(bf16[1024,512]{1,0:T(8,128)(2,1)} %pad_maximum_fusion), channel_id=1, source_target_pairs={{0,8},{8,0},{1,9},{9,1},{2,10},{10,2},{3,11},{11,3},{4,12},{12,4},... | collective-permute-start | bytes 3145736 | tf_op jit(solution)/shard_map/ppermute | solution.py:265
  156.4 21.8 %copy-start.9 = (bf16[2,256,256]{2,1,0:T(8,128)(2,1)S(1)}, bf16[2,256,256]{2,1,0:T(8,128)(2,1)}, u32[]{:S(2)}) copy-start(bf16[2,256,256]{2,1,0:T(8,128)(2,1)} %constant.271.clone.ahead_ref) | copy-start | bytes 786436
  158.1 20.1 %all-to-all-start.2 = ((bf16[32,32,128]{2,1,0:T(8,128)(2,1)}), bf16[32,32,128]{2,1,0:T(8,128)(2,1)S(1)}, u32[]{:S(2)}, u32[]{:S(2)}) async-start(bf16[32,32,128]{2,1,0:T(8,128)(2,1)} %bitcast.193), calls=%async_computation.2 | async-start | bytes 524288 | tf_op jit(solution)/shard_map/all_to_all | solution.py:274
  178.2 1.0 copy-start.3
  184.7 9.7 %copy-start.23 = (bf16[1024,256]{1,0:T(8,128)(2,1)S(1)}, bf16[1024,256]{1,0:T(8,128)(2,1)}, u32[]{:S(2)}) copy-start(bf16[1024,256]{1,0:T(8,128)(2,1)} %get-tuple-element.45) | copy-start | bytes 1572868
  184.7 28.0 %all-to-all-start.3 = ((bf16[32,2,32,128]{3,2,1,0:T(8,128)(2,1)}), bf16[32,2,32,128]{3,2,1,0:T(8,128)(2,1)S(1)}, u32[]{:S(2)}, u32[]{:S(2)}) async-start(bf16[32,2,32,128]{3,2,1,0:T(8,128)(2,1)} %corr.1), calls=%async_computation.3 | async-start | bytes 1048576 | tf_op jit(solution)/shard_map/all_to_all | solution.py:274
  194.3 8.4 %copy-start.26 = (bf16[1024,256]{1,0:T(8,128)(2,1)S(1)}, bf16[1024,256]{1,0:T(8,128)(2,1)}, u32[]{:S(2)}) copy-start(bf16[1024,256]{1,0:T(8,128)(2,1)} %get-tuple-element.48) | copy-start | bytes 1572868
  197.5 34.5 %collective-permute-start.21 = (bf16[1024,256]{1,0:T(8,128)(2,1)}, bf16[1024,256]{1,0:T(8,128)(2,1)S(1)}, u32[]{:S(2)}, u32[]{:S(2)}) collective-permute-start(bf16[1024,256]{1,0:T(8,128)(2,1)} %convolution_convert_fusion.2), channel_id=1, source_target_pairs={{0,128},{64,192},{128,0},{192,64},{1,129},{65,193},{129,1},{193,65... | collective-permute-start | bytes 1572872 | tf_op jit(solution)/shard_map/ppermute | solution.py:268
  202.8 3.5 %copy-start.25 = (bf16[1024,256]{1,0:T(8,128)(2,1)S(1)}, bf16[1024,256]{1,0:T(8,128)(2,1)}, u32[]{:S(2)}) copy-start(bf16[1024,256]{1,0:T(8,128)(2,1)} %get-tuple-element.47) | copy-start | bytes 1572868
  205.9 35.4 %collective-permute-start.22 = (bf16[1024,256]{1,0:T(8,128)(2,1)}, bf16[1024,256]{1,0:T(8,128)(2,1)S(1)}, u32[]{:S(2)}, u32[]{:S(2)}) collective-permute-start(bf16[1024,256]{1,0:T(8,128)(2,1)} %convolution_convert_fusion.1), channel_id=1, source_target_pairs={{0,64},{64,128},{128,192},{192,0},{1,65},{65,129},{129,193},{193,1... | collective-permute-start | bytes 1572872 | tf_op jit(solution)/shard_map/ppermute | solution.py:268
  209.4 4.4 %copy-start.13 = (bf16[128,1024]{1,0:T(8,128)(2,1)S(1)}, bf16[128,1024]{1,0:T(8,128)(2,1)}, u32[]{:S(2)}) copy-start(bf16[128,1024]{1,0:T(8,128)(2,1)} %param.16) | copy-start | bytes 786436
  209.4 4.4 %copy-start.14 = (bf16[128,1024]{1,0:T(8,128)(2,1)S(1)}, bf16[128,1024]{1,0:T(8,128)(2,1)}, u32[]{:S(2)}) copy-start(bf16[128,1024]{1,0:T(8,128)(2,1)} %param.15) | copy-start | bytes 786436
  209.4 45.4 %collective-permute-start.23 = (bf16[1024,256]{1,0:T(8,128)(2,1)}, bf16[1024,256]{1,0:T(8,128)(2,1)}, u32[]{:S(2)}, u32[]{:S(2)}) collective-permute-start(bf16[1024,256]{1,0:T(8,128)(2,1)} %convolution_convert_fusion), channel_id=1, source_target_pairs={{0,192},{64,0},{128,64},{192,128},{1,193},{65,1},{129,65},{193,129... | collective-permute-start | bytes 1572872 | tf_op jit(solution)/shard_map/ppermute | solution.py:268
  212.7 42.1 %copy-start.24 = (bf16[1024,256]{1,0:T(8,128)(2,1)S(1)}, bf16[1024,256]{1,0:T(8,128)(2,1)}, u32[]{:S(2)}) copy-start(bf16[1024,256]{1,0:T(8,128)(2,1)} %get-tuple-element.46) | copy-start | bytes 1572868

commit v2 on v1

v2 whole, which is shorter than its diff:
```python
import functools
import math

import jax
import jax.numpy as jnp
import numpy as np
from jax import lax
from jax.experimental import pallas as pl
from jax.experimental.pallas import tpu as pltpu
from jax.sharding import Mesh
from jax.sharding import PartitionSpec as P

bf16 = jnp.bfloat16
f32 = jnp.float32
CTX = ("zh", "x", "core")
TEN = ("zl", "y")
VMEM_LIMIT = 60 * 1024 * 1024

OUTER, INNER = 64, 128
KEPT = OUTER // 2 + 1
HALF = OUTER // 2
GROUP = 16


@functools.cache
def tables(seq_len):
    length = 2 * seq_len
    i = np.arange(HALF)
    k = np.arange(KEPT)
    turn = 2.0 * np.pi * np.outer(k, i) / OUTER
    rows = np.concatenate([np.cos(turn), -np.sin(turn)[1:HALF]], 0)
    first = np.repeat(rows, 8, axis=1)
    weight = np.where((k == 0) | (k == HALF), 1.0, 2.0)[:, None]
    back = np.concatenate([weight * np.cos(turn), -(weight * np.sin(turn))[1:HALF]], 0).T
    last = np.repeat(back / (length * math.sqrt(seq_len)), 8, axis=1)
    b = np.arange(INNER)
    inner = 2.0 * np.pi * np.outer(b, b) / INNER
    twist = 2.0 * np.pi * np.outer(k, b) / length
    pieces = [first[:, :INNER], first[:, INNER:]]
    pieces += [last[:, INNER * n : INNER * (n + 1)] for n in range(4)]
    pieces += [np.cos(inner), np.sin(inner), np.cos(twist), np.sin(twist)]
    pieces = [np.pad(item, ((0, -len(item) % 8), (0, 0))) for item in pieces]
    return np.concatenate(pieces).astype(np.float32)


def unpack(table_ref):
    places = [0]
    for size in (OUTER, OUTER) + (HALF,) * 4 + (INNER, INNER, KEPT + 7, KEPT + 7):
        places.append(places[-1] + size)
    first_a, first_b, *back, c, s, cos, sin = [
        table_ref[places[n] : places[n + 1]] for n in range(10)
    ]

    def spread(table):
        rows, cols = table.shape
        shape = (rows, 8, cols)
        own = lax.broadcasted_iota(jnp.int32, shape, 1) == (
            lax.broadcasted_iota(jnp.int32, shape, 2) & 7
        )
        wide = jnp.broadcast_to(table[:, None, :], shape)
        return jnp.where(own, wide, 0.0).reshape(rows * 8, cols)

    first = split(spread(jnp.concatenate([first_a, first_b], 1)))
    last = split(spread(jnp.concatenate(back, 1)))
    ahead = split(jnp.concatenate([jnp.concatenate([c, -s], 1), jnp.concatenate([s, c], 1)], 0))
    behind = split(jnp.concatenate([jnp.concatenate([c, s], 1), jnp.concatenate([-s, c], 1)], 0))
    return first, (cos[:KEPT], sin[:KEPT]), ahead, behind, last


def dot(a, b):
    return jnp.dot(a, b, preferred_element_type=f32)


def split(x):
    high = x.astype(bf16)
    return high, (x - high.astype(f32)).astype(bf16)


def forward(field, first, twist, ahead, exact=True):
    packed = jnp.concatenate(
        [field[:, 8 * g : 8 * g + 8].reshape(8 * HALF, INNER) for g in range(2)], 1
    )
    high, low = split(packed)
    mixed = dot(first[0], high) + dot(first[1], high)
    if not exact:
        mixed = mixed + dot(first[0], low)
    halves = [mixed[:, INNER * g : INNER * (g + 1)].reshape(OUTER, 8, INNER) for g in range(2)]
    both = jnp.concatenate(halves, 1)
    zero = jnp.zeros((1, GROUP, INNER), f32)
    re = both[:KEPT]
    im = jnp.concatenate([zero, both[KEPT:], zero], 0)
    cos, sin = twist[0][:, None, :], twist[1][:, None, :]
    turned = jnp.concatenate([re * cos + im * sin, im * cos - re * sin], 2)
    high, low = split(turned.reshape(KEPT * GROUP, 2 * INNER))
    spec = dot(high, ahead[0]) + (dot(low, ahead[0]) + dot(high, ahead[1]))
    return spec[:, :INNER], spec[:, INNER:]


def backward(re, im, twist, behind, last):
    high, low = split(jnp.concatenate([re, im], 1))
    turned = dot(high, behind[0]) + (dot(low, behind[0]) + dot(high, behind[1]))
    re = turned[:, :INNER].reshape(KEPT, GROUP, INNER)
    im = turned[:, INNER:].reshape(KEPT, GROUP, INNER)
    cos, sin = twist[0][:, None, :], twist[1][:, None, :]
    rows = jnp.concatenate([re * cos - im * sin, (re * sin + im * cos)[1:HALF]], 0)
    packed = jnp.concatenate(
        [rows[:, 8 * g : 8 * g + 8].reshape(8 * OUTER, INNER) for g in range(2)], 1
    )
    high, low = split(packed)
    field = dot(last[0], high) + (dot(last[0], low) + dot(last[1], high))
    return jnp.concatenate(
        [field[:, INNER * g : INNER * (g + 1)].reshape(HALF, 8, INNER) for g in range(2)], 1
    )


def conv_kernel(place_ref, fields_ref, skip_ref, table_ref, *refs):
    total_ref, spec_ref, *mixed_refs, hold_ref = refs[-7:]
    first, twist, ahead, behind, last = unpack(table_ref)
    gated = fields_ref[:, 0].astype(f32)
    taps = fields_ref[:, 1].astype(f32)
    gated_re, gated_im = forward(gated, first, twist, ahead)
    taps_re, taps_im = forward(taps, first, twist, ahead)
    for place, part in enumerate((gated_re, gated_im, taps_re, taps_im)):
        spec_ref[place, 0] = part
    conv = backward(
        taps_re * gated_re - taps_im * gated_im,
        taps_re * gated_im + taps_im * gated_re,
        twist,
        behind,
        last,
    )
    total = conv + skip_ref[...][None] * gated
    total_ref[...] = total
    hold_ref[...] = (total * fields_ref[:, 2].astype(f32)).astype(bf16)
    for s, mixed_ref in enumerate(mixed_refs):
        x = lax.rem(place_ref[1] + s, 4)
        for core in range(2):
            for z in range(4):
                place = (core * 4 + z) * INNER
                mixed_ref[:, place : place + INNER] = hold_ref[z * 8 + x * 2 + core]


def corr_kernel(parts_ref, fields_ref, total_ref, spec_ref, skip_ref, table_ref, *refs):
    out_ref = refs[-1]
    first, twist, ahead, behind, last = unpack(table_ref)
    grad_mix = []
    for z in range(4):
        here = slice(z * INNER, (z + 1) * INNER)
        terms = [parts_ref[8 * n : 8 * n + 8, :, here].astype(f32) for n in range(4)]
        grad_mix.append((terms[0] + terms[1]) + (terms[2] + terms[3]))
    grad_mix = jnp.concatenate(grad_mix, 0)
    out_ref[:, 2] = (grad_mix * total_ref[...]).astype(bf16)
    gsig = grad_mix * fields_ref[:, 0].astype(f32)
    gsig_re, gsig_im = forward(gsig, first, twist, ahead, exact=False)
    gated_re, gated_im, taps_re, taps_im = [spec_ref[place, 0] for place in range(4)]
    grad_gated = backward(
        taps_re * gsig_re + taps_im * gsig_im,
        taps_re * gsig_im - taps_im * gsig_re,
        twist,
        behind,
        last,
    )
    out_ref[:, 0] = (grad_gated + skip_ref[...][None] * gsig).astype(bf16)
    grad_taps = backward(
        gated_re * gsig_re + gated_im * gsig_im,
        gated_re * gsig_im - gated_im * gsig_re,
        twist,
        behind,
        last,
    )
    out_ref[:, 1] = grad_taps.astype(bf16)


def params():
    return pltpu.CompilerParams(vmem_limit_bytes=VMEM_LIMIT)


def cost(flops, megabytes):
    return pl.CostEstimate(flops=flops, bytes_accessed=megabytes * 2**20, transcendentals=0)


def conv_call(place, fields, skip_rows, table, after):
    blocks, _, owned, inner = fields.shape
    steps = owned // GROUP
    spec_rows = KEPT * GROUP
    return pl.pallas_call(
        conv_kernel,
        grid=(steps,),
        in_specs=[
            pl.BlockSpec(memory_space=pltpu.SMEM),
            pl.BlockSpec((blocks, 3, GROUP, inner), lambda g: (0, 0, g, 0)),
            pl.BlockSpec((GROUP, inner), lambda g: (g, 0)),
            pl.BlockSpec(table.shape, lambda g: (0, 0)),
        ]
        + [pl.BlockSpec(memory_space=pl.ANY)] * len(after),
        out_specs=[
            pl.BlockSpec((blocks, GROUP, inner), lambda g: (0, g, 0)),
            pl.BlockSpec((4, 1, spec_rows, inner), lambda g: (0, g, 0, 0)),
        ]
        + [pl.BlockSpec((GROUP, 8 * inner), lambda g: (g, 0))] * 4,
        out_shape=[
            jax.ShapeDtypeStruct((blocks, owned, inner), f32),
            jax.ShapeDtypeStruct((4, steps, spec_rows, inner), f32),
        ]
        + [jax.ShapeDtypeStruct((owned, 8 * inner), bf16)] * 4,
        scratch_shapes=[pltpu.VMEM((blocks, GROUP, inner), bf16)],
        compiler_params=params(),
        cost_estimate=cost(10**9, 6),
        name="conv",
    )(place, fields, skip_rows, table, *after)


def corr_call(parts, fields, total, spec, skip_rows, table, after):
    blocks, owned, inner = total.shape
    steps = owned // GROUP
    spec_rows = KEPT * GROUP
    return pl.pallas_call(
        corr_kernel,
        grid=(steps,),
        in_specs=[
            pl.BlockSpec((blocks, GROUP, 4 * inner), lambda g: (0, g, 0)),
            pl.BlockSpec((blocks, 1, GROUP, inner), lambda g: (0, 2, g, 0)),
            pl.BlockSpec((blocks, GROUP, inner), lambda g: (0, g, 0)),
            pl.BlockSpec((4, 1, spec_rows, inner), lambda g: (0, g, 0, 0)),
            pl.BlockSpec((GROUP, inner), lambda g: (g, 0)),
            pl.BlockSpec(table.shape, lambda g: (0, 0)),
        ]
        + [pl.BlockSpec(memory_space=pl.ANY)] * len(after),
        out_specs=pl.BlockSpec((blocks, 3, GROUP, inner), lambda g: (0, 0, g, 0)),
        out_shape=jax.ShapeDtypeStruct((blocks, 3, owned, inner), bf16),
        compiler_params=params(),
        cost_estimate=cost(10**9, 6),
        name="corr",
    )(parts, fields, total, spec, skip_rows, table, *after)


def prep_kernel(key_ref, value_ref, taps_ref, query_ref, *refs):
    fields_ref = refs[-1]
    gated = key_ref[...].astype(f32) * value_ref[...].astype(f32)
    shape = fields_ref.shape[:1] + fields_ref.shape[2:]
    fields_ref[:, 0] = gated.T.astype(bf16).reshape(shape)
    fields_ref[:, 1] = taps_ref[...].astype(f32).T.astype(bf16).reshape(shape)
    fields_ref[:, 2] = query_ref[...].astype(f32).T.astype(bf16).reshape(shape)


def prep_call(key_proj, value_proj, filter_taps, query_proj, owned, after):
    toks, channels = key_proj.shape
    wide = 512
    tall = pl.BlockSpec((toks, wide), lambda n: (0, n))
    return pl.pallas_call(
        prep_kernel,
        grid=(channels // wide,),
        in_specs=[tall] * 4 + [pl.BlockSpec(memory_space=pl.ANY)] * len(after),
        out_specs=pl.BlockSpec((wide // owned, 3, owned, toks), lambda n: (n, 0, 0, 0)),
        out_shape=jax.ShapeDtypeStruct((channels // owned, 3, owned, toks), bf16),
        compiler_params=params(),
        cost_estimate=cost(10**7, 2),
        name="prep",
    )(key_proj, value_proj, filter_taps, query_proj, *after)


def last_kernel(corr_ref, key_ref, value_ref, grad_key_ref, grad_value_ref, grad_filter_ref, grad_query_ref):
    rows = corr_ref.shape[0] * corr_ref.shape[2]

    def turned(n):
        return corr_ref[:, n].astype(f32).reshape(rows, corr_ref.shape[3]).T

    grad_gated = turned(0)
    grad_key_ref[...] = (grad_gated * value_ref[...].astype(f32)).astype(bf16)
    grad_value_ref[...] = (grad_gated * key_ref[...].astype(f32)).astype(bf16)
    grad_filter_ref[...] = turned(1).astype(bf16)
    grad_query_ref[...] = turned(2).astype(bf16)


def last_call(corr, key_proj, value_proj):
    toks, channels = key_proj.shape
    owned = corr.shape[2]
    wide = 512
    tall = pl.BlockSpec((toks, wide), lambda n: (0, n))
    return pl.pallas_call(
        last_kernel,
        grid=(channels // wide,),
        in_specs=[pl.BlockSpec((wide // owned, 3, owned, toks), lambda n: (n, 0, 0, 0)), tall, tall],
        out_specs=[tall] * 4,
        out_shape=[jax.ShapeDtypeStruct((toks, channels), bf16)] * 4,
        compiler_params=params(),
        cost_estimate=cost(10**7, 3),
        name="last",
    )(corr, key_proj, value_proj)


def mix_kernel(place_ref, grad_out_ref, *refs):
    near_w, far_w, passed = refs[:4], refs[4:8], refs[8:12]
    parts, near_out, far_out = refs[13:16]
    weight, grad, sems, out_sems = refs[16:]
    my_z, my_x, my_core, my_y = (place_ref[n] for n in range(4))
    width = weight.shape[3]
    copies = []

    def begin(source, target):
        copy = pltpu.make_async_copy(source, target, sems.at[len(copies)])
        copy.start()
        copies.append(copy)

    for back in range(4):
        col = lax.rem(my_x - back + 4, 4)
        begin(near_w[back], weight.at[my_core, col])
        begin(far_w[back], weight.at[1 - my_core, col])
    for back in range(4):
        for core in range(2):
            for s in range(1, 4):
                begin(
                    passed[back].at[s - 1, :, pl.ds(core * width, width)],
                    grad.at[lax.rem(my_y - back + 4, 4), core, lax.rem(my_z - s + 4, 4)],
                )
    for col in range(4):
        for core in range(2):
            start = pl.multiple_of(((my_z * 4 + col) * 2 + core) * width, width)
            begin(grad_out_ref.at[:, pl.ds(start, width)], grad.at[col, core, my_z])
    for copy in copies:
        copy.wait()

    near_copy = pltpu.make_async_copy(grad.at[:, my_core], near_out, out_sems.at[0])
    far_copy = pltpu.make_async_copy(grad.at[:, 1 - my_core], far_out, out_sems.at[1])
    near_copy.start()
    far_copy.start()

    step = 256
    for pair in ((0, 1), (2, 3)):
        lines = [jnp.concatenate([grad[n // 2, n % 2, z] for n in range(8)], 1) for z in pair]
        grad_rows = jnp.concatenate(lines, 0)
        toks = grad_rows.shape[0]

        def body(m, _, grad_rows=grad_rows, pair=pair, toks=toks):
            here = pl.ds(pl.multiple_of(m * step, step), step)
            rows = jnp.concatenate([weight[n % 2, n // 2, here, :] for n in range(8)], 1)
            part = lax.dot_general(
                rows, grad_rows, (((1,), (1,)), ((), ())), preferred_element_type=f32
            )
            start = pair[0] // 2 * toks
            parts[here, start : start + toks] = part.astype(bf16)
            return 0

        lax.fori_loop(0, weight.shape[2] // step, body, 0)
    near_copy.wait()
    far_copy.wait()


def mix_call(place, grad_out, near_w, far_w, passed, after):
    toks = grad_out.shape[0]
    rows, width = near_w[0].shape
    any_spec = pl.BlockSpec(memory_space=pl.ANY)
    vmem = pl.BlockSpec(memory_space=pltpu.VMEM)
    blocks = jax.ShapeDtypeStruct((4, 4, toks, width), bf16)
    return pl.pallas_call(
        mix_kernel,
        in_specs=[pl.BlockSpec(memory_space=pltpu.SMEM)] + [any_spec] * 14,
        out_specs=[vmem] + [any_spec] * 2,
        out_shape=[jax.ShapeDtypeStruct((rows, 4 * toks), bf16)] + [blocks] * 2,
        scratch_shapes=[
            pltpu.VMEM((2, 4, rows, width), bf16),
            pltpu.VMEM((4, 2, 4, toks, width), bf16),
            pltpu.SemaphoreType.DMA((40,)),
            pltpu.SemaphoreType.DMA((2,)),
        ],
        compiler_params=params(),
        cost_estimate=cost(2 * rows * toks * 4 * 8 * width, 9),
        name="mix",
    )(place, grad_out, *near_w, *far_w, *passed, after)


def product_kernel(cols_ref, *refs):
    mixed, near, far, outs = refs[:8], refs[8], refs[9], refs[11:]
    my_z, my_core = cols_ref[4], cols_ref[5]
    my_x = cols_ref[6]
    xs, owned, depth = mixed[0].shape
    half = depth // 2
    lines = [
        jnp.concatenate([mixed[4 * n + s][...].reshape(xs * owned, depth) for s in range(4)], 0)
        for n in range(2)
    ]
    for n, out in enumerate(outs):
        col = cols_ref[n]
        own = near[col].reshape(half, near.shape[3])
        other = far[col].reshape(half, far.shape[3])
        columns = jnp.concatenate(
            [jnp.where(my_core == 0, own, other), jnp.where(my_core == 0, other, own)], 0
        )
        for core, rows in zip((my_core, 1 - my_core), lines):
            product = dot(rows, columns).astype(out.dtype).reshape(4, xs, owned, near.shape[3])
            for s in range(4):
                for t in range(4):
                    z, x = lax.rem(my_z - s + 4, 4), lax.rem(my_x - t + 4, 4)
                    out[z, x, core] = product[s, t]


def product_call(cols, mixed, near, far, after, kinds):
    xs, owned, depth = mixed[0].shape
    width = near.shape[3]
    vmem = pl.BlockSpec(memory_space=pltpu.VMEM)
    return pl.pallas_call(
        product_kernel,
        in_specs=[pl.BlockSpec(memory_space=pltpu.SMEM)]
        + [vmem] * 10
        + [pl.BlockSpec(memory_space=pl.ANY)],
        out_specs=[vmem] * len(kinds),
        out_shape=[jax.ShapeDtypeStruct((4, xs, 2, owned, width), kind) for kind in kinds],
        compiler_params=params(),
        cost_estimate=cost(16 * xs * owned * width * depth * len(kinds), 5),
        name="product",
    )(cols, *mixed, near, far, after)


def shards(grad_out, out_weight, query_proj, key_proj, value_proj, filter_taps, skip_gain):
    tok_rows = grad_out.shape[0]
    context_size = lax.axis_size(CTX)
    seq_len = tok_rows * context_size
    group_width, width = out_weight.shape
    owned = group_width // context_size
    norm_scale = 1.0 / math.sqrt(seq_len)
    my_z, my_x, my_core, my_y = (lax.axis_index(name) for name in ("zh", "x", "core", "y"))
    table = jnp.asarray(tables(seq_len))
    order = (1, 3, 2)

    def shift(item, axis, by):
        size = lax.axis_size(axis)
        return lax.ppermute(item, axis, [(n, (n + by) % size) for n in range(size)])

    def swap(item):
        return shift(item, "core", 1)

    def to_all(item):
        return lax.all_to_all(item, CTX, split_axis=0, concat_axis=0, tiled=True)

    passed, near_w = {}, {0: out_weight}
    for s in order:
        start = ((my_z + s) % 4 * 4 + my_y) * (2 * width)
        passed[s] = shift(lax.dynamic_slice_in_dim(grad_out, start, 2 * width, 1), "zh", s)
        if s != 2:
            near_w[s] = shift(out_weight, "x", s)
    passed = {0: jnp.stack([passed[s] for s in range(1, 4)])}
    late_w = lax.optimization_barrier((out_weight, passed[0]))[0]
    near_w[2] = shift(late_w, "x", 2)
    for s in order:
        passed[s] = shift(passed[0], "y", s)
    held = lax.optimization_barrier((*near_w.values(), *passed.values()))
    far_w = {s: swap(item) for s, item in zip(near_w, held)}
    far_w = [far_w[s] for s in range(4)]

    fields = prep_call(key_proj, value_proj, filter_taps, query_proj, owned, [near_w[1], near_w[3], passed[0]])
    fields = to_all(fields)

    place = jnp.stack([my_z, my_x, my_core, my_y]).astype(jnp.int32)
    skip_rows = lax.dynamic_slice_in_dim(
        skip_gain, lax.axis_index(CTX) * owned, owned, 0
    )
    skip_rows = jnp.broadcast_to(skip_rows[:, None], (owned, tok_rows))
    total, spec, *mixed = conv_call(place, fields, skip_rows, table, [])
    mixed = jnp.stack(mixed[:1] + [shift(mixed[s], "x", s) for s in range(1, 4)])

    parts, near, far = mix_call(
        place, grad_out, [near_w[s] for s in range(4)], far_w, [passed[s] for s in range(4)], total
    )
    mixed = lax.optimization_barrier((mixed, parts))[0]
    far = swap(far)
    parts = to_all(parts.reshape(context_size, owned, 4 * tok_rows))

    mixed = [mixed] + [shift(mixed, "zh", s) for s in range(1, 4)]
    corr = corr_call(parts, fields, total, spec, skip_rows, table, [mixed[s] for s in order])
    mixed += [swap(item) for item in mixed]

    cols = [(my_x + s) % 4 for s in (2, 1, 3, 0)]
    near_cols = jnp.stack(cols + [my_z, my_core, my_x]).astype(jnp.int32)
    last_cols = jnp.stack(cols[3:] * 4 + [my_z, my_core, my_x]).astype(jnp.int32)
    sent = product_call(near_cols, mixed, near, far, corr, (bf16,) * 3)
    sent = {s: shift(item, "x", s) for s, item in zip((2, 1, 3), sent)}
    grad_weight = product_call(last_cols, mixed, near, far, corr, (f32,))[0]
    corr = to_all(corr)
    grad_key, grad_value, grad_filter, grad_query = last_call(corr, key_proj, value_proj)
    for s in (1, 3, 2):
        grad_weight = grad_weight + sent[s].astype(f32)
    grad_weight = (grad_weight * norm_scale).astype(bf16).reshape(group_width, width)
    return (grad_query, grad_key, grad_value, grad_filter, grad_weight)


def solution(mesh):
    fine = Mesh(mesh.devices.reshape(4, 4, 2, 2, 4), CTX + TEN)
    rows_cols = P(CTX, TEN)
    in_specs = (P(CTX, None), P(TEN, CTX)) + (rows_cols,) * 4 + (P(TEN),)
    out_specs = (rows_cols,) * 4 + (P(TEN, CTX),)
    return jax.shard_map(
        shards, mesh=fine, in_specs=in_specs, out_specs=out_specs, check_vma=False
    )
```

time: 261 us -> 202 us (0.77)
  local copies, waits for them, and re-layouts: 40.2 us -> 9.76 us
  matrix products: 12.6 us -> 0 us
  starting transfers between devices: 81.4 us -> 70.3 us
    unnamed x67 -> x54, local copies, waits for them, and re-layouts: 25.6 us -> 5.96 us
    all_to_all x4 -> x3, starting transfers between devices: 41.2 us -> 27.5 us  [to_all(): return lax.all_to_all(item, CTX, split_axis=0, concat_axis=0, tiled=True)]
    dot_general x4 -> x0, matrix products: 12.6 us -> none  [dot(): return jnp.dot(a, b, preferred_element_type=f32)]
    ppermute x24 -> x27, waiting for transfers between devices: 75.1 us -> 80.3 us  [shift(): return lax.ppermute(item, axis, [(n, (n + by) % size) for n in range(size)])]
    slice x5 -> x0, local copies, waits for them, and re-layouts: 5.04 us -> none  [the longest x4 5 us: shards(): far = [swap(grads[s][size_z:]) for s in range(size_x)]]
    pallas_call x6, Pallas kernels: 33.2 us -> 29 us  [the longest x2 9.02 us: product_call(): pl.pallas_call(product_kernel, in_specs=[pl.BlockSpec(memory_space=pltpu....]
    concatenate x2 -> x0, local copies, waits for them, and re-layouts: 3.99 us -> none  [the longest x1 2.35 us: shards(): lines = jnp.concatenate([lines, swap(lines)], 1)]
    all_to_all x4 -> x3, waiting for transfers between devices: 2.63 us -> 0.01 us  [to_all(): return lax.all_to_all(item, CTX, split_axis=0, concat_axis=0, tiled=True)]
  transfers between devices with their start and end apart: 28 -> 30, of which waited for: 10 -> 14; matrix products, arithmetic and copies ran while one was open for 18% -> 4% of each run, Pallas kernels for 15% -> 12%
where the time goes in v2:
time: 202 us; the launch traced here: 201 us
  waiting for transfers between devices  80.3 us (40%)
  starting transfers between devices  70.3 us (35%)
  Pallas kernels  36.3 us (18%)
  local copies, waits for them, and re-layouts  9.76 us (5%)
  other arithmetic  3.8 us (2%)
    ppermute x27, waiting for transfers between devices, shift(): return lax.ppermute(item, axis, [(n, (n + by) % size) for n in range(size)])  80.3 us
    ppermute x27, starting transfers between devices, shift(): return lax.ppermute(item, axis, [(n, (n + by) % size) for n in range(size)])  42.8 us
    all_to_all x3, starting transfers between devices, to_all(): return lax.all_to_all(item, CTX, split_axis=0, concat_axis=0, tiled=True)  27.5 us
    pallas_call x2, Pallas kernels, product_call(): pl.pallas_call(product_kernel, in_specs=[pl.BlockSpec(memory_space=pltpu....  9.02 us
    pallas_call x1, Pallas kernels, mix_call(): pl.pallas_call(mix_kernel, in_specs=[pl.BlockSpec(memory_space=pltpu.SMEM...  8.57 us
    pallas_call x1, Pallas kernels, corr_call(): pl.pallas_call(corr_kernel, grid=(steps,), in_specs=[pl.BlockSpec((blocks...  7.32 us
    pallas_call x1, Pallas kernels, conv_call(): pl.pallas_call(conv_kernel, grid=(steps,), in_specs=[pl.BlockSpec(memory_...  6.95 us
    unnamed x54, local copies, waits for them, and re-layouts  5.96 us
  transfers between devices with their start and end apart: 30, of which 14 were waited for; matrix products, arithmetic and copies ran while one was open for 4% of the time, Pallas kernels for 12%

profile of v2, /device:TPU:1, one launch (start us, length us, event | category | flops | bytes accessed | tf_op | source)
XLA Modules:
  0.0 201.5 jit_solution(966822670441005357)
XLA Ops:
  0.6 3.4 %collective-permute-start.5 = (bf16[1024,256]{1,0:T(8,128)(2,1)}, bf16[1024,256]{1,0:T(8,128)(2,1)S(1)}, u32[]{:S(2)}, u32[]{:S(2)}) collective-permute-start(bf16[1024,256]{1,0:T(8,128)(2,1)} %refs_0_.1), channel_id=1, source_target_pairs={{0,48},{16,0},{32,16},{48,32},{1,49},{17,1},{33,17},{49,33},{2,50}... | collective-permute-start | bytes 1572872 | tf_op jit(solution)/shard_map/ppermute | solution.py:427
  4.0 1.1 constant_dynamic-slice_fusion.2
  5.1 3.1 %collective-permute-start.1 = (bf16[128,512]{1,0:T(8,128)(2,1)S(1)}, bf16[128,512]{1,0:T(8,128)(2,1)S(1)}, u32[]{:S(2)}, u32[]{:S(2)}) collective-permute-start(bf16[128,512]{1,0:T(8,128)(2,1)S(1)} %get-tuple-element.49), channel_id=1, source_target_pairs={{0,64},{64,128},{128,192},{192,0},{1,65},{65,129},{129,193},{193,1... | collective-permute-start | bytes 393224 | tf_op jit(solution)/shard_map/ppermute | solution.py:427
  8.1 5.1 %collective-permute-start.2 = (bf16[128,512]{1,0:T(8,128)(2,1)S(1)}, bf16[128,512]{1,0:T(8,128)(2,1)S(1)}, u32[]{:S(2)}, u32[]{:S(2)}) collective-permute-start(bf16[128,512]{1,0:T(8,128)(2,1)S(1)} %get-tuple-element.50), channel_id=1, source_target_pairs={{0,128},{64,192},{128,0},{192,64},{1,129},{65,193},{129,1},{193,65... | collective-permute-start | bytes 393224 | tf_op jit(solution)/shard_map/ppermute | solution.py:427
  13.3 2.4 %collective-permute-start.3 = (bf16[128,512]{1,0:T(8,128)(2,1)S(1)}, bf16[128,512]{1,0:T(8,128)(2,1)S(1)}, u32[]{:S(2)}, u32[]{:S(2)}) collective-permute-start(bf16[128,512]{1,0:T(8,128)(2,1)S(1)} %get-tuple-element.51), channel_id=1, source_target_pairs={{0,192},{64,0},{128,64},{192,128},{1,193},{65,1},{129,65},{193,129... | collective-permute-start | bytes 393224 | tf_op jit(solution)/shard_map/ppermute | solution.py:427
  15.6 5.6 %collective-permute-done.2 = bf16[128,512]{1,0:T(8,128)(2,1)S(1)} collective-permute-done((bf16[128,512]{1,0:T(8,128)(2,1)S(1)}, bf16[128,512]{1,0:T(8,128)(2,1)S(1)}, u32[]{:S(2)}, u32[]{:S(2)}) %collective-permute-start.2) | collective-permute-done | bytes 131104 | tf_op jit(solution)/shard_map/ppermute | solution.py:427
  21.3 4.9 %collective-permute-done.3 = bf16[128,512]{1,0:T(8,128)(2,1)S(1)} collective-permute-done((bf16[128,512]{1,0:T(8,128)(2,1)S(1)}, bf16[128,512]{1,0:T(8,128)(2,1)S(1)}, u32[]{:S(2)}, u32[]{:S(2)}) %collective-permute-start.3) | collective-permute-done | bytes 131104 | tf_op jit(solution)/shard_map/ppermute | solution.py:427
  26.2 0.8 pad_maximum_fusion.refs_2_.refs_8_
  27.0 0.8 copy-done.4
  27.8 0.8 copy-done.5
  28.6 2.2 %prep.1 = bf16[32,3,32,128]{3,2,1,0:T(8,128)(2,1)} custom-call(bf16[128,1024]{1,0:T(8,128)(2,1)} %key_ref.3, bf16[128,1024]{1,0:T(8,128)(2,1)} %value_ref.3, bf16[128,1024]{1,0:T(8,128)(2,1)} %taps_ref.1, bf16[128,1024]{1,0:T(8,128)(2,1)} %query_ref.1, bf16[1024,256]{1,0:T(8,128)(2,1)} %copy-done.5, bf16[1024,256]{1,0:T(8,128)(2,1)} %copy-done.4, ...), custom_call_target="tpu_custom_call" | custom-call | flops 10000000 | bytes 2097152 | tf_op jit(solution)/shard_map/prep/pallas_call | solution.py:250
  30.8 8.6 %all-to-all-start = ((bf16[32,3,32,128]{3,2,1,0:T(8,128)(2,1)}), bf16[32,3,32,128]{3,2,1,0:T(8,128)(2,1)S(1)}, u32[]{:S(2)}, u32[]{:S(2)}) async-start(bf16[32,3,32,128]{3,2,1,0:T(8,128)(2,1)} %prep.1), calls=%async_computation | async-start | bytes 1572864 | tf_op jit(solution)/shard_map/all_to_all | solution.py:433
  39.4 3.0 %collective-permute-start.4 = (bf16[1024,256]{1,0:T(8,128)(2,1)S(1)}, bf16[1024,256]{1,0:T(8,128)(2,1)S(1)}, u32[]{:S(2)}, u32[]{:S(2)}) collective-permute-start(bf16[1024,256]{1,0:T(8,128)(2,1)S(1)} %copy-done.11), channel_id=1, source_target_pairs={{0,32},{16,48},{32,0},{48,16},{1,33},{17,49},{33,1},{49,17},{2,34}... | collective-permute-start | bytes 1572872 | tf_op jit(solution)/shard_map/ppermute | solution.py:427
  42.4 2.9 %collective-permute-start.8 = (bf16[3,128,512]{2,1,0:T(8,128)(2,1)S(1)}, bf16[3,128,512]{2,1,0:T(8,128)(2,1)S(1)}, u32[]{:S(2)}, u32[]{:S(2)}) collective-permute-start(bf16[3,128,512]{2,1,0:T(8,128)(2,1)S(1)} %copy-done.1), channel_id=1, source_target_pairs={{0,2},{1,3},{2,0},{3,1},{4,6},{5,7},{6,4},{7,5},{8,10},{9,11},{10,... | collective-permute-start | bytes 1179656 | tf_op jit(solution)/shard_map/ppermute | solution.py:427
  45.3 0.8 collective-permute-start.7
  46.1 0.7 collective-permute-start.6
  46.8 7.2 %collective-permute-done.8.refs_10_ = bf16[3,128,512]{2,1,0:T(8,128)(2,1)S(1)} collective-permute-done((bf16[3,128,512]{2,1,0:T(8,128)(2,1)S(1)}, bf16[3,128,512]{2,1,0:T(8,128)(2,1)S(1)}, u32[]{:S(2)}, u32[]{:S(2)}) %collective-permute-start.8) | collective-permute-done | bytes 393248 | tf_op jit(solution)/shard_map/ppermute | solution.py:427
  54.0 8.8 %collective-permute-done.7.refs_11_ = bf16[3,128,512]{2,1,0:T(8,128)(2,1)S(1)} collective-permute-done((bf16[3,128,512]{2,1,0:T(8,128)(2,1)S(1)}, bf16[3,128,512]{2,1,0:T(8,128)(2,1)S(1)}, u32[]{:S(2)}, u32[]{:S(2)}) %collective-permute-start.7) | collective-permute-done | bytes 393248 | tf_op jit(solution)/shard_map/ppermute | solution.py:427
  62.7 0.6 collective-permute-done.6.refs_9_
  63.4 1.0 collective-permute-start.9
  64.5 0.5 collective-permute-start.11
  65.1 0.8 dynamic_slice.15
  65.9 0.6 pad_add_fusion.place_ref
  66.5 0.8 broadcast_in_dim.2.skip_ref
  67.4 7.0 %conv.1 = (f32[32,32,128]{2,1,0:T(8,128)}, f32[4,2,528,128]{3,2,1,0:T(8,128)}, bf16[32,1024]{1,0:T(8,128)(2,1)}, bf16[32,1024]{1,0:T(8,128)(2,1)}, bf16[32,1024]{1,0:T(8,128)(2,1)}, /*index=5*/bf16[32,1024]{1,0:T(8,128)(2,1)}) custom-call(s32[4]{0:T(128)} %pad_add_fusion.place_ref, bf16[32,3,32,128]{3,2,1,0:T(8,128)(2,1)} %copy-done.2, ...), custom_call_target="tpu_custom_call" | custom-call | flops 1000000000 | bytes 6291456 | tf_op jit(solution)/shard_map/conv/pallas_call | solution.py:186
  74.4 0.7 copy-done.13
  75.5 8.6 %mix.1 = (bf16[1024,512]{1,0:T(8,128)(2,1)}, bf16[4,4,128,256]{3,2,1,0:T(8,128)(2,1)}, bf16[4,4,128,256]{3,2,1,0:T(8,128)(2,1)}) custom-call(s32[4]{0:T(128)} %pad_add_fusion.place_ref, bf16[128,8192]{1,0:T(8,128)(2,1)} %grad_out_ref.1, bf16[1024,256]{1,0:T(8,128)(2,1)} %refs_0_.1, bf16[1024,256]{1,0:T(8,128)(2,1)} %copy-done.5, ...), custom_call_target="tpu_custom_call" | custom-call | flops 2147483648 | bytes 9437184 | tf_op jit(solution)/shard_map/mix/pallas_call | solution.py:355
  84.2 7.9 %all-to-all-start.1 = ((bf16[32,32,512]{2,1,0:T(8,128)(2,1)}), bf16[32,32,512]{2,1,0:T(8,128)(2,1)S(1)}, u32[]{:S(2)}, u32[]{:S(2)}) async-start(bf16[32,32,512]{2,1,0:T(8,128)(2,1)} %bitcast.17), calls=%async_computation.1 | async-start | bytes 2097152 | tf_op jit(solution)/shard_map/all_to_all | solution.py:433
  92.1 1.5 collective-permute-start.13
  93.6 2.4 %collective-permute-start.14 = (bf16[32,1024]{1,0:T(8,128)(2,1)S(1)}, bf16[32,1024]{1,0:T(8,128)(2,1)S(1)}, u32[]{:S(2)}, u32[]{:S(2)}) collective-permute-start(bf16[32,1024]{1,0:T(8,128)(2,1)S(1)} %copy-done.25), channel_id=1, source_target_pairs={{0,32},{16,48},{32,0},{48,16},{1,33},{17,49},{33,1},{49,17},{2,34}... | collective-permute-start | bytes 196616 | tf_op jit(solution)/shard_map/ppermute | solution.py:427
  96.0 1.2 collective-permute-start.15
  97.1 1.2 collective-permute-start.23
  98.3 1.4 collective-permute-done.13
  99.8 2.2 %collective-permute-done.14 = bf16[32,1024]{1,0:T(8,128)(2,1)S(1)} collective-permute-done((bf16[32,1024]{1,0:T(8,128)(2,1)S(1)}, bf16[32,1024]{1,0:T(8,128)(2,1)S(1)}, u32[]{:S(2)}, u32[]{:S(2)}) %collective-permute-start.14) | collective-permute-done | bytes 65568 | tf_op jit(solution)/shard_map/ppermute | solution.py:427
  102.0 5.7 %collective-permute-start.18 = (bf16[4,32,1024]{2,1,0:T(8,128)(2,1)S(1)}, bf16[4,32,1024]{2,1,0:T(8,128)(2,1)S(1)}, u32[]{:S(2)}, u32[]{:S(2)}) collective-permute-start(bf16[4,32,1024]{2,1,0:T(8,128)(2,1)S(1)} %pad_maximum_fusion.1.refs_0_), channel_id=1, source_target_pairs={{0,128},{64,192},{128,0},{192,64},{1,129},{65,193},{129,1},{193,65... | collective-permute-start | bytes 786440 | tf_op jit(solution)/shard_map/ppermute | solution.py:427
  107.8 2.4 %collective-permute-start.16 = (bf16[4,32,1024]{2,1,0:T(8,128)(2,1)S(1)}, bf16[4,32,1024]{2,1,0:T(8,128)(2,1)S(1)}, u32[]{:S(2)}, u32[]{:S(2)}) collective-permute-start(bf16[4,32,1024]{2,1,0:T(8,128)(2,1)S(1)} %pad_maximum_fusion.1.refs_0_), channel_id=1, source_target_pairs={{0,64},{64,128},{128,192},{192,0},{1,65},{65,129},{129,193},{193,1... | collective-permute-start | bytes 786440 | tf_op jit(solution)/shard_map/ppermute | solution.py:427
  110.1 18.9 %collective-permute-done.18.refs_2_ = bf16[4,32,1024]{2,1,0:T(8,128)(2,1)S(1)} collective-permute-done((bf16[4,32,1024]{2,1,0:T(8,128)(2,1)S(1)}, bf16[4,32,1024]{2,1,0:T(8,128)(2,1)S(1)}, u32[]{:S(2)}, u32[]{:S(2)}) %collective-permute-start.18) | collective-permute-done | bytes 262176 | tf_op jit(solution)/shard_map/ppermute | solution.py:427
  129.1 6.9 %collective-permute-done.16.refs_0_.refs_1_ = bf16[4,32,1024]{2,1,0:T(8,128)(2,1)S(1)} collective-permute-done((bf16[4,32,1024]{2,1,0:T(8,128)(2,1)S(1)}, bf16[4,32,1024]{2,1,0:T(8,128)(2,1)S(1)}, u32[]{:S(2)}, u32[]{:S(2)}) %collective-permute-start.16) | collective-permute-done | bytes 262176 | tf_op jit(solution)/shard_map/ppermute | solution.py:427
  135.9 0.7 copy-done.8
  136.6 0.4 copy-done
  137.0 7.3 %corr.1.refs_10_ = bf16[32,3,32,128]{3,2,1,0:T(8,128)(2,1)} custom-call(bf16[32,32,512]{2,1,0:T(8,128)(2,1)} %copy-done, bf16[32,3,32,128]{3,2,1,0:T(8,128)(2,1)} %copy-done.2, f32[32,32,128]{2,1,0:T(8,128)} %get-tuple-element.32.refs_12_.total_ref, f32[4,2,528,128]{3,2,1,0:T(8,128)} %get-tuple-element.34.spec_ref, f32[32,128]{1,0:T(8,128)} %broadcast_in_dim.2.skip_ref, ...), custom_call_target="tpu_custom_call" | custom-call | flops 1000000000 | bytes 6291456 | tf_op jit(solution)/shard_map/corr/pallas_call | solution.py:217
  144.3 11.0 %all-to-all-start.2 = ((bf16[32,3,32,128]{3,2,1,0:T(8,128)(2,1)}), bf16[32,3,32,128]{3,2,1,0:T(8,128)(2,1)S(1)}, u32[]{:S(2)}, u32[]{:S(2)}) async-start(bf16[32,3,32,128]{3,2,1,0:T(8,128)(2,1)} %corr.1.refs_10_), calls=%async_computation.2 | async-start | bytes 1572864 | tf_op jit(solution)/shard_map/all_to_all | solution.py:433
  155.3 0.3 collective-permute-start.19
  155.7 0.3 collective-permute-start.21
  155.9 0.2 collective-permute-start.22
  156.2 0.3 collective-permute-start.20
  156.5 0.6 stack.89.cols_ref
  157.1 0.5 collective-permute-done.21.refs_6_
  157.6 0.4 collective-permute-done.22.refs_7_
  157.9 0.4 collective-permute-done.20.refs_5_
  158.3 0.3 copy-done.21
  158.6 0.4 copy-done.22
  159.0 0.4 copy-done.10
  159.4 5.1 %product.3 = (bf16[4,4,2,32,256]{4,3,2,1,0:T(8,128)(2,1)}, bf16[4,4,2,32,256]{4,3,2,1,0:T(8,128)(2,1)}, bf16[4,4,2,32,256]{4,3,2,1,0:T(8,128)(2,1)}) custom-call(s32[7]{0:T(128)} %stack.89.cols_ref, bf16[4,32,1024]{2,1,0:T(8,128)(2,1)} %copy-done.9, bf16[4,32,1024]{2,1,0:T(8,128)(2,1)} %copy-done.8, bf16[4,32,1024]{2,1,0:T(8,128)(2,1)} %copy-done.6, ...), custom_call_target="tpu_custom_call" | custom-call | flops 1610612736 | bytes 5242880 | tf_op jit(solution)/shard_map/product/pallas_call | solution.py:401
  164.5 1.4 collective-permute-start.24
  165.9 1.3 collective-permute-start.25
  167.2 1.7 collective-permute-start.26
  168.9 0.6 stack.85.cols_ref
  169.5 3.9 %product.2 = f32[4,4,2,32,256]{4,3,2,1,0:T(8,128)} custom-call(s32[7]{0:T(128)} %stack.85.cols_ref, bf16[4,32,1024]{2,1,0:T(8,128)(2,1)} %copy-done.9, bf16[4,32,1024]{2,1,0:T(8,128)(2,1)} %copy-done.8, bf16[4,32,1024]{2,1,0:T(8,128)(2,1)} %copy-done.6, bf16[4,32,1024]{2,1,0:T(8,128)(2,1)} %copy-done.7, bf16[4,32,1024]{2,1,0:T(8,128)(2,1)} %copy-done.19, ...), custom_call_target="tpu_custom_call" | custom-call | flops 536870912 | bytes 5242880 | tf_op jit(solution)/shard_map/product/pallas_call | solution.py:401
  173.4 10.4 %collective-permute-done.24 = bf16[4,4,2,32,256]{4,3,2,1,0:T(8,128)(2,1)S(1)} collective-permute-done((bf16[4,4,2,32,256]{4,3,2,1,0:T(8,128)(2,1)}, bf16[4,4,2,32,256]{4,3,2,1,0:T(8,128)(2,1)S(1)}, u32[]{:S(2)}, u32[]{:S(2)}) %collective-permute-start.24) | collective-permute-done | bytes 524320 | tf_op jit(solution)/shard_map/ppermute | solution.py:427
  183.8 12.1 %collective-permute-done.26 = bf16[4,4,2,32,256]{4,3,2,1,0:T(8,128)(2,1)S(1)} collective-permute-done((bf16[4,4,2,32,256]{4,3,2,1,0:T(8,128)(2,1)}, bf16[4,4,2,32,256]{4,3,2,1,0:T(8,128)(2,1)S(1)}, u32[]{:S(2)}, u32[]{:S(2)}) %collective-permute-start.26) | collective-permute-done | bytes 524320 | tf_op jit(solution)/shard_map/ppermute | solution.py:427
  195.9 2.4 %multiply_convert_fusion = bf16[4,4,2,32,256]{4,3,2,1,0:T(8,128)(2,1)} fusion(bf16[4,4,2,32,256]{4,3,2,1,0:T(8,128)(2,1)S(1)} %collective-permute-done.26, bf16[4,4,2,32,256]{4,3,2,1,0:T(8,128)(2,1)S(1)} %collective-permute-done.25, f32[4,4,2,32,256]{4,3,2,1,0:T(8,128)} %product.2, bf16[4,4,2,32,256]{4,3,2,1,0:T(8,128)(2,1)S(1)} %collective-permute-done.24), kind=kLoop, calls=%fused_computation | loop fusion | flops 2097152 | bytes 3145728 | tf_op jit(solution)/shard_map/convert_element_type | solution.py:482
  198.3 0.9 copy-done.3
  199.2 2.2 %last.1 = (bf16[128,1024]{1,0:T(8,128)(2,1)}, bf16[128,1024]{1,0:T(8,128)(2,1)}, bf16[128,1024]{1,0:T(8,128)(2,1)}, bf16[128,1024]{1,0:T(8,128)(2,1)}) custom-call(bf16[32,3,32,128]{3,2,1,0:T(8,128)(2,1)} %copy-done.3, bf16[128,1024]{1,0:T(8,128)(2,1)} %key_ref.3, bf16[128,1024]{1,0:T(8,128)(2,1)} %value_ref.3), custom_call_target="tpu_custom_call" | custom-call | flops 10000000 | bytes 3145728 | tf_op jit(solution)/shard_map/last/pallas_call | solution.py:280
  (66 shorter events, 0.9 us)
Async XLA Ops:
  0.6 26.4 %collective-permute-start.5 = (bf16[1024,256]{1,0:T(8,128)(2,1)}, bf16[1024,256]{1,0:T(8,128)(2,1)S(1)}, u32[]{:S(2)}, u32[]{:S(2)}) collective-permute-start(bf16[1024,256]{1,0:T(8,128)(2,1)} %refs_0_.1), channel_id=1, source_target_pairs={{0,48},{16,0},{32,16},{48,32},{1,49},{17,1},{33,17},{49,33},{2,50}... | collective-permute-start | bytes 1572872 | tf_op jit(solution)/shard_map/ppermute | solution.py:427
  4.0 23.0 %collective-permute-start = (bf16[1024,256]{1,0:T(8,128)(2,1)}, bf16[1024,256]{1,0:T(8,128)(2,1)S(1)}, u32[]{:S(2)}, u32[]{:S(2)}) collective-permute-start(bf16[1024,256]{1,0:T(8,128)(2,1)} %refs_0_.1), channel_id=1, source_target_pairs={{0,16},{16,32},{32,48},{48,0},{1,17},{17,33},{33,49},{49,1},{2,18}... | collective-permute-start | bytes 1572872 | tf_op jit(solution)/shard_map/ppermute | solution.py:427
  5.1 10.6 %collective-permute-start.1 = (bf16[128,512]{1,0:T(8,128)(2,1)S(1)}, bf16[128,512]{1,0:T(8,128)(2,1)S(1)}, u32[]{:S(2)}, u32[]{:S(2)}) collective-permute-start(bf16[128,512]{1,0:T(8,128)(2,1)S(1)} %get-tuple-element.49), channel_id=1, source_target_pairs={{0,64},{64,128},{128,192},{192,0},{1,65},{65,129},{129,193},{193,1... | collective-permute-start | bytes 393224 | tf_op jit(solution)/shard_map/ppermute | solution.py:427
  8.1 13.1 %collective-permute-start.2 = (bf16[128,512]{1,0:T(8,128)(2,1)S(1)}, bf16[128,512]{1,0:T(8,128)(2,1)S(1)}, u32[]{:S(2)}, u32[]{:S(2)}) collective-permute-start(bf16[128,512]{1,0:T(8,128)(2,1)S(1)} %get-tuple-element.50), channel_id=1, source_target_pairs={{0,128},{64,192},{128,0},{192,64},{1,129},{65,193},{129,1},{193,65... | collective-permute-start | bytes 393224 | tf_op jit(solution)/shard_map/ppermute | solution.py:427
  13.3 12.9 %collective-permute-start.3 = (bf16[128,512]{1,0:T(8,128)(2,1)S(1)}, bf16[128,512]{1,0:T(8,128)(2,1)S(1)}, u32[]{:S(2)}, u32[]{:S(2)}) collective-permute-start(bf16[128,512]{1,0:T(8,128)(2,1)S(1)} %get-tuple-element.51), channel_id=1, source_target_pairs={{0,192},{64,0},{128,64},{192,128},{1,193},{65,1},{129,65},{193,129... | collective-permute-start | bytes 393224 | tf_op jit(solution)/shard_map/ppermute | solution.py:427
  27.0 12.4 %copy-start.11 = (bf16[1024,256]{1,0:T(8,128)(2,1)S(1)}, bf16[1024,256]{1,0:T(8,128)(2,1)}, u32[]{:S(2)}) copy-start(bf16[1024,256]{1,0:T(8,128)(2,1)} %refs_0_.1) | copy-start | bytes 1572868
  27.0 15.4 %copy-start.1 = (bf16[3,128,512]{2,1,0:T(8,128)(2,1)S(1)}, bf16[3,128,512]{2,1,0:T(8,128)(2,1)}, u32[]{:S(2)}) copy-start(bf16[3,128,512]{2,1,0:T(8,128)(2,1)} %pad_maximum_fusion.refs_2_.refs_8_) | copy-start | bytes 1179652
  27.0 0.8 copy-start.4
  27.8 0.8 copy-start.5
  30.8 35.7 %all-to-all-start = ((bf16[32,3,32,128]{3,2,1,0:T(8,128)(2,1)}), bf16[32,3,32,128]{3,2,1,0:T(8,128)(2,1)S(1)}, u32[]{:S(2)}, u32[]{:S(2)}) async-start(bf16[32,3,32,128]{3,2,1,0:T(8,128)(2,1)} %prep.1), calls=%async_computation | async-start | bytes 1572864 | tf_op jit(solution)/shard_map/all_to_all | solution.py:433
  39.4 24.0 %collective-permute-start.4 = (bf16[1024,256]{1,0:T(8,128)(2,1)S(1)}, bf16[1024,256]{1,0:T(8,128)(2,1)S(1)}, u32[]{:S(2)}, u32[]{:S(2)}) collective-permute-start(bf16[1024,256]{1,0:T(8,128)(2,1)S(1)} %copy-done.11), channel_id=1, source_target_pairs={{0,32},{16,48},{32,0},{48,16},{1,33},{17,49},{33,1},{49,17},{2,34}... | collective-permute-start | bytes 1572872 | tf_op jit(solution)/shard_map/ppermute | solution.py:427
  42.4 11.6 %collective-permute-start.8 = (bf16[3,128,512]{2,1,0:T(8,128)(2,1)S(1)}, bf16[3,128,512]{2,1,0:T(8,128)(2,1)S(1)}, u32[]{:S(2)}, u32[]{:S(2)}) collective-permute-start(bf16[3,128,512]{2,1,0:T(8,128)(2,1)S(1)} %copy-done.1), channel_id=1, source_target_pairs={{0,2},{1,3},{2,0},{3,1},{4,6},{5,7},{6,4},{7,5},{8,10},{9,11},{10,... | collective-permute-start | bytes 1179656 | tf_op jit(solution)/shard_map/ppermute | solution.py:427
  45.3 17.4 %collective-permute-start.7 = (bf16[3,128,512]{2,1,0:T(8,128)(2,1)S(1)}, bf16[3,128,512]{2,1,0:T(8,128)(2,1)S(1)}, u32[]{:S(2)}, u32[]{:S(2)}) collective-permute-start(bf16[3,128,512]{2,1,0:T(8,128)(2,1)S(1)} %copy-done.1), channel_id=1, source_target_pairs={{0,3},{1,0},{2,1},{3,2},{4,7},{5,4},{6,5},{7,6},{8,11},{9,8},{10,9... | collective-permute-start | bytes 1179656 | tf_op jit(solution)/shard_map/ppermute | solution.py:427
  46.1 17.3 %collective-permute-start.6 = (bf16[3,128,512]{2,1,0:T(8,128)(2,1)S(1)}, bf16[3,128,512]{2,1,0:T(8,128)(2,1)S(1)}, u32[]{:S(2)}, u32[]{:S(2)}) collective-permute-start(bf16[3,128,512]{2,1,0:T(8,128)(2,1)S(1)} %copy-done.1), channel_id=1, source_target_pairs={{0,1},{1,2},{2,3},{3,0},{4,5},{5,6},{6,7},{7,4},{8,9},{9,10},{10,1... | collective-permute-start | bytes 1179656 | tf_op jit(solution)/shard_map/ppermute | solution.py:427
  54.0 10.4 %copy-start.16 = (bf16[3,128,512]{2,1,0:T(8,128)(2,1)}, bf16[3,128,512]{2,1,0:T(8,128)(2,1)S(1)}, u32[]{:S(2)}) copy-start(bf16[3,128,512]{2,1,0:T(8,128)(2,1)S(1)} %collective-permute-done.8.refs_10_) | copy-start | bytes 1179652
  62.7 1.7 copy-start.17
  63.4 1.6 copy-start.18
  63.4 11.1 %copy-start.12 = (bf16[1024,256]{1,0:T(8,128)(2,1)}, bf16[1024,256]{1,0:T(8,128)(2,1)S(1)}, u32[]{:S(2)}) copy-start(bf16[1024,256]{1,0:T(8,128)(2,1)S(1)} %collective-permute-done.4.refs_2_) | copy-start | bytes 1572868
  63.4 11.0 %collective-permute-start.9 = (bf16[1024,256]{1,0:T(8,128)(2,1)S(1)}, bf16[1024,256]{1,0:T(8,128)(2,1)S(1)}, u32[]{:S(2)}, u32[]{:S(2)}) collective-permute-start(bf16[1024,256]{1,0:T(8,128)(2,1)S(1)} %copy-done.11), channel_id=1, source_target_pairs={{0,8},{8,0},{1,9},{9,1},{2,10},{10,2},{3,11},{11,3},{4,12},{12,4},... | collective-permute-start | bytes 1572872 | tf_op jit(solution)/shard_map/ppermute | solution.py:427
  64.4 10.0 %collective-permute-start.10 = (bf16[1024,256]{1,0:T(8,128)(2,1)}, bf16[1024,256]{1,0:T(8,128)(2,1)S(1)}, u32[]{:S(2)}, u32[]{:S(2)}) collective-permute-start(bf16[1024,256]{1,0:T(8,128)(2,1)} %copy-done.5), channel_id=1, source_target_pairs={{0,8},{8,0},{1,9},{9,1},{2,10},{10,2},{3,11},{11,3},{4,12},{12,4},... | collective-permute-start | bytes 1572872 | tf_op jit(solution)/shard_map/ppermute | solution.py:427
  64.5 9.9 %collective-permute-start.11 = (bf16[1024,256]{1,0:T(8,128)(2,1)S(1)}, bf16[1024,256]{1,0:T(8,128)(2,1)S(1)}, u32[]{:S(2)}, u32[]{:S(2)}) collective-permute-start(bf16[1024,256]{1,0:T(8,128)(2,1)S(1)} %collective-permute-done.4.refs_2_), channel_id=1, source_target_pairs={{0,8},{8,0},{1,9},{9,1},{2,10},{10,2},{3,11},{11,3},{4,12},{12,4},... | collective-permute-start | bytes 1572872 | tf_op jit(solution)/shard_map/ppermute | solution.py:427
  65.0 9.4 %collective-permute-start.12 = (bf16[1024,256]{1,0:T(8,128)(2,1)}, bf16[1024,256]{1,0:T(8,128)(2,1)}, u32[]{:S(2)}, u32[]{:S(2)}) collective-permute-start(bf16[1024,256]{1,0:T(8,128)(2,1)} %copy-done.4), channel_id=1, source_target_pairs={{0,8},{8,0},{1,9},{9,1},{2,10},{10,2},{3,11},{11,3},{4,12},{12,4},... | collective-permute-start | bytes 1572872 | tf_op jit(solution)/shard_map/ppermute | solution.py:427
  66.5 0.9 copy-start.2
  74.4 0.8 copy-start.13
  74.4 0.9 copy-start.14
  74.4 1.1 copy-start.15
  84.1 8.0 %copy-start.26 = (bf16[32,1024]{1,0:T(8,128)(2,1)S(1)}, bf16[32,1024]{1,0:T(8,128)(2,1)}, u32[]{:S(2)}) copy-start(bf16[32,1024]{1,0:T(8,128)(2,1)} %get-tuple-element.36) | copy-start | bytes 196612
  84.1 9.4 %copy-start.25 = (bf16[32,1024]{1,0:T(8,128)(2,1)S(1)}, bf16[32,1024]{1,0:T(8,128)(2,1)}, u32[]{:S(2)}) copy-start(bf16[32,1024]{1,0:T(8,128)(2,1)} %get-tuple-element.37) | copy-start | bytes 196612
  84.1 11.8 %copy-start.24 = (bf16[32,1024]{1,0:T(8,128)(2,1)S(1)}, bf16[32,1024]{1,0:T(8,128)(2,1)}, u32[]{:S(2)}) copy-start(bf16[32,1024]{1,0:T(8,128)(2,1)} %get-tuple-element.38) | copy-start | bytes 196612
  84.1 17.8 %copy-start.23 = (bf16[32,1024]{1,0:T(8,128)(2,1)S(1)}, bf16[32,1024]{1,0:T(8,128)(2,1)}, u32[]{:S(2)}) copy-start(bf16[32,1024]{1,0:T(8,128)(2,1)} %get-tuple-element.35) | copy-start | bytes 196612
  84.2 51.8 %all-to-all-start.1 = ((bf16[32,32,512]{2,1,0:T(8,128)(2,1)}), bf16[32,32,512]{2,1,0:T(8,128)(2,1)S(1)}, u32[]{:S(2)}, u32[]{:S(2)}) async-start(bf16[32,32,512]{2,1,0:T(8,128)(2,1)} %bitcast.17), calls=%async_computation.1 | async-start | bytes 2097152 | tf_op jit(solution)/shard_map/all_to_all | solution.py:433
  92.1 7.7 %collective-permute-start.13 = (bf16[32,1024]{1,0:T(8,128)(2,1)S(1)}, bf16[32,1024]{1,0:T(8,128)(2,1)S(1)}, u32[]{:S(2)}, u32[]{:S(2)}) collective-permute-start(bf16[32,1024]{1,0:T(8,128)(2,1)S(1)} %copy-done.26), channel_id=1, source_target_pairs={{0,16},{16,32},{32,48},{48,0},{1,17},{17,33},{33,49},{49,1},{2,18}... | collective-permute-start | bytes 196616 | tf_op jit(solution)/shard_map/ppermute | solution.py:427
  93.6 8.4 %collective-permute-start.14 = (bf16[32,1024]{1,0:T(8,128)(2,1)S(1)}, bf16[32,1024]{1,0:T(8,128)(2,1)S(1)}, u32[]{:S(2)}, u32[]{:S(2)}) collective-permute-start(bf16[32,1024]{1,0:T(8,128)(2,1)S(1)} %copy-done.25), channel_id=1, source_target_pairs={{0,32},{16,48},{32,0},{48,16},{1,33},{17,49},{33,1},{49,17},{2,34}... | collective-permute-start | bytes 196616 | tf_op jit(solution)/shard_map/ppermute | solution.py:427
  96.0 6.0 %collective-permute-start.15 = (bf16[32,1024]{1,0:T(8,128)(2,1)S(1)}, bf16[32,1024]{1,0:T(8,128)(2,1)S(1)}, u32[]{:S(2)}, u32[]{:S(2)}) collective-permute-start(bf16[32,1024]{1,0:T(8,128)(2,1)S(1)} %copy-done.24), channel_id=1, source_target_pairs={{0,48},{16,0},{32,16},{48,32},{1,49},{17,1},{33,17},{49,33},{2,50}... | collective-permute-start | bytes 196616 | tf_op jit(solution)/shard_map/ppermute | solution.py:427
  97.1 61.2 %collective-permute-start.23 = (bf16[4,4,128,256]{3,2,1,0:T(8,128)(2,1)}, bf16[4,4,128,256]{3,2,1,0:T(8,128)(2,1)S(1)}, u32[]{:S(2)}, u32[]{:S(2)}) collective-permute-start(bf16[4,4,128,256]{3,2,1,0:T(8,128)(2,1)} %get-tuple-element.45), channel_id=1, source_target_pairs={{0,8},{8,0},{1,9},{9,1},{2,10},{10,2},{3,11},{11,3},{4,12},{12,4},... | collective-permute-start | bytes 3145736 | tf_op jit(solution)/shard_map/ppermute | solution.py:427
  102.0 56.3 %copy-start.9 = (bf16[4,32,1024]{2,1,0:T(8,128)(2,1)}, bf16[4,32,1024]{2,1,0:T(8,128)(2,1)S(1)}, u32[]{:S(2)}) copy-start(bf16[4,32,1024]{2,1,0:T(8,128)(2,1)S(1)} %pad_maximum_fusion.1.refs_0_) | copy-start | bytes 786436
  102.0 27.0 %collective-permute-start.18 = (bf16[4,32,1024]{2,1,0:T(8,128)(2,1)S(1)}, bf16[4,32,1024]{2,1,0:T(8,128)(2,1)S(1)}, u32[]{:S(2)}, u32[]{:S(2)}) collective-permute-start(bf16[4,32,1024]{2,1,0:T(8,128)(2,1)S(1)} %pad_maximum_fusion.1.refs_0_), channel_id=1, source_target_pairs={{0,128},{64,192},{128,0},{192,64},{1,129},{65,193},{129,1},{193,65... | collective-permute-start | bytes 786440 | tf_op jit(solution)/shard_map/ppermute | solution.py:427
  107.8 21.3 %collective-permute-start.17 = (bf16[4,32,1024]{2,1,0:T(8,128)(2,1)S(1)}, bf16[4,32,1024]{2,1,0:T(8,128)(2,1)S(1)}, u32[]{:S(2)}, u32[]{:S(2)}) collective-permute-start(bf16[4,32,1024]{2,1,0:T(8,128)(2,1)S(1)} %pad_maximum_fusion.1.refs_0_), channel_id=1, source_target_pairs={{0,192},{64,0},{128,64},{192,128},{1,193},{65,1},{129,65},{193,129... | collective-permute-start | bytes 786440 | tf_op jit(solution)/shard_map/ppermute | solution.py:427
  107.8 28.2 %collective-permute-start.16 = (bf16[4,32,1024]{2,1,0:T(8,128)(2,1)S(1)}, bf16[4,32,1024]{2,1,0:T(8,128)(2,1)S(1)}, u32[]{:S(2)}, u32[]{:S(2)}) collective-permute-start(bf16[4,32,1024]{2,1,0:T(8,128)(2,1)S(1)} %pad_maximum_fusion.1.refs_0_), channel_id=1, source_target_pairs={{0,64},{64,128},{128,192},{192,0},{1,65},{65,129},{129,193},{193,1... | collective-permute-start | bytes 786440 | tf_op jit(solution)/shard_map/ppermute | solution.py:427
  129.0 6.9 %copy-start.6 = (bf16[4,32,1024]{2,1,0:T(8,128)(2,1)}, bf16[4,32,1024]{2,1,0:T(8,128)(2,1)S(1)}, u32[]{:S(2)}) copy-start(bf16[4,32,1024]{2,1,0:T(8,128)(2,1)S(1)} %collective-permute-done.18.refs_2_) | copy-start | bytes 786436
  129.1 6.9 %copy-start.7 = (bf16[4,32,1024]{2,1,0:T(8,128)(2,1)}, bf16[4,32,1024]{2,1,0:T(8,128)(2,1)S(1)}, u32[]{:S(2)}) copy-start(bf16[4,32,1024]{2,1,0:T(8,128)(2,1)S(1)} %collective-permute-done.17.refs_1_.refs_3_) | copy-start | bytes 786436
  135.9 0.7 copy-start.8
  135.9 1.1 copy-start
  144.3 53.9 %all-to-all-start.2 = ((bf16[32,3,32,128]{3,2,1,0:T(8,128)(2,1)}), bf16[32,3,32,128]{3,2,1,0:T(8,128)(2,1)S(1)}, u32[]{:S(2)}, u32[]{:S(2)}) async-start(bf16[32,3,32,128]{3,2,1,0:T(8,128)(2,1)} %corr.1.refs_10_), calls=%async_computation.2 | async-start | bytes 1572864 | tf_op jit(solution)/shard_map/all_to_all | solution.py:433
  155.3 1.7 collective-permute-start.19
  155.7 1.9 collective-permute-start.21
  155.9 2.0 collective-permute-start.22
  156.2 2.1 %collective-permute-start.20 = (bf16[4,32,1024]{2,1,0:T(8,128)(2,1)}, bf16[4,32,1024]{2,1,0:T(8,128)(2,1)S(1)}, u32[]{:S(2)}, u32[]{:S(2)}) collective-permute-start(bf16[4,32,1024]{2,1,0:T(8,128)(2,1)} %copy-done.8), channel_id=1, source_target_pairs={{0,8},{8,0},{1,9},{9,1},{2,10},{10,2},{3,11},{11,3},{4,12},{12,4},... | collective-permute-start | bytes 786440 | tf_op jit(solution)/shard_map/ppermute | solution.py:427
  157.1 1.3 copy-start.19
  157.6 0.8 copy-start.20
  157.9 0.7 copy-start.21
  158.3 0.7 copy-start.22
  158.3 1.1 copy-start.10
  164.5 19.3 %collective-permute-start.24 = (bf16[4,4,2,32,256]{4,3,2,1,0:T(8,128)(2,1)}, bf16[4,4,2,32,256]{4,3,2,1,0:T(8,128)(2,1)S(1)}, u32[]{:S(2)}, u32[]{:S(2)}) collective-permute-start(bf16[4,4,2,32,256]{4,3,2,1,0:T(8,128)(2,1)} %get-tuple-element.46), channel_id=1, source_target_pairs={{0,16},{16,32},{32,48},{48,0},{1,17},{17,33},{33,49},{49,1},{2,18}... | collective-permute-start | bytes 1572872 | tf_op jit(solution)/shard_map/ppermute | solution.py:427
  165.9 17.9 %collective-permute-start.25 = (bf16[4,4,2,32,256]{4,3,2,1,0:T(8,128)(2,1)}, bf16[4,4,2,32,256]{4,3,2,1,0:T(8,128)(2,1)S(1)}, u32[]{:S(2)}, u32[]{:S(2)}) collective-permute-start(bf16[4,4,2,32,256]{4,3,2,1,0:T(8,128)(2,1)} %get-tuple-element.47), channel_id=1, source_target_pairs={{0,48},{16,0},{32,16},{48,32},{1,49},{17,1},{33,17},{49,33},{2,50}... | collective-permute-start | bytes 1572872 | tf_op jit(solution)/shard_map/ppermute | solution.py:427
  167.2 28.7 %collective-permute-start.26 = (bf16[4,4,2,32,256]{4,3,2,1,0:T(8,128)(2,1)}, bf16[4,4,2,32,256]{4,3,2,1,0:T(8,128)(2,1)S(1)}, u32[]{:S(2)}, u32[]{:S(2)}) collective-permute-start(bf16[4,4,2,32,256]{4,3,2,1,0:T(8,128)(2,1)} %get-tuple-element.48), channel_id=1, source_target_pairs={{0,32},{16,48},{32,0},{48,16},{1,33},{17,49},{33,1},{49,17},{2,34}... | collective-permute-start | bytes 1572872 | tf_op jit(solution)/shard_map/ppermute | solution.py:427
  198.3 0.9 copy-start.3

commit v3 on v2

--- a/solution.py
+++ b/solution.py
@@ -113,8 +113,8 @@
     )
 
 
-def conv_kernel(place_ref, fields_ref, skip_ref, table_ref, *refs):
-    total_ref, spec_ref, *mixed_refs, hold_ref = refs[-7:]
+def conv_kernel(fields_ref, skip_ref, table_ref, *refs):
+    total_ref, spec_ref, mixed_ref = refs[-3:]
     first, twist, ahead, behind, last = unpack(table_ref)
     gated = fields_ref[:, 0].astype(f32)
     taps = fields_ref[:, 1].astype(f32)
@@ -131,13 +131,14 @@
     )
     total = conv + skip_ref[...][None] * gated
     total_ref[...] = total
-    hold_ref[...] = (total * fields_ref[:, 2].astype(f32)).astype(bf16)
-    for s, mixed_ref in enumerate(mixed_refs):
-        x = lax.rem(place_ref[1] + s, 4)
+    mixed = (total * fields_ref[:, 2].astype(f32)).astype(bf16)
+    for x in range(4):
         for core in range(2):
             for z in range(4):
                 place = (core * 4 + z) * INNER
-                mixed_ref[:, place : place + INNER] = hold_ref[z * 8 + x * 2 + core]
+                block = mixed[z * 8 + x * 2 + core]
+                for copy in range(4):
+                    mixed_ref[copy, x, :, place : place + INNER] = block
 
 
 def corr_kernel(parts_ref, fields_ref, total_ref, spec_ref, skip_ref, table_ref, *refs):
@@ -179,7 +180,7 @@
     return pl.CostEstimate(flops=flops, bytes_accessed=megabytes * 2**20, transcendentals=0)
 
 
-def conv_call(place, fields, skip_rows, table, after):
+def conv_call(fields, skip_rows, table, after):
     blocks, _, owned, inner = fields.shape
     steps = owned // GROUP
     spec_rows = KEPT * GROUP
@@ -187,7 +188,6 @@
         conv_kernel,
         grid=(steps,),
         in_specs=[
-            pl.BlockSpec(memory_space=pltpu.SMEM),
             pl.BlockSpec((blocks, 3, GROUP, inner), lambda g: (0, 0, g, 0)),
             pl.BlockSpec((GROUP, inner), lambda g: (g, 0)),
             pl.BlockSpec(table.shape, lambda g: (0, 0)),
@@ -196,18 +196,17 @@
         out_specs=[
             pl.BlockSpec((blocks, GROUP, inner), lambda g: (0, g, 0)),
             pl.BlockSpec((4, 1, spec_rows, inner), lambda g: (0, g, 0, 0)),
-        ]
-        + [pl.BlockSpec((GROUP, 8 * inner), lambda g: (g, 0))] * 4,
+            pl.BlockSpec((4, 4, GROUP, 8 * inner), lambda g: (0, 0, g, 0)),
+        ],
         out_shape=[
             jax.ShapeDtypeStruct((blocks, owned, inner), f32),
             jax.ShapeDtypeStruct((4, steps, spec_rows, inner), f32),
-        ]
-        + [jax.ShapeDtypeStruct((owned, 8 * inner), bf16)] * 4,
-        scratch_shapes=[pltpu.VMEM((blocks, GROUP, inner), bf16)],
+            jax.ShapeDtypeStruct((4, 4, owned, 8 * inner), bf16),
+        ],
         compiler_params=params(),
         cost_estimate=cost(10**9, 6),
         name="conv",
-    )(place, fields, skip_rows, table, *after)
+    )(fields, skip_rows, table, *after)
 
 
 def corr_call(parts, fields, total, spec, skip_rows, table, after):
@@ -369,16 +368,11 @@
     )(place, grad_out, *near_w, *far_w, *passed, after)
 
 
-def product_kernel(cols_ref, *refs):
-    mixed, near, far, outs = refs[:8], refs[8], refs[9], refs[11:]
-    my_z, my_core = cols_ref[4], cols_ref[5]
-    my_x = cols_ref[6]
-    xs, owned, depth = mixed[0].shape
+def product_kernel(cols_ref, mixed_near, mixed_far, near, far, _, *outs):
+    my_core = cols_ref[4]
+    owners, owned, depth = mixed_near.shape
     half = depth // 2
-    lines = [
-        jnp.concatenate([mixed[4 * n + s][...].reshape(xs * owned, depth) for s in range(4)], 0)
-        for n in range(2)
-    ]
+    lines = [item[...].reshape(owners * owned, depth) for item in (mixed_near, mixed_far)]
     for n, out in enumerate(outs):
         col = cols_ref[n]
         own = near[col].reshape(half, near.shape[3])
@@ -387,28 +381,23 @@
             [jnp.where(my_core == 0, own, other), jnp.where(my_core == 0, other, own)], 0
         )
         for core, rows in zip((my_core, 1 - my_core), lines):
-            product = dot(rows, columns).astype(out.dtype).reshape(4, xs, owned, near.shape[3])
-            for s in range(4):
-                for t in range(4):
-                    z, x = lax.rem(my_z - s + 4, 4), lax.rem(my_x - t + 4, 4)
-                    out[z, x, core] = product[s, t]
-
-
-def product_call(cols, mixed, near, far, after, kinds):
-    xs, owned, depth = mixed[0].shape
+            product = dot(rows, columns).astype(out.dtype)
+            out[:, core] = product.reshape(owners, owned, product.shape[1])
+
+
+def product_call(cols, mixed_near, mixed_far, near, far, after, kinds):
+    owners, owned, depth = mixed_near.shape
     width = near.shape[3]
     vmem = pl.BlockSpec(memory_space=pltpu.VMEM)
     return pl.pallas_call(
         product_kernel,
-        in_specs=[pl.BlockSpec(memory_space=pltpu.SMEM)]
-        + [vmem] * 10
-        + [pl.BlockSpec(memory_space=pl.ANY)],
+        in_specs=[pl.BlockSpec(memory_space=pltpu.SMEM)] + [vmem] * 4 + [pl.BlockSpec(memory_space=pl.ANY)],
         out_specs=[vmem] * len(kinds),
-        out_shape=[jax.ShapeDtypeStruct((4, xs, 2, owned, width), kind) for kind in kinds],
-        compiler_params=params(),
-        cost_estimate=cost(16 * xs * owned * width * depth * len(kinds), 5),
+        out_shape=[jax.ShapeDtypeStruct((owners, 2, owned, width), kind) for kind in kinds],
+        compiler_params=params(),
+        cost_estimate=cost(4 * owners * owned * width * depth * len(kinds), 5),
         name="product",
-    )(cols, *mixed, near, far, after)
+    )(cols, mixed_near, mixed_far, near, far, after)
 
 
 def shards(grad_out, out_weight, query_proj, key_proj, value_proj, filter_taps, skip_gain):
@@ -443,38 +432,39 @@
     near_w[2] = shift(late_w, "x", 2)
     for s in order:
         passed[s] = shift(passed[0], "y", s)
-    held = lax.optimization_barrier((*near_w.values(), *passed.values()))
-    far_w = {s: swap(item) for s, item in zip(near_w, held)}
-    far_w = [far_w[s] for s in range(4)]
-
-    fields = prep_call(key_proj, value_proj, filter_taps, query_proj, owned, [near_w[1], near_w[3], passed[0]])
-    fields = to_all(fields)
-
     place = jnp.stack([my_z, my_x, my_core, my_y]).astype(jnp.int32)
     skip_rows = lax.dynamic_slice_in_dim(
         skip_gain, lax.axis_index(CTX) * owned, owned, 0
     )
     skip_rows = jnp.broadcast_to(skip_rows[:, None], (owned, tok_rows))
-    total, spec, *mixed = conv_call(place, fields, skip_rows, table, [])
-    mixed = jnp.stack(mixed[:1] + [shift(mixed[s], "x", s) for s in range(1, 4)])
-
+
+    fields = prep_call(key_proj, value_proj, filter_taps, query_proj, owned, [near_w[1], near_w[3], passed[0], skip_rows, place])
+    fields = to_all(fields)
+
+    total, spec, mixed = conv_call(
+        fields, skip_rows, table, [near_w[2]] + [passed[s] for s in order]
+    )
+    mixed = lax.all_to_all(
+        mixed.reshape(16, owned, 8 * tok_rows), ("zh", "x"), split_axis=0, concat_axis=0, tiled=True
+    )
+
+    held = lax.optimization_barrier((*near_w.values(), *passed.values(), total))
+    far_w = {s: swap(item) for s, item in zip(near_w, held)}
+    far_w = [far_w[s] for s in range(4)]
     parts, near, far = mix_call(
         place, grad_out, [near_w[s] for s in range(4)], far_w, [passed[s] for s in range(4)], total
     )
-    mixed = lax.optimization_barrier((mixed, parts))[0]
     far = swap(far)
     parts = to_all(parts.reshape(context_size, owned, 4 * tok_rows))
-
-    mixed = [mixed] + [shift(mixed, "zh", s) for s in range(1, 4)]
-    corr = corr_call(parts, fields, total, spec, skip_rows, table, [mixed[s] for s in order])
-    mixed += [swap(item) for item in mixed]
+    mixed_far = swap(mixed)
 
     cols = [(my_x + s) % 4 for s in (2, 1, 3, 0)]
-    near_cols = jnp.stack(cols + [my_z, my_core, my_x]).astype(jnp.int32)
-    last_cols = jnp.stack(cols[3:] * 4 + [my_z, my_core, my_x]).astype(jnp.int32)
-    sent = product_call(near_cols, mixed, near, far, corr, (bf16,) * 3)
+    near_cols = jnp.stack(cols + [my_core]).astype(jnp.int32)
+    last_cols = jnp.stack(cols[3:] * 4 + [my_core]).astype(jnp.int32)
+    sent = product_call(near_cols, mixed, mixed_far, near, far, total, (bf16,) * 3)
     sent = {s: shift(item, "x", s) for s, item in zip((2, 1, 3), sent)}
-    grad_weight = product_call(last_cols, mixed, near, far, corr, (f32,))[0]
+    corr = corr_call(parts, fields, total, spec, skip_rows, table, [sent[1], sent[3]])
+    grad_weight = product_call(last_cols, mixed, mixed_far, near, far, corr, (f32,))[0]
     corr = to_all(corr)
     grad_key, grad_value, grad_filter, grad_query = last_call(corr, key_proj, value_proj)
     for s in (1, 3, 2):

time: 202 us -> 192 us (0.950)
  starting transfers between devices: 70.3 us -> 58.5 us
    ppermute x27 -> x18, waiting for transfers between devices: 80.3 us -> 51.9 us  [shift(): return lax.ppermute(item, axis, [(n, (n + by) % size) for n in range(size)])]
    all_to_all x3, waiting for transfers between devices: 0.01 us -> 16.3 us  [to_all(): return lax.all_to_all(item, CTX, split_axis=0, concat_axis=0, tiled=True)]
    all_to_all x0 -> x1, waiting for transfers between devices: none -> 13.8 us  [shards(): lax.all_to_all(mixed.reshape(16, owned, 8 * tok_rows), ('zh', 'x'), split...]
    ppermute x27 -> x18, starting transfers between devices: 42.8 us -> 30.2 us  [shift(): return lax.ppermute(item, axis, [(n, (n + by) % size) for n in range(size)])]
    all_to_all x0 -> x1, starting transfers between devices: none -> 7.22 us  [shards(): lax.all_to_all(mixed.reshape(16, owned, 8 * tok_rows), ('zh', 'x'), split...]
    all_to_all x3, starting transfers between devices: 27.5 us -> 21 us  [to_all(): return lax.all_to_all(item, CTX, split_axis=0, concat_axis=0, tiled=True)]
    unnamed x54 -> x48, local copies, waits for them, and re-layouts: 5.96 us -> 5.39 us
  transfers between devices with their start and end apart: 30 -> 22, of which waited for: 14 -> 14; matrix products, arithmetic and copies ran while one was open for 4% -> 4% of each run, Pallas kernels for 12% -> 9%
where the time goes in v3:
time: 192 us; the launch traced here: 191 us
  waiting for transfers between devices  82.1 us (43%)
  starting transfers between devices  58.5 us (30%)
  Pallas kernels  36.5 us (19%)
  local copies, waits for them, and re-layouts  9.17 us (5%)
  other arithmetic  3.77 us (2%)
    ppermute x18, waiting for transfers between devices, shift(): return lax.ppermute(item, axis, [(n, (n + by) % size) for n in range(size)])  51.9 us
    ppermute x18, starting transfers between devices, shift(): return lax.ppermute(item, axis, [(n, (n + by) % size) for n in range(size)])  30.2 us
    all_to_all x3, starting transfers between devices, to_all(): return lax.all_to_all(item, CTX, split_axis=0, concat_axis=0, tiled=True)  21 us
    all_to_all x3, waiting for transfers between devices, to_all(): return lax.all_to_all(item, CTX, split_axis=0, concat_axis=0, tiled=True)  16.3 us
    all_to_all x1, waiting for transfers between devices, shards(): lax.all_to_all(mixed.reshape(16, owned, 8 * tok_rows), ('zh', 'x'), split...  13.8 us
    pallas_call x2, Pallas kernels, product_call(): pl.pallas_call(product_kernel, in_specs=[pl.BlockSpec(memory_space=pltpu....  8.86 us
    pallas_call x1, Pallas kernels, mix_call(): pl.pallas_call(mix_kernel, in_specs=[pl.BlockSpec(memory_space=pltpu.SMEM...  8.56 us
    pallas_call x1, Pallas kernels, corr_call(): pl.pallas_call(corr_kernel, grid=(steps,), in_specs=[pl.BlockSpec((blocks...  7.42 us
  transfers between devices with their start and end apart: 22, of which 14 were waited for; matrix products, arithmetic and copies ran while one was open for 4% of the time, Pallas kernels for 9%

profile of v3, /device:TPU:1, one launch (start us, length us, event | category | flops | bytes accessed | tf_op | source)
XLA Modules:
  0.0 190.8 jit_solution(11828108482233411103)
XLA Ops:
  0.6 3.4 %collective-permute-start.5 = (bf16[1024,256]{1,0:T(8,128)(2,1)}, bf16[1024,256]{1,0:T(8,128)(2,1)S(1)}, u32[]{:S(2)}, u32[]{:S(2)}) collective-permute-start(bf16[1024,256]{1,0:T(8,128)(2,1)} %refs_0_.1), channel_id=1, source_target_pairs={{0,48},{16,0},{32,16},{48,32},{1,49},{17,1},{33,17},{49,33},{2,50}... | collective-permute-start | bytes 1572872 | tf_op jit(solution)/shard_map/ppermute | solution.py:416
  4.0 1.1 constant_dynamic-slice_fusion.2
  5.1 3.1 %collective-permute-start.1 = (bf16[128,512]{1,0:T(8,128)(2,1)S(1)}, bf16[128,512]{1,0:T(8,128)(2,1)S(1)}, u32[]{:S(2)}, u32[]{:S(2)}) collective-permute-start(bf16[128,512]{1,0:T(8,128)(2,1)S(1)} %get-tuple-element.41), channel_id=1, source_target_pairs={{0,64},{64,128},{128,192},{192,0},{1,65},{65,129},{129,193},{193,1... | collective-permute-start | bytes 393224 | tf_op jit(solution)/shard_map/ppermute | solution.py:416
  8.1 5.1 %collective-permute-start.2 = (bf16[128,512]{1,0:T(8,128)(2,1)S(1)}, bf16[128,512]{1,0:T(8,128)(2,1)S(1)}, u32[]{:S(2)}, u32[]{:S(2)}) collective-permute-start(bf16[128,512]{1,0:T(8,128)(2,1)S(1)} %get-tuple-element.42), channel_id=1, source_target_pairs={{0,128},{64,192},{128,0},{192,64},{1,129},{65,193},{129,1},{193,65... | collective-permute-start | bytes 393224 | tf_op jit(solution)/shard_map/ppermute | solution.py:416
  13.3 2.4 %collective-permute-start.3 = (bf16[128,512]{1,0:T(8,128)(2,1)S(1)}, bf16[128,512]{1,0:T(8,128)(2,1)S(1)}, u32[]{:S(2)}, u32[]{:S(2)}) collective-permute-start(bf16[128,512]{1,0:T(8,128)(2,1)S(1)} %get-tuple-element.43), channel_id=1, source_target_pairs={{0,192},{64,0},{128,64},{192,128},{1,193},{65,1},{129,65},{193,129... | collective-permute-start | bytes 393224 | tf_op jit(solution)/shard_map/ppermute | solution.py:416
  15.6 0.8 dynamic_slice.15
  16.4 0.6 pad_add_fusion.refs_4_.place_ref
  17.0 0.0 collective-permute-done.1
  17.0 4.3 %collective-permute-done.2 = bf16[128,512]{1,0:T(8,128)(2,1)S(1)} collective-permute-done((bf16[128,512]{1,0:T(8,128)(2,1)S(1)}, bf16[128,512]{1,0:T(8,128)(2,1)S(1)}, u32[]{:S(2)}, u32[]{:S(2)}) %collective-permute-start.2) | collective-permute-done | bytes 131104 | tf_op jit(solution)/shard_map/ppermute | solution.py:416
  21.3 4.9 %collective-permute-done.3 = bf16[128,512]{1,0:T(8,128)(2,1)S(1)} collective-permute-done((bf16[128,512]{1,0:T(8,128)(2,1)S(1)}, bf16[128,512]{1,0:T(8,128)(2,1)S(1)}, u32[]{:S(2)}, u32[]{:S(2)}) %collective-permute-start.3) | collective-permute-done | bytes 131104 | tf_op jit(solution)/shard_map/ppermute | solution.py:416
  26.2 0.8 pad_maximum_fusion.refs_2_.refs_8_
  27.0 0.0 collective-permute-done.refs_0_.refs_1_
  27.0 0.0 copy-start.7
  27.0 0.8 broadcast_in_dim.2.refs_3_.skip_ref
  27.8 0.1 copy-done.7
  28.0 2.4 %prep.1 = bf16[32,3,32,128]{3,2,1,0:T(8,128)(2,1)} custom-call(bf16[128,1024]{1,0:T(8,128)(2,1)} %key_ref.3, bf16[128,1024]{1,0:T(8,128)(2,1)} %value_ref.3, bf16[128,1024]{1,0:T(8,128)(2,1)} %taps_ref.1, bf16[128,1024]{1,0:T(8,128)(2,1)} %query_ref.1, bf16[1024,256]{1,0:T(8,128)(2,1)} %copy-done.7, bf16[1024,256]{1,0:T(8,128)(2,1)} %copy-done.5, ...), custom_call_target="tpu_custom_call" | custom-call | flops 10000000 | bytes 2097152 | tf_op jit(solution)/shard_map/prep/pallas_call | solution.py:249
  30.3 8.6 %all-to-all-start = ((bf16[32,3,32,128]{3,2,1,0:T(8,128)(2,1)}), bf16[32,3,32,128]{3,2,1,0:T(8,128)(2,1)S(1)}, u32[]{:S(2)}, u32[]{:S(2)}) async-start(bf16[32,3,32,128]{3,2,1,0:T(8,128)(2,1)} %prep.1), calls=%async_computation | async-start | bytes 1572864 | tf_op jit(solution)/shard_map/all_to_all | solution.py:422
  38.9 0.0 copy-start.8
  38.9 3.0 %collective-permute-start.4 = (bf16[1024,256]{1,0:T(8,128)(2,1)S(1)}, bf16[1024,256]{1,0:T(8,128)(2,1)S(1)}, u32[]{:S(2)}, u32[]{:S(2)}) collective-permute-start(bf16[1024,256]{1,0:T(8,128)(2,1)S(1)} %copy-done.14), channel_id=1, source_target_pairs={{0,32},{16,48},{32,0},{48,16},{1,33},{17,49},{33,1},{49,17},{2,34}... | collective-permute-start | bytes 1572872 | tf_op jit(solution)/shard_map/ppermute | solution.py:416
  41.9 2.9 %collective-permute-start.8 = (bf16[3,128,512]{2,1,0:T(8,128)(2,1)S(1)}, bf16[3,128,512]{2,1,0:T(8,128)(2,1)S(1)}, u32[]{:S(2)}, u32[]{:S(2)}) collective-permute-start(bf16[3,128,512]{2,1,0:T(8,128)(2,1)S(1)} %copy-done.2), channel_id=1, source_target_pairs={{0,2},{1,3},{2,0},{3,1},{4,6},{5,7},{6,4},{7,5},{8,10},{9,11},{10,... | collective-permute-start | bytes 1179656 | tf_op jit(solution)/shard_map/ppermute | solution.py:416
  44.8 0.8 collective-permute-start.7
  45.6 0.7 collective-permute-start.6
  46.3 7.2 %collective-permute-done.8.refs_3_.refs_10_ = bf16[3,128,512]{2,1,0:T(8,128)(2,1)S(1)} collective-permute-done((bf16[3,128,512]{2,1,0:T(8,128)(2,1)S(1)}, bf16[3,128,512]{2,1,0:T(8,128)(2,1)S(1)}, u32[]{:S(2)}, u32[]{:S(2)}) %collective-permute-start.8) | collective-permute-done | bytes 393248 | tf_op jit(solution)/shard_map/ppermute | solution.py:416
  53.5 8.8 %collective-permute-done.7.refs_2_.refs_11_ = bf16[3,128,512]{2,1,0:T(8,128)(2,1)S(1)} collective-permute-done((bf16[3,128,512]{2,1,0:T(8,128)(2,1)S(1)}, bf16[3,128,512]{2,1,0:T(8,128)(2,1)S(1)}, u32[]{:S(2)}, u32[]{:S(2)}) %collective-permute-start.7) | collective-permute-done | bytes 393248 | tf_op jit(solution)/shard_map/ppermute | solution.py:416
  62.3 0.6 collective-permute-done.6.refs_1_.refs_9_
  62.9 0.1 copy-done.21
  63.0 0.7 copy-done.22
  63.8 0.8 copy-done.15
  64.6 0.9 copy-done.3
  65.4 7.1 %conv.1 = (f32[32,32,128]{2,1,0:T(8,128)}, f32[4,2,528,128]{3,2,1,0:T(8,128)}, bf16[4,4,32,1024]{3,2,1,0:T(8,128)(2,1)}) custom-call(bf16[32,3,32,128]{3,2,1,0:T(8,128)(2,1)} %copy-done.3, f32[32,128]{1,0:T(8,128)} %broadcast_in_dim.2.refs_3_.skip_ref, f32[592,128]{1,0:T(8,128)} %constant.74.clone.table_ref, bf16[1024,256]{1,0:T(8,128)(2,1)} %copy-done.15, ...), custom_call_target="tpu_custom_call" | custom-call | flops 1000000000 | bytes 6291456 | tf_op jit(solution)/shard_map/conv/pallas_call | solution.py:187
  72.6 7.2 %all-to-all-start.2 = ((bf16[16,32,1024]{2,1,0:T(8,128)(2,1)}), bf16[16,32,1024]{2,1,0:T(8,128)(2,1)S(1)}, u32[]{:S(2)}, u32[]{:S(2)}) async-start(bf16[16,32,1024]{2,1,0:T(8,128)(2,1)} %bitcast.15), calls=%async_computation.2 | async-start | bytes 2097152 | tf_op jit(solution)/shard_map/all_to_all | solution.py:447
  79.8 1.9 collective-permute-start.9
  81.7 0.1 collective-permute-start.10
  81.8 0.4 collective-permute-start.11
  82.2 0.3 collective-permute-start.12
  82.4 0.7 collective-permute-done.9.refs_4_
  83.2 0.7 collective-permute-done.10.refs_5_
  83.9 1.5 collective-permute-done.11.refs_6_
  85.4 0.8 copy-done.19
  86.3 0.0 collective-permute-done.12.refs_7_
  86.3 8.6 %mix.1 = (bf16[1024,512]{1,0:T(8,128)(2,1)}, bf16[4,4,128,256]{3,2,1,0:T(8,128)(2,1)}, bf16[4,4,128,256]{3,2,1,0:T(8,128)(2,1)}) custom-call(s32[4]{0:T(128)} %pad_add_fusion.refs_4_.place_ref, bf16[128,8192]{1,0:T(8,128)(2,1)} %grad_out_ref.1, bf16[1024,256]{1,0:T(8,128)(2,1)} %refs_0_.1, bf16[1024,256]{1,0:T(8,128)(2,1)} %copy-done.7, ...), custom_call_target="tpu_custom_call" | custom-call | flops 2147483648 | bytes 9437184 | tf_op jit(solution)/shard_map/mix/pallas_call | solution.py:354
  94.8 13.8 %all-to-all-done.2.mixed_near = bf16[16,32,1024]{2,1,0:T(8,128)(2,1)S(1)} async-done(((bf16[16,32,1024]{2,1,0:T(8,128)(2,1)}), bf16[16,32,1024]{2,1,0:T(8,128)(2,1)S(1)}, u32[]{:S(2)}, u32[]{:S(2)}) %all-to-all-start.2) | async-done | bytes 1048608 | tf_op jit(solution)/shard_map/all_to_all | solution.py:447
  108.7 4.8 %all-to-all-start.1 = ((bf16[32,32,512]{2,1,0:T(8,128)(2,1)}), bf16[32,32,512]{2,1,0:T(8,128)(2,1)S(1)}, u32[]{:S(2)}, u32[]{:S(2)}) async-start(bf16[32,32,512]{2,1,0:T(8,128)(2,1)} %bitcast.14), calls=%async_computation.1 | async-start | bytes 2097152 | tf_op jit(solution)/shard_map/all_to_all | solution.py:422
  113.5 0.3 collective-permute-start.14
  113.9 0.3 collective-permute-start.13
  114.1 0.6 stack.64.cols_ref
  114.7 1.8 collective-permute-done.14.far
  116.5 1.4 collective-permute-done.13.mixed_far
  117.9 4.8 %product.2 = (bf16[16,2,32,256]{3,2,1,0:T(8,128)(2,1)}, bf16[16,2,32,256]{3,2,1,0:T(8,128)(2,1)}, bf16[16,2,32,256]{3,2,1,0:T(8,128)(2,1)}) custom-call(s32[5]{0:T(128)} %stack.64.cols_ref, bf16[16,32,1024]{2,1,0:T(8,128)(2,1)} %copy-done.1, bf16[16,32,1024]{2,1,0:T(8,128)(2,1)} %collective-permute-done.13.mixed_far, ...), custom_call_target="tpu_custom_call" | custom-call | flops 1610612736 | bytes 5242880 | tf_op jit(solution)/shard_map/product/pallas_call | solution.py:392
  122.8 1.4 collective-permute-start.15
  124.1 1.3 collective-permute-start.16
  125.4 16.3 %all-to-all-done.1.parts_ref = bf16[32,32,512]{2,1,0:T(8,128)(2,1)S(1)} async-done(((bf16[32,32,512]{2,1,0:T(8,128)(2,1)}), bf16[32,32,512]{2,1,0:T(8,128)(2,1)S(1)}, u32[]{:S(2)}, u32[]{:S(2)}) %all-to-all-start.1) | async-done | bytes 1048608 | tf_op jit(solution)/shard_map/all_to_all | solution.py:422
  141.7 3.8 %collective-permute-done.15.refs_0_ = bf16[16,2,32,256]{3,2,1,0:T(8,128)(2,1)S(1)} collective-permute-done((bf16[16,2,32,256]{3,2,1,0:T(8,128)(2,1)}, bf16[16,2,32,256]{3,2,1,0:T(8,128)(2,1)S(1)}, u32[]{:S(2)}, u32[]{:S(2)}) %collective-permute-start.15) | collective-permute-done | bytes 524320 | tf_op jit(solution)/shard_map/ppermute | solution.py:416
  145.5 0.8 copy-done.9
  146.3 0.1 copy-done.11
  146.4 7.4 %corr.1._ = bf16[32,3,32,128]{3,2,1,0:T(8,128)(2,1)} custom-call(bf16[32,32,512]{2,1,0:T(8,128)(2,1)} %copy-done, bf16[32,3,32,128]{3,2,1,0:T(8,128)(2,1)} %copy-done.3, f32[32,32,128]{2,1,0:T(8,128)} %get-tuple-element.24.refs_12_._.total_ref, f32[4,2,528,128]{3,2,1,0:T(8,128)} %get-tuple-element.30.spec_ref, f32[32,128]{1,0:T(8,128)} %broadcast_in_dim.2.refs_3_.skip_ref, ...), custom_call_target="tpu_custom_call" | custom-call | flops 1000000000 | bytes 6291456 | tf_op jit(solution)/shard_map/corr/pallas_call | solution.py:216
  153.9 7.6 %all-to-all-start.3 = ((bf16[32,3,32,128]{3,2,1,0:T(8,128)(2,1)}), bf16[32,3,32,128]{3,2,1,0:T(8,128)(2,1)S(1)}, u32[]{:S(2)}, u32[]{:S(2)}) async-start(bf16[32,3,32,128]{3,2,1,0:T(8,128)(2,1)} %corr.1._), calls=%async_computation.3 | async-start | bytes 1572864 | tf_op jit(solution)/shard_map/all_to_all | solution.py:422
  161.5 3.0 %collective-permute-start.17 = (bf16[16,2,32,256]{3,2,1,0:T(8,128)(2,1)S(1)}, bf16[16,2,32,256]{3,2,1,0:T(8,128)(2,1)S(1)}, u32[]{:S(2)}, u32[]{:S(2)}) collective-permute-start(bf16[16,2,32,256]{3,2,1,0:T(8,128)(2,1)S(1)} %copy-done.23), channel_id=1, source_target_pairs={{0,32},{16,48},{32,0},{48,16},{1,33},{17,49},{33,1},{49,17},{2,34}... | collective-permute-start | bytes 1572872 | tf_op jit(solution)/shard_map/ppermute | solution.py:416
  164.5 0.6 stack.65.cols_ref
  165.1 4.0 %product.3 = f32[16,2,32,256]{3,2,1,0:T(8,128)} custom-call(s32[5]{0:T(128)} %stack.65.cols_ref, bf16[16,32,1024]{2,1,0:T(8,128)(2,1)} %copy-done.1, bf16[16,32,1024]{2,1,0:T(8,128)(2,1)} %collective-permute-done.13.mixed_far, bf16[4,4,128,256]{3,2,1,0:T(8,128)(2,1)} %get-tuple-element.32.near, bf16[4,4,128,256]{3,2,1,0:T(8,128)(2,1)} %copy-done.13, ...), custom_call_target="tpu_custom_call" | custom-call | flops 536870912 | bytes 5242880 | tf_op jit(solution)/shard_map/product/pallas_call | solution.py:392
  169.1 16.2 %collective-permute-done.17 = bf16[16,2,32,256]{3,2,1,0:T(8,128)(2,1)S(1)} collective-permute-done((bf16[16,2,32,256]{3,2,1,0:T(8,128)(2,1)S(1)}, bf16[16,2,32,256]{3,2,1,0:T(8,128)(2,1)S(1)}, u32[]{:S(2)}, u32[]{:S(2)}) %collective-permute-start.17) | collective-permute-done | bytes 524320 | tf_op jit(solution)/shard_map/ppermute | solution.py:416
  185.3 2.4 %multiply_convert_fusion = bf16[16,2,32,256]{3,2,1,0:T(8,128)(2,1)} fusion(bf16[16,2,32,256]{3,2,1,0:T(8,128)(2,1)S(1)} %collective-permute-done.17, bf16[16,2,32,256]{3,2,1,0:T(8,128)(2,1)S(1)} %copy-done.12, f32[16,2,32,256]{3,2,1,0:T(8,128)} %product.3, bf16[16,2,32,256]{3,2,1,0:T(8,128)(2,1)S(1)} %copy-done.10), kind=kLoop, calls=%fused_computation | loop fusion | flops 2097152 | bytes 3145728 | tf_op jit(solution)/shard_map/convert_element_type | solution.py:472
  187.7 0.9 copy-done.4
  188.6 2.2 %last.1 = (bf16[128,1024]{1,0:T(8,128)(2,1)}, bf16[128,1024]{1,0:T(8,128)(2,1)}, bf16[128,1024]{1,0:T(8,128)(2,1)}, bf16[128,1024]{1,0:T(8,128)(2,1)}) custom-call(bf16[32,3,32,128]{3,2,1,0:T(8,128)(2,1)} %copy-done.4, bf16[128,1024]{1,0:T(8,128)(2,1)} %key_ref.3, bf16[128,1024]{1,0:T(8,128)(2,1)} %value_ref.3), custom_call_target="tpu_custom_call" | custom-call | flops 10000000 | bytes 3145728 | tf_op jit(solution)/shard_map/last/pallas_call | solution.py:279
  (43 shorter events, 0.1 us)
Async XLA Ops:
  0.6 26.4 %collective-permute-start.5 = (bf16[1024,256]{1,0:T(8,128)(2,1)}, bf16[1024,256]{1,0:T(8,128)(2,1)S(1)}, u32[]{:S(2)}, u32[]{:S(2)}) collective-permute-start(bf16[1024,256]{1,0:T(8,128)(2,1)} %refs_0_.1), channel_id=1, source_target_pairs={{0,48},{16,0},{32,16},{48,32},{1,49},{17,1},{33,17},{49,33},{2,50}... | collective-permute-start | bytes 1572872 | tf_op jit(solution)/shard_map/ppermute | solution.py:416
  4.0 23.0 %collective-permute-start = (bf16[1024,256]{1,0:T(8,128)(2,1)}, bf16[1024,256]{1,0:T(8,128)(2,1)S(1)}, u32[]{:S(2)}, u32[]{:S(2)}) collective-permute-start(bf16[1024,256]{1,0:T(8,128)(2,1)} %refs_0_.1), channel_id=1, source_target_pairs={{0,16},{16,32},{32,48},{48,0},{1,17},{17,33},{33,49},{49,1},{2,18}... | collective-permute-start | bytes 1572872 | tf_op jit(solution)/shard_map/ppermute | solution.py:416
  5.1 11.9 %collective-permute-start.1 = (bf16[128,512]{1,0:T(8,128)(2,1)S(1)}, bf16[128,512]{1,0:T(8,128)(2,1)S(1)}, u32[]{:S(2)}, u32[]{:S(2)}) collective-permute-start(bf16[128,512]{1,0:T(8,128)(2,1)S(1)} %get-tuple-element.41), channel_id=1, source_target_pairs={{0,64},{64,128},{128,192},{192,0},{1,65},{65,129},{129,193},{193,1... | collective-permute-start | bytes 393224 | tf_op jit(solution)/shard_map/ppermute | solution.py:416
  8.1 13.1 %collective-permute-start.2 = (bf16[128,512]{1,0:T(8,128)(2,1)S(1)}, bf16[128,512]{1,0:T(8,128)(2,1)S(1)}, u32[]{:S(2)}, u32[]{:S(2)}) collective-permute-start(bf16[128,512]{1,0:T(8,128)(2,1)S(1)} %get-tuple-element.42), channel_id=1, source_target_pairs={{0,128},{64,192},{128,0},{192,64},{1,129},{65,193},{129,1},{193,65... | collective-permute-start | bytes 393224 | tf_op jit(solution)/shard_map/ppermute | solution.py:416
  13.3 12.9 %collective-permute-start.3 = (bf16[128,512]{1,0:T(8,128)(2,1)S(1)}, bf16[128,512]{1,0:T(8,128)(2,1)S(1)}, u32[]{:S(2)}, u32[]{:S(2)}) collective-permute-start(bf16[128,512]{1,0:T(8,128)(2,1)S(1)} %get-tuple-element.43), channel_id=1, source_target_pairs={{0,192},{64,0},{128,64},{192,128},{1,193},{65,1},{129,65},{193,129... | collective-permute-start | bytes 393224 | tf_op jit(solution)/shard_map/ppermute | solution.py:416
  27.0 0.8 copy-start.5
  27.0 1.0 copy-start.7
  28.0 10.9 %copy-start.14 = (bf16[1024,256]{1,0:T(8,128)(2,1)S(1)}, bf16[1024,256]{1,0:T(8,128)(2,1)}, u32[]{:S(2)}) copy-start(bf16[1024,256]{1,0:T(8,128)(2,1)} %refs_0_.1) | copy-start | bytes 1572868
  28.0 13.9 %copy-start.2 = (bf16[3,128,512]{2,1,0:T(8,128)(2,1)S(1)}, bf16[3,128,512]{2,1,0:T(8,128)(2,1)}, u32[]{:S(2)}) copy-start(bf16[3,128,512]{2,1,0:T(8,128)(2,1)} %pad_maximum_fusion.refs_2_.refs_8_) | copy-start | bytes 1179652
  30.3 33.4 %all-to-all-start = ((bf16[32,3,32,128]{3,2,1,0:T(8,128)(2,1)}), bf16[32,3,32,128]{3,2,1,0:T(8,128)(2,1)S(1)}, u32[]{:S(2)}, u32[]{:S(2)}) async-start(bf16[32,3,32,128]{3,2,1,0:T(8,128)(2,1)} %prep.1), calls=%async_computation | async-start | bytes 1572864 | tf_op jit(solution)/shard_map/all_to_all | solution.py:422
  38.9 42.7 %copy-start.8 = (bf16[1024,256]{1,0:T(8,128)(2,1)S(1)}, bf16[1024,256]{1,0:T(8,128)(2,1)}, u32[]{:S(2)}) copy-start(bf16[1024,256]{1,0:T(8,128)(2,1)} %copy-done.7) | copy-start | bytes 1572868
  38.9 43.2 %copy-start.6 = (bf16[1024,256]{1,0:T(8,128)(2,1)S(1)}, bf16[1024,256]{1,0:T(8,128)(2,1)}, u32[]{:S(2)}) copy-start(bf16[1024,256]{1,0:T(8,128)(2,1)} %copy-done.5) | copy-start | bytes 1572868
  38.9 24.8 %collective-permute-start.4 = (bf16[1024,256]{1,0:T(8,128)(2,1)S(1)}, bf16[1024,256]{1,0:T(8,128)(2,1)S(1)}, u32[]{:S(2)}, u32[]{:S(2)}) collective-permute-start(bf16[1024,256]{1,0:T(8,128)(2,1)S(1)} %copy-done.14), channel_id=1, source_target_pairs={{0,32},{16,48},{32,0},{48,16},{1,33},{17,49},{33,1},{49,17},{2,34}... | collective-permute-start | bytes 1572872 | tf_op jit(solution)/shard_map/ppermute | solution.py:416
  41.9 11.6 %collective-permute-start.8 = (bf16[3,128,512]{2,1,0:T(8,128)(2,1)S(1)}, bf16[3,128,512]{2,1,0:T(8,128)(2,1)S(1)}, u32[]{:S(2)}, u32[]{:S(2)}) collective-permute-start(bf16[3,128,512]{2,1,0:T(8,128)(2,1)S(1)} %copy-done.2), channel_id=1, source_target_pairs={{0,2},{1,3},{2,0},{3,1},{4,6},{5,7},{6,4},{7,5},{8,10},{9,11},{10,... | collective-permute-start | bytes 1179656 | tf_op jit(solution)/shard_map/ppermute | solution.py:416
  44.8 17.4 %collective-permute-start.7 = (bf16[3,128,512]{2,1,0:T(8,128)(2,1)S(1)}, bf16[3,128,512]{2,1,0:T(8,128)(2,1)S(1)}, u32[]{:S(2)}, u32[]{:S(2)}) collective-permute-start(bf16[3,128,512]{2,1,0:T(8,128)(2,1)S(1)} %copy-done.2), channel_id=1, source_target_pairs={{0,3},{1,0},{2,1},{3,2},{4,7},{5,4},{6,5},{7,6},{8,11},{9,8},{10,9... | collective-permute-start | bytes 1179656 | tf_op jit(solution)/shard_map/ppermute | solution.py:416
  45.6 17.3 %collective-permute-start.6 = (bf16[3,128,512]{2,1,0:T(8,128)(2,1)S(1)}, bf16[3,128,512]{2,1,0:T(8,128)(2,1)S(1)}, u32[]{:S(2)}, u32[]{:S(2)}) collective-permute-start(bf16[3,128,512]{2,1,0:T(8,128)(2,1)S(1)} %copy-done.2), channel_id=1, source_target_pairs={{0,1},{1,2},{2,3},{3,0},{4,5},{5,6},{6,7},{7,4},{8,9},{9,10},{10,1... | collective-permute-start | bytes 1179656 | tf_op jit(solution)/shard_map/ppermute | solution.py:416
  53.5 9.4 %copy-start.20 = (bf16[3,128,512]{2,1,0:T(8,128)(2,1)}, bf16[3,128,512]{2,1,0:T(8,128)(2,1)S(1)}, u32[]{:S(2)}) copy-start(bf16[3,128,512]{2,1,0:T(8,128)(2,1)S(1)} %collective-permute-done.8.refs_3_.refs_10_) | copy-start | bytes 1179652
  62.3 0.8 copy-start.21
  63.0 0.7 copy-start.22
  63.8 0.8 copy-start.15
  64.6 0.9 copy-start.3
  72.6 9.2 %copy-start.16 = (bf16[1024,256]{1,0:T(8,128)(2,1)S(1)}, bf16[1024,256]{1,0:T(8,128)(2,1)}, u32[]{:S(2)}) copy-start(bf16[1024,256]{1,0:T(8,128)(2,1)} %copy-done.15) | copy-start | bytes 1572868
  72.6 36.1 %all-to-all-start.2 = ((bf16[16,32,1024]{2,1,0:T(8,128)(2,1)}), bf16[16,32,1024]{2,1,0:T(8,128)(2,1)S(1)}, u32[]{:S(2)}, u32[]{:S(2)}) async-start(bf16[16,32,1024]{2,1,0:T(8,128)(2,1)} %bitcast.15), calls=%async_computation.2 | async-start | bytes 2097152 | tf_op jit(solution)/shard_map/all_to_all | solution.py:447
  79.8 3.4 %collective-permute-start.9 = (bf16[1024,256]{1,0:T(8,128)(2,1)S(1)}, bf16[1024,256]{1,0:T(8,128)(2,1)S(1)}, u32[]{:S(2)}, u32[]{:S(2)}) collective-permute-start(bf16[1024,256]{1,0:T(8,128)(2,1)S(1)} %copy-done.14), channel_id=1, source_target_pairs={{0,8},{8,0},{1,9},{9,1},{2,10},{10,2},{3,11},{11,3},{4,12},{12,4},... | collective-permute-start | bytes 1572872 | tf_op jit(solution)/shard_map/ppermute | solution.py:416
  81.7 2.3 %collective-permute-start.10 = (bf16[1024,256]{1,0:T(8,128)(2,1)S(1)}, bf16[1024,256]{1,0:T(8,128)(2,1)S(1)}, u32[]{:S(2)}, u32[]{:S(2)}) collective-permute-start(bf16[1024,256]{1,0:T(8,128)(2,1)S(1)} %copy-done.8), channel_id=1, source_target_pairs={{0,8},{8,0},{1,9},{9,1},{2,10},{10,2},{3,11},{11,3},{4,12},{12,4},... | collective-permute-start | bytes 1572872 | tf_op jit(solution)/shard_map/ppermute | solution.py:416
  81.8 3.7 %collective-permute-start.11 = (bf16[1024,256]{1,0:T(8,128)(2,1)S(1)}, bf16[1024,256]{1,0:T(8,128)(2,1)S(1)}, u32[]{:S(2)}, u32[]{:S(2)}) collective-permute-start(bf16[1024,256]{1,0:T(8,128)(2,1)S(1)} %copy-done.16), channel_id=1, source_target_pairs={{0,8},{8,0},{1,9},{9,1},{2,10},{10,2},{3,11},{11,3},{4,12},{12,4},... | collective-permute-start | bytes 1572872 | tf_op jit(solution)/shard_map/ppermute | solution.py:416
  82.2 4.1 %collective-permute-start.12 = (bf16[1024,256]{1,0:T(8,128)(2,1)S(1)}, bf16[1024,256]{1,0:T(8,128)(2,1)}, u32[]{:S(2)}, u32[]{:S(2)}) collective-permute-start(bf16[1024,256]{1,0:T(8,128)(2,1)S(1)} %copy-done.6), channel_id=1, source_target_pairs={{0,8},{8,0},{1,9},{9,1},{2,10},{10,2},{3,11},{11,3},{4,12},{12,4},... | collective-permute-start | bytes 1572872 | tf_op jit(solution)/shard_map/ppermute | solution.py:416
  83.2 3.1 %copy-start.17 = (bf16[1024,256]{1,0:T(8,128)(2,1)}, bf16[1024,256]{1,0:T(8,128)(2,1)S(1)}, u32[]{:S(2)}) copy-start(bf16[1024,256]{1,0:T(8,128)(2,1)S(1)} %collective-permute-done.9.refs_4_) | copy-start | bytes 1572868
  83.9 1.5 copy-start.18
  85.4 0.8 copy-start.19
  108.7 9.2 %copy-start.1 = (bf16[16,32,1024]{2,1,0:T(8,128)(2,1)}, bf16[16,32,1024]{2,1,0:T(8,128)(2,1)S(1)}, u32[]{:S(2)}) copy-start(bf16[16,32,1024]{2,1,0:T(8,128)(2,1)S(1)} %all-to-all-done.2.mixed_near) | copy-start | bytes 3145732
  108.7 33.0 %all-to-all-start.1 = ((bf16[32,32,512]{2,1,0:T(8,128)(2,1)}), bf16[32,32,512]{2,1,0:T(8,128)(2,1)S(1)}, u32[]{:S(2)}, u32[]{:S(2)}) async-start(bf16[32,32,512]{2,1,0:T(8,128)(2,1)} %bitcast.14), calls=%async_computation.1 | async-start | bytes 2097152 | tf_op jit(solution)/shard_map/all_to_all | solution.py:422
  113.5 3.0 %collective-permute-start.14 = (bf16[4,4,128,256]{3,2,1,0:T(8,128)(2,1)}, bf16[4,4,128,256]{3,2,1,0:T(8,128)(2,1)S(1)}, u32[]{:S(2)}, u32[]{:S(2)}) collective-permute-start(bf16[4,4,128,256]{3,2,1,0:T(8,128)(2,1)} %get-tuple-element.33), channel_id=1, source_target_pairs={{0,8},{8,0},{1,9},{9,1},{2,10},{10,2},{3,11},{11,3},{4,12},{12,4},... | collective-permute-start | bytes 3145736 | tf_op jit(solution)/shard_map/ppermute | solution.py:416
  113.9 4.1 %collective-permute-start.13 = (bf16[16,32,1024]{2,1,0:T(8,128)(2,1)S(1)}, bf16[16,32,1024]{2,1,0:T(8,128)(2,1)}, u32[]{:S(2)}, u32[]{:S(2)}) collective-permute-start(bf16[16,32,1024]{2,1,0:T(8,128)(2,1)S(1)} %all-to-all-done.2.mixed_near), channel_id=1, source_target_pairs={{0,8},{8,0},{1,9},{9,1},{2,10},{10,2},{3,11},{11,3},{4,12},{12,4},... | collective-permute-start | bytes 3145736 | tf_op jit(solution)/shard_map/ppermute | solution.py:416
  116.5 1.4 copy-start.13
  122.8 22.7 %collective-permute-start.15 = (bf16[16,2,32,256]{3,2,1,0:T(8,128)(2,1)}, bf16[16,2,32,256]{3,2,1,0:T(8,128)(2,1)S(1)}, u32[]{:S(2)}, u32[]{:S(2)}) collective-permute-start(bf16[16,2,32,256]{3,2,1,0:T(8,128)(2,1)} %get-tuple-element.34), channel_id=1, source_target_pairs={{0,16},{16,32},{32,48},{48,0},{1,17},{17,33},{33,49},{49,1},{2,18}... | collective-permute-start | bytes 1572872 | tf_op jit(solution)/shard_map/ppermute | solution.py:416
  124.1 21.3 %collective-permute-start.16 = (bf16[16,2,32,256]{3,2,1,0:T(8,128)(2,1)}, bf16[16,2,32,256]{3,2,1,0:T(8,128)(2,1)S(1)}, u32[]{:S(2)}, u32[]{:S(2)}) collective-permute-start(bf16[16,2,32,256]{3,2,1,0:T(8,128)(2,1)} %get-tuple-element.35), channel_id=1, source_target_pairs={{0,48},{16,0},{32,16},{48,32},{1,49},{17,1},{33,17},{49,33},{2,50}... | collective-permute-start | bytes 1572872 | tf_op jit(solution)/shard_map/ppermute | solution.py:416
  141.7 3.8 %copy-start = (bf16[32,32,512]{2,1,0:T(8,128)(2,1)}, bf16[32,32,512]{2,1,0:T(8,128)(2,1)S(1)}, u32[]{:S(2)}) copy-start(bf16[32,32,512]{2,1,0:T(8,128)(2,1)S(1)} %all-to-all-done.1.parts_ref) | copy-start | bytes 3145732
  145.5 0.8 copy-start.9
  145.5 0.9 copy-start.11
  146.4 15.1 %copy-start.23 = (bf16[16,2,32,256]{3,2,1,0:T(8,128)(2,1)S(1)}, bf16[16,2,32,256]{3,2,1,0:T(8,128)(2,1)}, u32[]{:S(2)}) copy-start(bf16[16,2,32,256]{3,2,1,0:T(8,128)(2,1)} %get-tuple-element.40) | copy-start | bytes 1572868
  153.9 33.8 %all-to-all-start.3 = ((bf16[32,3,32,128]{3,2,1,0:T(8,128)(2,1)}), bf16[32,3,32,128]{3,2,1,0:T(8,128)(2,1)S(1)}, u32[]{:S(2)}, u32[]{:S(2)}) async-start(bf16[32,3,32,128]{3,2,1,0:T(8,128)(2,1)} %corr.1._), calls=%async_computation.3 | async-start | bytes 1572864 | tf_op jit(solution)/shard_map/all_to_all | solution.py:422
  161.5 23.8 %collective-permute-start.17 = (bf16[16,2,32,256]{3,2,1,0:T(8,128)(2,1)S(1)}, bf16[16,2,32,256]{3,2,1,0:T(8,128)(2,1)S(1)}, u32[]{:S(2)}, u32[]{:S(2)}) collective-permute-start(bf16[16,2,32,256]{3,2,1,0:T(8,128)(2,1)S(1)} %copy-done.23), channel_id=1, source_target_pairs={{0,32},{16,48},{32,0},{48,16},{1,33},{17,49},{33,1},{49,17},{2,34}... | collective-permute-start | bytes 1572872 | tf_op jit(solution)/shard_map/ppermute | solution.py:416
  165.1 20.2 %copy-start.10 = (bf16[16,2,32,256]{3,2,1,0:T(8,128)(2,1)S(1)}, bf16[16,2,32,256]{3,2,1,0:T(8,128)(2,1)}, u32[]{:S(2)}) copy-start(bf16[16,2,32,256]{3,2,1,0:T(8,128)(2,1)} %copy-done.9) | copy-start | bytes 1572868
  165.1 20.2 %copy-start.12 = (bf16[16,2,32,256]{3,2,1,0:T(8,128)(2,1)S(1)}, bf16[16,2,32,256]{3,2,1,0:T(8,128)(2,1)}, u32[]{:S(2)}) copy-start(bf16[16,2,32,256]{3,2,1,0:T(8,128)(2,1)} %copy-done.11) | copy-start | bytes 1572868
  187.7 0.9 copy-start.4

commit v4 on v3

--- a/solution.py
+++ b/solution.py
@@ -113,8 +113,7 @@
     )
 
 
-def conv_kernel(fields_ref, skip_ref, table_ref, *refs):
-    total_ref, spec_ref, mixed_ref = refs[-3:]
+def conv_kernel(fields_ref, skip_ref, table_ref, total_ref, spec_ref, mixed_ref):
     first, twist, ahead, behind, last = unpack(table_ref)
     gated = fields_ref[:, 0].astype(f32)
     taps = fields_ref[:, 1].astype(f32)
@@ -141,8 +140,7 @@
                     mixed_ref[copy, x, :, place : place + INNER] = block
 
 
-def corr_kernel(parts_ref, fields_ref, total_ref, spec_ref, skip_ref, table_ref, *refs):
-    out_ref = refs[-1]
+def corr_kernel(parts_ref, fields_ref, total_ref, spec_ref, skip_ref, table_ref, out_ref):
     first, twist, ahead, behind, last = unpack(table_ref)
     grad_mix = []
     for z in range(4):
@@ -180,7 +178,7 @@
     return pl.CostEstimate(flops=flops, bytes_accessed=megabytes * 2**20, transcendentals=0)
 
 
-def conv_call(fields, skip_rows, table, after):
+def conv_call(fields, skip_rows, table):
     blocks, _, owned, inner = fields.shape
     steps = owned // GROUP
     spec_rows = KEPT * GROUP
@@ -191,8 +189,7 @@
             pl.BlockSpec((blocks, 3, GROUP, inner), lambda g: (0, 0, g, 0)),
             pl.BlockSpec((GROUP, inner), lambda g: (g, 0)),
             pl.BlockSpec(table.shape, lambda g: (0, 0)),
-        ]
-        + [pl.BlockSpec(memory_space=pl.ANY)] * len(after),
+        ],
         out_specs=[
             pl.BlockSpec((blocks, GROUP, inner), lambda g: (0, g, 0)),
             pl.BlockSpec((4, 1, spec_rows, inner), lambda g: (0, g, 0, 0)),
@@ -206,10 +203,10 @@
         compiler_params=params(),
         cost_estimate=cost(10**9, 6),
         name="conv",
-    )(fields, skip_rows, table, *after)
-
-
-def corr_call(parts, fields, total, spec, skip_rows, table, after):
+    )(fields, skip_rows, table)
+
+
+def corr_call(parts, fields, total, spec, skip_rows, table):
     blocks, owned, inner = total.shape
     steps = owned // GROUP
     spec_rows = KEPT * GROUP
@@ -223,14 +220,13 @@
             pl.BlockSpec((4, 1, spec_rows, inner), lambda g: (0, g, 0, 0)),
             pl.BlockSpec((GROUP, inner), lambda g: (g, 0)),
             pl.BlockSpec(table.shape, lambda g: (0, 0)),
-        ]
-        + [pl.BlockSpec(memory_space=pl.ANY)] * len(after),
+        ],
         out_specs=pl.BlockSpec((blocks, 3, GROUP, inner), lambda g: (0, 0, g, 0)),
         out_shape=jax.ShapeDtypeStruct((blocks, 3, owned, inner), bf16),
         compiler_params=params(),
         cost_estimate=cost(10**9, 6),
         name="corr",
-    )(parts, fields, total, spec, skip_rows, table, *after)
+    )(parts, fields, total, spec, skip_rows, table)
 
 
 def prep_kernel(key_ref, value_ref, taps_ref, query_ref, *refs):
@@ -242,20 +238,20 @@
     fields_ref[:, 2] = query_ref[...].astype(f32).T.astype(bf16).reshape(shape)
 
 
-def prep_call(key_proj, value_proj, filter_taps, query_proj, owned, after):
+def prep_call(key_proj, value_proj, filter_taps, query_proj, owned):
     toks, channels = key_proj.shape
     wide = 512
     tall = pl.BlockSpec((toks, wide), lambda n: (0, n))
     return pl.pallas_call(
         prep_kernel,
         grid=(channels // wide,),
-        in_specs=[tall] * 4 + [pl.BlockSpec(memory_space=pl.ANY)] * len(after),
+        in_specs=[tall] * 4,
         out_specs=pl.BlockSpec((wide // owned, 3, owned, toks), lambda n: (n, 0, 0, 0)),
         out_shape=jax.ShapeDtypeStruct((channels // owned, 3, owned, toks), bf16),
         compiler_params=params(),
         cost_estimate=cost(10**7, 2),
         name="prep",
-    )(key_proj, value_proj, filter_taps, query_proj, *after)
+    )(key_proj, value_proj, filter_taps, query_proj)
 
 
 def last_kernel(corr_ref, key_ref, value_ref, grad_key_ref, grad_value_ref, grad_filter_ref, grad_query_ref):
@@ -290,8 +286,7 @@
 
 def mix_kernel(place_ref, grad_out_ref, *refs):
     near_w, far_w, passed = refs[:4], refs[4:8], refs[8:12]
-    parts, near_out, far_out = refs[13:16]
-    weight, grad, sems, out_sems = refs[16:]
+    parts, near_out, far_out, weight, grad, sems, out_sems = refs[-7:]
     my_z, my_x, my_core, my_y = (place_ref[n] for n in range(4))
     width = weight.shape[3]
     copies = []
@@ -301,10 +296,6 @@
         copy.start()
         copies.append(copy)
 
-    for back in range(4):
-        col = lax.rem(my_x - back + 4, 4)
-        begin(near_w[back], weight.at[my_core, col])
-        begin(far_w[back], weight.at[1 - my_core, col])
     for back in range(4):
         for core in range(2):
             for s in range(1, 4):
@@ -316,7 +307,15 @@
         for core in range(2):
             start = pl.multiple_of(((my_z * 4 + col) * 2 + core) * width, width)
             begin(grad_out_ref.at[:, pl.ds(start, width)], grad.at[col, core, my_z])
-    for copy in copies:
+    fixed = len(copies)
+    step = 256
+    for m in range(weight.shape[2] // step):
+        here = pl.ds(m * step, step)
+        for back in range(4):
+            col = lax.rem(my_x - back + 4, 4)
+            begin(near_w[back].at[here], weight.at[my_core, col, here])
+            begin(far_w[back].at[here], weight.at[1 - my_core, col, here])
+    for copy in copies[:fixed]:
         copy.wait()
 
     near_copy = pltpu.make_async_copy(grad.at[:, my_core], near_out, out_sems.at[0])
@@ -324,28 +323,24 @@
     near_copy.start()
     far_copy.start()
 
-    step = 256
-    for pair in ((0, 1), (2, 3)):
-        lines = [jnp.concatenate([grad[n // 2, n % 2, z] for n in range(8)], 1) for z in pair]
-        grad_rows = jnp.concatenate(lines, 0)
-        toks = grad_rows.shape[0]
-
-        def body(m, _, grad_rows=grad_rows, pair=pair, toks=toks):
-            here = pl.ds(pl.multiple_of(m * step, step), step)
-            rows = jnp.concatenate([weight[n % 2, n // 2, here, :] for n in range(8)], 1)
-            part = lax.dot_general(
-                rows, grad_rows, (((1,), (1,)), ((), ())), preferred_element_type=f32
-            )
-            start = pair[0] // 2 * toks
-            parts[here, start : start + toks] = part.astype(bf16)
-            return 0
-
-        lax.fori_loop(0, weight.shape[2] // step, body, 0)
+    lines = [
+        jnp.concatenate([grad[n // 2, n % 2, z] for n in range(8)], 1) for z in range(4)
+    ]
+    grad_rows = jnp.concatenate(lines, 0)
+    for m in range(weight.shape[2] // step):
+        for copy in copies[fixed + 8 * m : fixed + 8 * m + 8]:
+            copy.wait()
+        here = slice(m * step, (m + 1) * step)
+        rows = jnp.concatenate([weight[n % 2, n // 2, here, :] for n in range(8)], 1)
+        part = lax.dot_general(
+            rows, grad_rows, (((1,), (1,)), ((), ())), preferred_element_type=f32
+        )
+        parts[here, :] = part.astype(bf16)
     near_copy.wait()
     far_copy.wait()
 
 
-def mix_call(place, grad_out, near_w, far_w, passed, after):
+def mix_call(place, grad_out, near_w, far_w, passed):
     toks = grad_out.shape[0]
     rows, width = near_w[0].shape
     any_spec = pl.BlockSpec(memory_space=pl.ANY)
@@ -353,22 +348,22 @@
     blocks = jax.ShapeDtypeStruct((4, 4, toks, width), bf16)
     return pl.pallas_call(
         mix_kernel,
-        in_specs=[pl.BlockSpec(memory_space=pltpu.SMEM)] + [any_spec] * 14,
+        in_specs=[pl.BlockSpec(memory_space=pltpu.SMEM)] + [any_spec] * 13,
         out_specs=[vmem] + [any_spec] * 2,
         out_shape=[jax.ShapeDtypeStruct((rows, 4 * toks), bf16)] + [blocks] * 2,
         scratch_shapes=[
             pltpu.VMEM((2, 4, rows, width), bf16),
             pltpu.VMEM((4, 2, 4, toks, width), bf16),
-            pltpu.SemaphoreType.DMA((40,)),
+            pltpu.SemaphoreType.DMA((64,)),
             pltpu.SemaphoreType.DMA((2,)),
         ],
         compiler_params=params(),
         cost_estimate=cost(2 * rows * toks * 4 * 8 * width, 9),
         name="mix",
-    )(place, grad_out, *near_w, *far_w, *passed, after)
-
-
-def product_kernel(cols_ref, mixed_near, mixed_far, near, far, _, *outs):
+    )(place, grad_out, *near_w, *far_w, *passed)
+
+
+def product_kernel(cols_ref, mixed_near, mixed_far, near, far, *outs):
     my_core = cols_ref[4]
     owners, owned, depth = mixed_near.shape
     half = depth // 2
@@ -385,19 +380,19 @@
             out[:, core] = product.reshape(owners, owned, product.shape[1])
 
 
-def product_call(cols, mixed_near, mixed_far, near, far, after, kinds):
+def product_call(cols, mixed_near, mixed_far, near, far, kinds):
     owners, owned, depth = mixed_near.shape
     width = near.shape[3]
     vmem = pl.BlockSpec(memory_space=pltpu.VMEM)
     return pl.pallas_call(
         product_kernel,
-        in_specs=[pl.BlockSpec(memory_space=pltpu.SMEM)] + [vmem] * 4 + [pl.BlockSpec(memory_space=pl.ANY)],
+        in_specs=[pl.BlockSpec(memory_space=pltpu.SMEM)] + [vmem] * 4,
         out_specs=[vmem] * len(kinds),
         out_shape=[jax.ShapeDtypeStruct((owners, 2, owned, width), kind) for kind in kinds],
         compiler_params=params(),
         cost_estimate=cost(4 * owners * owned * width * depth * len(kinds), 5),
         name="product",
-    )(cols, mixed_near, mixed_far, near, far, after)
+    )(cols, mixed_near, mixed_far, near, far)
 
 
 def shards(grad_out, out_weight, query_proj, key_proj, value_proj, filter_taps, skip_gain):
@@ -421,29 +416,32 @@
     def to_all(item):
         return lax.all_to_all(item, CTX, split_axis=0, concat_axis=0, tiled=True)
 
-    passed, near_w = {}, {0: out_weight}
-    for s in order:
-        start = ((my_z + s) % 4 * 4 + my_y) * (2 * width)
-        passed[s] = shift(lax.dynamic_slice_in_dim(grad_out, start, 2 * width, 1), "zh", s)
-        if s != 2:
-            near_w[s] = shift(out_weight, "x", s)
-    passed = {0: jnp.stack([passed[s] for s in range(1, 4)])}
-    late_w = lax.optimization_barrier((out_weight, passed[0]))[0]
-    near_w[2] = shift(late_w, "x", 2)
-    for s in order:
-        passed[s] = shift(passed[0], "y", s)
     place = jnp.stack([my_z, my_x, my_core, my_y]).astype(jnp.int32)
     skip_rows = lax.dynamic_slice_in_dim(
         skip_gain, lax.axis_index(CTX) * owned, owned, 0
     )
     skip_rows = jnp.broadcast_to(skip_rows[:, None], (owned, tok_rows))
 
-    fields = prep_call(key_proj, value_proj, filter_taps, query_proj, owned, [near_w[1], near_w[3], passed[0], skip_rows, place])
-    fields = to_all(fields)
-
-    total, spec, mixed = conv_call(
-        fields, skip_rows, table, [near_w[2]] + [passed[s] for s in order]
-    )
+    def after(item, *others):
+        return lax.optimization_barrier((item, *others))[0]
+
+    packed = prep_call(key_proj, value_proj, filter_taps, query_proj, owned)
+    fields = to_all(packed)
+    grad_late, weight_late = after(grad_out, packed), after(out_weight, packed)
+
+    passed, near_w = {}, {0: weight_late}
+    for s in order:
+        start = ((my_z + s) % 4 * 4 + my_y) * (2 * width)
+        passed[s] = shift(lax.dynamic_slice_in_dim(grad_late, start, 2 * width, 1), "zh", s)
+        if s != 2:
+            near_w[s] = shift(weight_late, "x", s)
+    passed = {0: jnp.stack([passed[s] for s in range(1, 4)])}
+    near_w[2] = shift(after(out_weight, passed[0]), "x", 2)
+    for s in order:
+        passed[s] = shift(passed[0], "y", s)
+
+    fields = after(fields, passed[0], near_w[1], near_w[3], skip_rows, place)
+    total, spec, mixed = conv_call(fields, skip_rows, table)
     mixed = lax.all_to_all(
         mixed.reshape(16, owned, 8 * tok_rows), ("zh", "x"), split_axis=0, concat_axis=0, tiled=True
     )
@@ -452,7 +450,7 @@
     far_w = {s: swap(item) for s, item in zip(near_w, held)}
     far_w = [far_w[s] for s in range(4)]
     parts, near, far = mix_call(
-        place, grad_out, [near_w[s] for s in range(4)], far_w, [passed[s] for s in range(4)], total
+        place, grad_out, [near_w[s] for s in range(4)], far_w, [passed[s] for s in range(4)]
     )
     far = swap(far)
     parts = to_all(parts.reshape(context_size, owned, 4 * tok_rows))
@@ -461,10 +459,11 @@
     cols = [(my_x + s) % 4 for s in (2, 1, 3, 0)]
     near_cols = jnp.stack(cols + [my_core]).astype(jnp.int32)
     last_cols = jnp.stack(cols[3:] * 4 + [my_core]).astype(jnp.int32)
-    sent = product_call(near_cols, mixed, mixed_far, near, far, total, (bf16,) * 3)
+    sent = product_call(near_cols, mixed, mixed_far, near, far, (bf16,) * 3)
     sent = {s: shift(item, "x", s) for s, item in zip((2, 1, 3), sent)}
-    corr = corr_call(parts, fields, total, spec, skip_rows, table, [sent[1], sent[3]])
-    grad_weight = product_call(last_cols, mixed, mixed_far, near, far, corr, (f32,))[0]
+    parts = after(parts, sent[1], sent[3])
+    corr = corr_call(parts, fields, total, spec, skip_rows, table)
+    grad_weight = product_call(after(last_cols, corr), mixed, mixed_far, near, far, (f32,))[0]
     corr = to_all(corr)
     grad_key, grad_value, grad_filter, grad_query = last_call(corr, key_proj, value_proj)
     for s in (1, 3, 2):

time: 192 us -> 186 us (0.969)
  waiting for transfers between devices: 82.1 us -> 73.9 us
  starting transfers between devices: 58.5 us -> 66.1 us
  local copies, waits for them, and re-layouts: 9.17 us -> 6.58 us
    all_to_all x1, waiting for transfers between devices: 13.8 us -> 0.01 us  [shards(): lax.all_to_all(mixed.reshape(16, owned, 8 * tok_rows), ('zh', 'x'), split...]
    all_to_all x3, starting transfers between devices: 21 us -> 31.3 us  [to_all(): return lax.all_to_all(item, CTX, split_axis=0, concat_axis=0, tiled=True)]
    ppermute x18, waiting for transfers between devices: 51.9 us -> 56.9 us  [shift(): return lax.ppermute(item, axis, [(n, (n + by) % size) for n in range(size)])]
    ppermute x18, starting transfers between devices: 30.2 us -> 26.7 us  [shift(): return lax.ppermute(item, axis, [(n, (n + by) % size) for n in range(size)])]
    unnamed x48 -> x32, local copies, waits for them, and re-layouts: 5.39 us -> 2.66 us
  transfers between devices with their start and end apart: 22 -> 22, of which waited for: 14 -> 13; matrix products, arithmetic and copies ran while one was open for 4% -> 3% of each run, Pallas kernels for 9% -> 9%
where the time goes in v4:
time: 186 us; the launch traced here: 185 us
  waiting for transfers between devices  73.9 us (40%)
  starting transfers between devices  66.1 us (36%)
  Pallas kernels  35 us (19%)
  local copies, waits for them, and re-layouts  6.58 us (4%)
  other arithmetic  3.02 us (2%)
    ppermute x18, waiting for transfers between devices, shift(): return lax.ppermute(item, axis, [(n, (n + by) % size) for n in range(size)])  56.9 us
    all_to_all x3, starting transfers between devices, to_all(): return lax.all_to_all(item, CTX, split_axis=0, concat_axis=0, tiled=True)  31.3 us
    ppermute x18, starting transfers between devices, shift(): return lax.ppermute(item, axis, [(n, (n + by) % size) for n in range(size)])  26.7 us
    all_to_all x3, waiting for transfers between devices, to_all(): return lax.all_to_all(item, CTX, split_axis=0, concat_axis=0, tiled=True)  17 us
    pallas_call x2, Pallas kernels, product_call(): pl.pallas_call(product_kernel, in_specs=[pl.BlockSpec(memory_space=pltpu....  8.78 us
    all_to_all x1, starting transfers between devices, shards(): lax.all_to_all(mixed.reshape(16, owned, 8 * tok_rows), ('zh', 'x'), split...  8.19 us
    pallas_call x1, Pallas kernels, corr_call(): pl.pallas_call(corr_kernel, grid=(steps,), in_specs=[pl.BlockSpec((blocks...  7.34 us
    pallas_call x1, Pallas kernels, mix_call(): pl.pallas_call(mix_kernel, in_specs=[pl.BlockSpec(memory_space=pltpu.SMEM...  7.21 us
  transfers between devices with their start and end apart: 22, of which 13 were waited for; matrix products, arithmetic and copies ran while one was open for 3% of the time, Pallas kernels for 9%

profile of v4, /device:TPU:1, one launch (start us, length us, event | category | flops | bytes accessed | tf_op | source)
XLA Modules:
  0.0 185.4 jit_solution(5699711125210853080)
XLA Ops:
  0.6 0.0 copy-start.6
  0.6 2.3 %prep.1 = bf16[32,3,32,128]{3,2,1,0:T(8,128)(2,1)} custom-call(bf16[128,1024]{1,0:T(8,128)(2,1)} %key_ref.3, bf16[128,1024]{1,0:T(8,128)(2,1)} %value_ref.3, bf16[128,1024]{1,0:T(8,128)(2,1)} %taps_ref.1, bf16[128,1024]{1,0:T(8,128)(2,1)} %query_ref.1), custom_call_target="tpu_custom_call" | custom-call | flops 10000000 | bytes 2097152 | tf_op jit(solution)/shard_map/prep/pallas_call | solution.py:245
  2.9 12.6 %all-to-all-start = ((bf16[32,3,32,128]{3,2,1,0:T(8,128)(2,1)}), bf16[32,3,32,128]{3,2,1,0:T(8,128)(2,1)S(1)}, u32[]{:S(2)}, u32[]{:S(2)}) async-start(bf16[32,3,32,128]{3,2,1,0:T(8,128)(2,1)} %prep.1), calls=%async_computation | async-start | bytes 1572864 | tf_op jit(solution)/shard_map/all_to_all | solution.py:417
  15.5 2.7 %collective-permute-start.5 = (bf16[1024,256]{1,0:T(8,128)(2,1)S(1)}, bf16[1024,256]{1,0:T(8,128)(2,1)S(1)}, u32[]{:S(2)}, u32[]{:S(2)}) collective-permute-start(bf16[1024,256]{1,0:T(8,128)(2,1)S(1)} %copy-done.6), channel_id=1, source_target_pairs={{0,48},{16,0},{32,16},{48,32},{1,49},{17,1},{33,17},{49,33},{2,50}... | collective-permute-start | bytes 1572872 | tf_op jit(solution)/shard_map/ppermute | solution.py:411
  18.2 0.0 collective-permute-start
  18.2 1.1 constant_dynamic-slice_fusion.2
  19.3 2.2 %collective-permute-start.1 = (bf16[128,512]{1,0:T(8,128)(2,1)S(1)}, bf16[128,512]{1,0:T(8,128)(2,1)S(1)}, u32[]{:S(2)}, u32[]{:S(2)}) collective-permute-start(bf16[128,512]{1,0:T(8,128)(2,1)S(1)} %get-tuple-element.51), channel_id=1, source_target_pairs={{0,64},{64,128},{128,192},{192,0},{1,65},{65,129},{129,193},{193,1... | collective-permute-start | bytes 393224 | tf_op jit(solution)/shard_map/ppermute | solution.py:411
  21.5 1.5 collective-permute-start.3
  22.9 5.1 %collective-permute-start.2 = (bf16[128,512]{1,0:T(8,128)(2,1)S(1)}, bf16[128,512]{1,0:T(8,128)(2,1)S(1)}, u32[]{:S(2)}, u32[]{:S(2)}) collective-permute-start(bf16[128,512]{1,0:T(8,128)(2,1)S(1)} %get-tuple-element.53), channel_id=1, source_target_pairs={{0,128},{64,192},{128,0},{192,64},{1,129},{65,193},{129,1},{193,65... | collective-permute-start | bytes 393224 | tf_op jit(solution)/shard_map/ppermute | solution.py:411
  28.1 0.8 dynamic_slice.15
  28.8 0.6 pad_add_fusion.place_ref
  29.4 9.4 %collective-permute-done.1 = bf16[128,512]{1,0:T(8,128)(2,1)S(1)} collective-permute-done((bf16[128,512]{1,0:T(8,128)(2,1)S(1)}, bf16[128,512]{1,0:T(8,128)(2,1)S(1)}, u32[]{:S(2)}, u32[]{:S(2)}) %collective-permute-start.1) | collective-permute-done | bytes 131104 | tf_op jit(solution)/shard_map/ppermute | solution.py:411
  38.9 6.6 %collective-permute-done.3 = bf16[128,512]{1,0:T(8,128)(2,1)S(1)} collective-permute-done((bf16[128,512]{1,0:T(8,128)(2,1)S(1)}, bf16[128,512]{1,0:T(8,128)(2,1)S(1)}, u32[]{:S(2)}, u32[]{:S(2)}) %collective-permute-start.3) | collective-permute-done | bytes 131104 | tf_op jit(solution)/shard_map/ppermute | solution.py:411
  45.5 0.0 collective-permute-done.2
  45.6 0.0 collective-permute-done.5.refs_3_
  45.6 0.0 collective-permute-done.refs_1_
  45.6 0.0 copy-start.8
  45.6 0.0 all-to-all-done.fields_ref
  45.6 0.8 broadcast_in_dim.2.skip_ref
  46.5 0.1 copy-done.3
  46.6 7.1 %conv.1 = (f32[32,32,128]{2,1,0:T(8,128)}, f32[4,2,528,128]{3,2,1,0:T(8,128)}, bf16[4,4,32,1024]{3,2,1,0:T(8,128)(2,1)}) custom-call(bf16[32,3,32,128]{3,2,1,0:T(8,128)(2,1)} %copy-done.3, f32[32,128]{1,0:T(8,128)} %broadcast_in_dim.2.skip_ref, f32[592,128]{1,0:T(8,128)} %constant.74.clone.table_ref), custom_call_target="tpu_custom_call" | custom-call | flops 1000000000 | bytes 6291456 | tf_op jit(solution)/shard_map/conv/pallas_call | solution.py:185
  53.7 8.2 %all-to-all-start.2 = ((bf16[16,32,1024]{2,1,0:T(8,128)(2,1)}), bf16[16,32,1024]{2,1,0:T(8,128)(2,1)S(1)}, u32[]{:S(2)}, u32[]{:S(2)}) async-start(bf16[16,32,1024]{2,1,0:T(8,128)(2,1)} %bitcast.15), calls=%async_computation.2 | async-start | bytes 2097152 | tf_op jit(solution)/shard_map/all_to_all | solution.py:445
  61.9 2.9 %collective-permute-start.4 = (bf16[1024,256]{1,0:T(8,128)(2,1)S(1)}, bf16[1024,256]{1,0:T(8,128)(2,1)S(1)}, u32[]{:S(2)}, u32[]{:S(2)}) collective-permute-start(bf16[1024,256]{1,0:T(8,128)(2,1)S(1)} %copy-done.6), channel_id=1, source_target_pairs={{0,32},{16,48},{32,0},{48,16},{1,33},{17,49},{33,1},{49,17},{2,34}... | collective-permute-start | bytes 1572872 | tf_op jit(solution)/shard_map/ppermute | solution.py:411
  64.8 2.9 %collective-permute-start.8 = (bf16[3,128,512]{2,1,0:T(8,128)(2,1)S(1)}, bf16[3,128,512]{2,1,0:T(8,128)(2,1)S(1)}, u32[]{:S(2)}, u32[]{:S(2)}) collective-permute-start(bf16[3,128,512]{2,1,0:T(8,128)(2,1)S(1)} %pad_maximum_fusion.refs_8_), channel_id=1, source_target_pairs={{0,2},{1,3},{2,0},{3,1},{4,6},{5,7},{6,4},{7,5},{8,10},{9,11},{10,... | collective-permute-start | bytes 1179656 | tf_op jit(solution)/shard_map/ppermute | solution.py:411
  67.7 0.8 collective-permute-start.7
  68.5 0.7 collective-permute-start.6
  69.2 5.8 %collective-permute-done.8.refs_10_ = bf16[3,128,512]{2,1,0:T(8,128)(2,1)S(1)} collective-permute-done((bf16[3,128,512]{2,1,0:T(8,128)(2,1)S(1)}, bf16[3,128,512]{2,1,0:T(8,128)(2,1)S(1)}, u32[]{:S(2)}, u32[]{:S(2)}) %collective-permute-start.8) | collective-permute-done | bytes 393248 | tf_op jit(solution)/shard_map/ppermute | solution.py:411
  75.0 10.1 %collective-permute-done.7.refs_11_ = bf16[3,128,512]{2,1,0:T(8,128)(2,1)S(1)} collective-permute-done((bf16[3,128,512]{2,1,0:T(8,128)(2,1)S(1)}, bf16[3,128,512]{2,1,0:T(8,128)(2,1)S(1)}, u32[]{:S(2)}, u32[]{:S(2)}) %collective-permute-start.7) | collective-permute-done | bytes 393248 | tf_op jit(solution)/shard_map/ppermute | solution.py:411
  85.1 0.5 collective-permute-done.6.refs_9_
  85.6 0.0 collective-permute-done.4.refs_2_
  85.6 0.2 copy-done.14
  85.9 0.5 copy-done.15
  86.4 1.2 collective-permute-start.9
  87.5 0.0 collective-permute-start.10
  87.5 0.5 collective-permute-start.11
  88.1 0.0 collective-permute-start.12
  88.1 1.0 collective-permute-done.9.refs_4_
  89.1 1.5 collective-permute-done.10.refs_5_
  90.6 0.7 collective-permute-done.11.refs_6_
  91.3 0.1 copy-done.11
  91.4 0.8 copy-done.12
  92.2 0.0 collective-permute-done.12.refs_7_
  92.2 7.2 %mix.1 = (bf16[1024,512]{1,0:T(8,128)(2,1)}, bf16[4,4,128,256]{3,2,1,0:T(8,128)(2,1)}, bf16[4,4,128,256]{3,2,1,0:T(8,128)(2,1)}) custom-call(s32[4]{0:T(128)} %pad_add_fusion.place_ref, bf16[128,8192]{1,0:T(8,128)(2,1)} %grad_out_ref.1, bf16[1024,256]{1,0:T(8,128)(2,1)} %refs_0_, bf16[1024,256]{1,0:T(8,128)(2,1)} %copy-done.8, bf16[1024,256]{1,0:T(8,128)(2,1)} %copy-done.9, ...), custom_call_target="tpu_custom_call" | custom-call | flops 2147483648 | bytes 9437184 | tf_op jit(solution)/shard_map/mix/pallas_call | solution.py:349
  99.5 10.6 %all-to-all-start.1 = ((bf16[32,32,512]{2,1,0:T(8,128)(2,1)}), bf16[32,32,512]{2,1,0:T(8,128)(2,1)S(1)}, u32[]{:S(2)}, u32[]{:S(2)}) async-start(bf16[32,32,512]{2,1,0:T(8,128)(2,1)} %bitcast.14), calls=%async_computation.1 | async-start | bytes 2097152 | tf_op jit(solution)/shard_map/all_to_all | solution.py:417
  110.1 0.3 collective-permute-start.14
  110.4 0.3 collective-permute-start.13
  110.7 0.7 stack.64.cols_ref
  111.3 1.7 collective-permute-done.14.far
  113.0 1.4 collective-permute-done.13.mixed_far
  114.4 4.8 %product.2 = (bf16[16,2,32,256]{3,2,1,0:T(8,128)(2,1)}, bf16[16,2,32,256]{3,2,1,0:T(8,128)(2,1)}, bf16[16,2,32,256]{3,2,1,0:T(8,128)(2,1)}) custom-call(s32[5]{0:T(128)} %stack.64.cols_ref, bf16[16,32,1024]{2,1,0:T(8,128)(2,1)} %copy-done, bf16[16,32,1024]{2,1,0:T(8,128)(2,1)} %collective-permute-done.13.mixed_far, ...), custom_call_target="tpu_custom_call" | custom-call | flops 1610612736 | bytes 5242880 | tf_op jit(solution)/shard_map/product/pallas_call | solution.py:387
  119.3 1.4 collective-permute-start.15
  120.7 1.3 collective-permute-start.16
  122.0 17.0 %all-to-all-done.1.parts_ref = bf16[32,32,512]{2,1,0:T(8,128)(2,1)S(1)} async-done(((bf16[32,32,512]{2,1,0:T(8,128)(2,1)}), bf16[32,32,512]{2,1,0:T(8,128)(2,1)S(1)}, u32[]{:S(2)}, u32[]{:S(2)}) %all-to-all-start.1) | async-done | bytes 1048608 | tf_op jit(solution)/shard_map/all_to_all | solution.py:417
  139.0 1.8 collective-permute-done.15
  140.7 7.3 %corr.1 = bf16[32,3,32,128]{3,2,1,0:T(8,128)(2,1)} custom-call(bf16[32,32,512]{2,1,0:T(8,128)(2,1)} %copy-done.1, bf16[32,3,32,128]{3,2,1,0:T(8,128)(2,1)} %copy-done.3, f32[32,32,128]{2,1,0:T(8,128)} %get-tuple-element.32.total_ref, f32[4,2,528,128]{3,2,1,0:T(8,128)} %get-tuple-element.44.spec_ref, f32[32,128]{1,0:T(8,128)} %broadcast_in_dim.2.skip_ref, ...), custom_call_target="tpu_custom_call" | custom-call | flops 1000000000 | bytes 6291456 | tf_op jit(solution)/shard_map/corr/pallas_call | solution.py:213
  148.1 8.1 %all-to-all-start.3 = ((bf16[32,3,32,128]{3,2,1,0:T(8,128)(2,1)}), bf16[32,3,32,128]{3,2,1,0:T(8,128)(2,1)S(1)}, u32[]{:S(2)}, u32[]{:S(2)}) async-start(bf16[32,3,32,128]{3,2,1,0:T(8,128)(2,1)} %corr.1), calls=%async_computation.3 | async-start | bytes 1572864 | tf_op jit(solution)/shard_map/all_to_all | solution.py:417
  156.2 3.0 %collective-permute-start.17 = (bf16[16,2,32,256]{3,2,1,0:T(8,128)(2,1)}, bf16[16,2,32,256]{3,2,1,0:T(8,128)(2,1)S(1)}, u32[]{:S(2)}, u32[]{:S(2)}) collective-permute-start(bf16[16,2,32,256]{3,2,1,0:T(8,128)(2,1)} %get-tuple-element.50), channel_id=1, source_target_pairs={{0,32},{16,48},{32,0},{48,16},{1,33},{17,49},{33,1},{49,17},{2,34}... | collective-permute-start | bytes 1572872 | tf_op jit(solution)/shard_map/ppermute | solution.py:411
  159.2 0.6 stack.65.cols_ref
  159.8 3.9 %product.3 = f32[16,2,32,256]{3,2,1,0:T(8,128)} custom-call(s32[5]{0:T(128)} %stack.65.cols_ref, bf16[16,32,1024]{2,1,0:T(8,128)(2,1)} %copy-done, bf16[16,32,1024]{2,1,0:T(8,128)(2,1)} %collective-permute-done.13.mixed_far, bf16[4,4,128,256]{3,2,1,0:T(8,128)(2,1)} %get-tuple-element.39.near, bf16[4,4,128,256]{3,2,1,0:T(8,128)(2,1)} %copy-done.4), custom_call_target="tpu_custom_call" | custom-call | flops 536870912 | bytes 5242880 | tf_op jit(solution)/shard_map/product/pallas_call | solution.py:387
  163.7 16.2 %collective-permute-done.17 = bf16[16,2,32,256]{3,2,1,0:T(8,128)(2,1)S(1)} collective-permute-done((bf16[16,2,32,256]{3,2,1,0:T(8,128)(2,1)}, bf16[16,2,32,256]{3,2,1,0:T(8,128)(2,1)S(1)}, u32[]{:S(2)}, u32[]{:S(2)}) %collective-permute-start.17) | collective-permute-done | bytes 524320 | tf_op jit(solution)/shard_map/ppermute | solution.py:411
  179.9 2.4 %multiply_convert_fusion = bf16[16,2,32,256]{3,2,1,0:T(8,128)(2,1)} fusion(bf16[16,2,32,256]{3,2,1,0:T(8,128)(2,1)S(1)} %collective-permute-done.17, bf16[16,2,32,256]{3,2,1,0:T(8,128)(2,1)S(1)} %collective-permute-done.16, f32[16,2,32,256]{3,2,1,0:T(8,128)} %product.3, bf16[16,2,32,256]{3,2,1,0:T(8,128)(2,1)S(1)} %collective-permute-done.15), kind=kLoop, calls=%fused_computation | loop fusion | flops 2097152 | bytes 3145728 | tf_op jit(solution)/shard_map/convert_element_type | solution.py:471
  182.3 0.0 all-to-all-done.3.corr_ref
  182.3 0.9 copy-done.2
  183.2 2.2 %last.1 = (bf16[128,1024]{1,0:T(8,128)(2,1)}, bf16[128,1024]{1,0:T(8,128)(2,1)}, bf16[128,1024]{1,0:T(8,128)(2,1)}, bf16[128,1024]{1,0:T(8,128)(2,1)}) custom-call(bf16[32,3,32,128]{3,2,1,0:T(8,128)(2,1)} %copy-done.2, bf16[128,1024]{1,0:T(8,128)(2,1)} %key_ref.3, bf16[128,1024]{1,0:T(8,128)(2,1)} %value_ref.3), custom_call_target="tpu_custom_call" | custom-call | flops 10000000 | bytes 3145728 | tf_op jit(solution)/shard_map/last/pallas_call | solution.py:275
  (27 shorter events, 0.1 us)
Async XLA Ops:
  0.6 14.9 %copy-start.6 = (bf16[1024,256]{1,0:T(8,128)(2,1)S(1)}, bf16[1024,256]{1,0:T(8,128)(2,1)}, u32[]{:S(2)}) copy-start(bf16[1024,256]{1,0:T(8,128)(2,1)} %refs_0_) | copy-start | bytes 1572868
  2.9 42.7 %all-to-all-start = ((bf16[32,3,32,128]{3,2,1,0:T(8,128)(2,1)}), bf16[32,3,32,128]{3,2,1,0:T(8,128)(2,1)S(1)}, u32[]{:S(2)}, u32[]{:S(2)}) async-start(bf16[32,3,32,128]{3,2,1,0:T(8,128)(2,1)} %prep.1), calls=%async_computation | async-start | bytes 1572864 | tf_op jit(solution)/shard_map/all_to_all | solution.py:417
  15.5 30.0 %collective-permute-start.5 = (bf16[1024,256]{1,0:T(8,128)(2,1)S(1)}, bf16[1024,256]{1,0:T(8,128)(2,1)S(1)}, u32[]{:S(2)}, u32[]{:S(2)}) collective-permute-start(bf16[1024,256]{1,0:T(8,128)(2,1)S(1)} %copy-done.6), channel_id=1, source_target_pairs={{0,48},{16,0},{32,16},{48,32},{1,49},{17,1},{33,17},{49,33},{2,50}... | collective-permute-start | bytes 1572872 | tf_op jit(solution)/shard_map/ppermute | solution.py:411
  18.2 27.4 %collective-permute-start = (bf16[1024,256]{1,0:T(8,128)(2,1)S(1)}, bf16[1024,256]{1,0:T(8,128)(2,1)S(1)}, u32[]{:S(2)}, u32[]{:S(2)}) collective-permute-start(bf16[1024,256]{1,0:T(8,128)(2,1)S(1)} %copy-done.6), channel_id=1, source_target_pairs={{0,16},{16,32},{32,48},{48,0},{1,17},{17,33},{33,49},{49,1},{2,18}... | collective-permute-start | bytes 1572872 | tf_op jit(solution)/shard_map/ppermute | solution.py:411
  19.3 19.6 %collective-permute-start.1 = (bf16[128,512]{1,0:T(8,128)(2,1)S(1)}, bf16[128,512]{1,0:T(8,128)(2,1)S(1)}, u32[]{:S(2)}, u32[]{:S(2)}) collective-permute-start(bf16[128,512]{1,0:T(8,128)(2,1)S(1)} %get-tuple-element.51), channel_id=1, source_target_pairs={{0,64},{64,128},{128,192},{192,0},{1,65},{65,129},{129,193},{193,1... | collective-permute-start | bytes 393224 | tf_op jit(solution)/shard_map/ppermute | solution.py:411
  21.5 24.1 %collective-permute-start.3 = (bf16[128,512]{1,0:T(8,128)(2,1)S(1)}, bf16[128,512]{1,0:T(8,128)(2,1)S(1)}, u32[]{:S(2)}, u32[]{:S(2)}) collective-permute-start(bf16[128,512]{1,0:T(8,128)(2,1)S(1)} %get-tuple-element.52), channel_id=1, source_target_pairs={{0,192},{64,0},{128,64},{192,128},{1,193},{65,1},{129,65},{193,129... | collective-permute-start | bytes 393224 | tf_op jit(solution)/shard_map/ppermute | solution.py:411
  22.9 22.6 %collective-permute-start.2 = (bf16[128,512]{1,0:T(8,128)(2,1)S(1)}, bf16[128,512]{1,0:T(8,128)(2,1)S(1)}, u32[]{:S(2)}, u32[]{:S(2)}) collective-permute-start(bf16[128,512]{1,0:T(8,128)(2,1)S(1)} %get-tuple-element.53), channel_id=1, source_target_pairs={{0,128},{64,192},{128,0},{192,64},{1,129},{65,193},{129,1},{193,65... | collective-permute-start | bytes 393224 | tf_op jit(solution)/shard_map/ppermute | solution.py:411
  45.6 46.6 %copy-start.5 = (bf16[3,128,512]{2,1,0:T(8,128)(2,1)}, bf16[3,128,512]{2,1,0:T(8,128)(2,1)S(1)}, u32[]{:S(2)}) copy-start(bf16[3,128,512]{2,1,0:T(8,128)(2,1)S(1)} %pad_maximum_fusion.refs_8_) | copy-start | bytes 1179652
  45.6 46.6 %copy-start.7 = (bf16[1024,256]{1,0:T(8,128)(2,1)}, bf16[1024,256]{1,0:T(8,128)(2,1)S(1)}, u32[]{:S(2)}) copy-start(bf16[1024,256]{1,0:T(8,128)(2,1)S(1)} %collective-permute-done.5.refs_3_) | copy-start | bytes 1572868
  45.6 46.6 %copy-start.8 = (bf16[1024,256]{1,0:T(8,128)(2,1)}, bf16[1024,256]{1,0:T(8,128)(2,1)S(1)}, u32[]{:S(2)}) copy-start(bf16[1024,256]{1,0:T(8,128)(2,1)S(1)} %collective-permute-done.refs_1_) | copy-start | bytes 1572868
  45.6 1.0 copy-start.3
  53.7 45.7 %all-to-all-start.2 = ((bf16[16,32,1024]{2,1,0:T(8,128)(2,1)}), bf16[16,32,1024]{2,1,0:T(8,128)(2,1)S(1)}, u32[]{:S(2)}, u32[]{:S(2)}) async-start(bf16[16,32,1024]{2,1,0:T(8,128)(2,1)} %bitcast.15), calls=%async_computation.2 | async-start | bytes 2097152 | tf_op jit(solution)/shard_map/all_to_all | solution.py:445
  61.9 23.7 %collective-permute-start.4 = (bf16[1024,256]{1,0:T(8,128)(2,1)S(1)}, bf16[1024,256]{1,0:T(8,128)(2,1)S(1)}, u32[]{:S(2)}, u32[]{:S(2)}) collective-permute-start(bf16[1024,256]{1,0:T(8,128)(2,1)S(1)} %copy-done.6), channel_id=1, source_target_pairs={{0,32},{16,48},{32,0},{48,16},{1,33},{17,49},{33,1},{49,17},{2,34}... | collective-permute-start | bytes 1572872 | tf_op jit(solution)/shard_map/ppermute | solution.py:411
  64.8 10.2 %collective-permute-start.8 = (bf16[3,128,512]{2,1,0:T(8,128)(2,1)S(1)}, bf16[3,128,512]{2,1,0:T(8,128)(2,1)S(1)}, u32[]{:S(2)}, u32[]{:S(2)}) collective-permute-start(bf16[3,128,512]{2,1,0:T(8,128)(2,1)S(1)} %pad_maximum_fusion.refs_8_), channel_id=1, source_target_pairs={{0,2},{1,3},{2,0},{3,1},{4,6},{5,7},{6,4},{7,5},{8,10},{9,11},{10,... | collective-permute-start | bytes 1179656 | tf_op jit(solution)/shard_map/ppermute | solution.py:411
  67.7 17.4 %collective-permute-start.7 = (bf16[3,128,512]{2,1,0:T(8,128)(2,1)S(1)}, bf16[3,128,512]{2,1,0:T(8,128)(2,1)S(1)}, u32[]{:S(2)}, u32[]{:S(2)}) collective-permute-start(bf16[3,128,512]{2,1,0:T(8,128)(2,1)S(1)} %pad_maximum_fusion.refs_8_), channel_id=1, source_target_pairs={{0,3},{1,0},{2,1},{3,2},{4,7},{5,4},{6,5},{7,6},{8,11},{9,8},{10,9... | collective-permute-start | bytes 1179656 | tf_op jit(solution)/shard_map/ppermute | solution.py:411
  68.5 17.1 %collective-permute-start.6 = (bf16[3,128,512]{2,1,0:T(8,128)(2,1)S(1)}, bf16[3,128,512]{2,1,0:T(8,128)(2,1)S(1)}, u32[]{:S(2)}, u32[]{:S(2)}) collective-permute-start(bf16[3,128,512]{2,1,0:T(8,128)(2,1)S(1)} %pad_maximum_fusion.refs_8_), channel_id=1, source_target_pairs={{0,1},{1,2},{2,3},{3,0},{4,5},{5,6},{6,7},{7,4},{8,9},{9,10},{10,1... | collective-permute-start | bytes 1179656 | tf_op jit(solution)/shard_map/ppermute | solution.py:411
  75.0 10.6 %copy-start.13 = (bf16[3,128,512]{2,1,0:T(8,128)(2,1)}, bf16[3,128,512]{2,1,0:T(8,128)(2,1)S(1)}, u32[]{:S(2)}) copy-start(bf16[3,128,512]{2,1,0:T(8,128)(2,1)S(1)} %collective-permute-done.8.refs_10_) | copy-start | bytes 1179652
  85.1 0.8 copy-start.14
  85.6 0.7 copy-start.15
  85.8 6.4 %copy-start.9 = (bf16[1024,256]{1,0:T(8,128)(2,1)}, bf16[1024,256]{1,0:T(8,128)(2,1)S(1)}, u32[]{:S(2)}) copy-start(bf16[1024,256]{1,0:T(8,128)(2,1)S(1)} %collective-permute-done.4.refs_2_) | copy-start | bytes 1572868
  86.4 2.7 %collective-permute-start.9 = (bf16[1024,256]{1,0:T(8,128)(2,1)S(1)}, bf16[1024,256]{1,0:T(8,128)(2,1)S(1)}, u32[]{:S(2)}, u32[]{:S(2)}) collective-permute-start(bf16[1024,256]{1,0:T(8,128)(2,1)S(1)} %copy-done.6), channel_id=1, source_target_pairs={{0,8},{8,0},{1,9},{9,1},{2,10},{10,2},{3,11},{11,3},{4,12},{12,4},... | collective-permute-start | bytes 1572872 | tf_op jit(solution)/shard_map/ppermute | solution.py:411
  87.5 3.0 %collective-permute-start.10 = (bf16[1024,256]{1,0:T(8,128)(2,1)S(1)}, bf16[1024,256]{1,0:T(8,128)(2,1)S(1)}, u32[]{:S(2)}, u32[]{:S(2)}) collective-permute-start(bf16[1024,256]{1,0:T(8,128)(2,1)S(1)} %collective-permute-done.refs_1_), channel_id=1, source_target_pairs={{0,8},{8,0},{1,9},{9,1},{2,10},{10,2},{3,11},{11,3},{4,12},{12,4},... | collective-permute-start | bytes 1572872 | tf_op jit(solution)/shard_map/ppermute | solution.py:411
  87.5 3.8 %collective-permute-start.11 = (bf16[1024,256]{1,0:T(8,128)(2,1)S(1)}, bf16[1024,256]{1,0:T(8,128)(2,1)S(1)}, u32[]{:S(2)}, u32[]{:S(2)}) collective-permute-start(bf16[1024,256]{1,0:T(8,128)(2,1)S(1)} %collective-permute-done.4.refs_2_), channel_id=1, source_target_pairs={{0,8},{8,0},{1,9},{9,1},{2,10},{10,2},{3,11},{11,3},{4,12},{12,4},... | collective-permute-start | bytes 1572872 | tf_op jit(solution)/shard_map/ppermute | solution.py:411
  88.1 4.1 %collective-permute-start.12 = (bf16[1024,256]{1,0:T(8,128)(2,1)S(1)}, bf16[1024,256]{1,0:T(8,128)(2,1)}, u32[]{:S(2)}, u32[]{:S(2)}) collective-permute-start(bf16[1024,256]{1,0:T(8,128)(2,1)S(1)} %collective-permute-done.5.refs_3_), channel_id=1, source_target_pairs={{0,8},{8,0},{1,9},{9,1},{2,10},{10,2},{3,11},{11,3},{4,12},{12,4},... | collective-permute-start | bytes 1572872 | tf_op jit(solution)/shard_map/ppermute | solution.py:411
  89.1 2.3 %copy-start.10 = (bf16[1024,256]{1,0:T(8,128)(2,1)}, bf16[1024,256]{1,0:T(8,128)(2,1)S(1)}, u32[]{:S(2)}) copy-start(bf16[1024,256]{1,0:T(8,128)(2,1)S(1)} %collective-permute-done.9.refs_4_) | copy-start | bytes 1572868
  90.6 0.8 copy-start.11
  91.4 0.8 copy-start.12
  99.5 15.0 %copy-start = (bf16[16,32,1024]{2,1,0:T(8,128)(2,1)}, bf16[16,32,1024]{2,1,0:T(8,128)(2,1)S(1)}, u32[]{:S(2)}) copy-start(bf16[16,32,1024]{2,1,0:T(8,128)(2,1)S(1)} %all-to-all-done.2.mixed_near) | copy-start | bytes 3145732
  99.5 39.5 %all-to-all-start.1 = ((bf16[32,32,512]{2,1,0:T(8,128)(2,1)}), bf16[32,32,512]{2,1,0:T(8,128)(2,1)S(1)}, u32[]{:S(2)}, u32[]{:S(2)}) async-start(bf16[32,32,512]{2,1,0:T(8,128)(2,1)} %bitcast.14), calls=%async_computation.1 | async-start | bytes 2097152 | tf_op jit(solution)/shard_map/all_to_all | solution.py:417
  110.1 3.0 %collective-permute-start.14 = (bf16[4,4,128,256]{3,2,1,0:T(8,128)(2,1)}, bf16[4,4,128,256]{3,2,1,0:T(8,128)(2,1)S(1)}, u32[]{:S(2)}, u32[]{:S(2)}) collective-permute-start(bf16[4,4,128,256]{3,2,1,0:T(8,128)(2,1)} %get-tuple-element.40), channel_id=1, source_target_pairs={{0,8},{8,0},{1,9},{9,1},{2,10},{10,2},{3,11},{11,3},{4,12},{12,4},... | collective-permute-start | bytes 3145736 | tf_op jit(solution)/shard_map/ppermute | solution.py:411
  110.4 4.1 %collective-permute-start.13 = (bf16[16,32,1024]{2,1,0:T(8,128)(2,1)S(1)}, bf16[16,32,1024]{2,1,0:T(8,128)(2,1)}, u32[]{:S(2)}, u32[]{:S(2)}) collective-permute-start(bf16[16,32,1024]{2,1,0:T(8,128)(2,1)S(1)} %all-to-all-done.2.mixed_near), channel_id=1, source_target_pairs={{0,8},{8,0},{1,9},{9,1},{2,10},{10,2},{3,11},{11,3},{4,12},{12,4},... | collective-permute-start | bytes 3145736 | tf_op jit(solution)/shard_map/ppermute | solution.py:411
  113.0 1.4 copy-start.4
  119.3 21.4 %collective-permute-start.15 = (bf16[16,2,32,256]{3,2,1,0:T(8,128)(2,1)}, bf16[16,2,32,256]{3,2,1,0:T(8,128)(2,1)S(1)}, u32[]{:S(2)}, u32[]{:S(2)}) collective-permute-start(bf16[16,2,32,256]{3,2,1,0:T(8,128)(2,1)} %get-tuple-element.41), channel_id=1, source_target_pairs={{0,16},{16,32},{32,48},{48,0},{1,17},{17,33},{33,49},{49,1},{2,18}... | collective-permute-start | bytes 1572872 | tf_op jit(solution)/shard_map/ppermute | solution.py:411
  120.7 20.0 %collective-permute-start.16 = (bf16[16,2,32,256]{3,2,1,0:T(8,128)(2,1)}, bf16[16,2,32,256]{3,2,1,0:T(8,128)(2,1)S(1)}, u32[]{:S(2)}, u32[]{:S(2)}) collective-permute-start(bf16[16,2,32,256]{3,2,1,0:T(8,128)(2,1)} %get-tuple-element.42), channel_id=1, source_target_pairs={{0,48},{16,0},{32,16},{48,32},{1,49},{17,1},{33,17},{49,33},{2,50}... | collective-permute-start | bytes 1572872 | tf_op jit(solution)/shard_map/ppermute | solution.py:411
  138.9 1.8 copy-start.1
  148.1 34.2 %all-to-all-start.3 = ((bf16[32,3,32,128]{3,2,1,0:T(8,128)(2,1)}), bf16[32,3,32,128]{3,2,1,0:T(8,128)(2,1)S(1)}, u32[]{:S(2)}, u32[]{:S(2)}) async-start(bf16[32,3,32,128]{3,2,1,0:T(8,128)(2,1)} %corr.1), calls=%async_computation.3 | async-start | bytes 1572864 | tf_op jit(solution)/shard_map/all_to_all | solution.py:417
  156.2 23.7 %collective-permute-start.17 = (bf16[16,2,32,256]{3,2,1,0:T(8,128)(2,1)}, bf16[16,2,32,256]{3,2,1,0:T(8,128)(2,1)S(1)}, u32[]{:S(2)}, u32[]{:S(2)}) collective-permute-start(bf16[16,2,32,256]{3,2,1,0:T(8,128)(2,1)} %get-tuple-element.50), channel_id=1, source_target_pairs={{0,32},{16,48},{32,0},{48,16},{1,33},{17,49},{33,1},{49,17},{2,34}... | collective-permute-start | bytes 1572872 | tf_op jit(solution)/shard_map/ppermute | solution.py:411
  182.3 0.9 copy-start.2

commit v5 on v4

--- a/solution.py
+++ b/solution.py
@@ -14,7 +14,7 @@
 f32 = jnp.float32
 CTX = ("zh", "x", "core")
 TEN = ("zl", "y")
-VMEM_LIMIT = 60 * 1024 * 1024
+VMEM_LIMIT = 127 * 512 * 1024
 
 OUTER, INNER = 64, 128
 KEPT = OUTER // 2 + 1
@@ -363,7 +363,8 @@
     )(place, grad_out, *near_w, *far_w, *passed)
 
 
-def product_kernel(cols_ref, mixed_near, mixed_far, near, far, *outs):
+def product_kernel(extra, cols_ref, mixed_near, mixed_far, near, far, *refs):
+    adds, outs = refs[:extra], refs[extra:]
     my_core = cols_ref[4]
     owners, owned, depth = mixed_near.shape
     half = depth // 2
@@ -376,23 +377,26 @@
             [jnp.where(my_core == 0, own, other), jnp.where(my_core == 0, other, own)], 0
         )
         for core, rows in zip((my_core, 1 - my_core), lines):
-            product = dot(rows, columns).astype(out.dtype)
-            out[:, core] = product.reshape(owners, owned, product.shape[1])
-
-
-def product_call(cols, mixed_near, mixed_far, near, far, kinds):
+            product = dot(rows, columns)
+            product = product.reshape(owners, owned, product.shape[1])
+            for item in adds:
+                product = product + item[:, core].astype(f32)
+            out[:, core] = product.astype(out.dtype)
+
+
+def product_call(cols, mixed_near, mixed_far, near, far, adds, kinds):
     owners, owned, depth = mixed_near.shape
     width = near.shape[3]
     vmem = pl.BlockSpec(memory_space=pltpu.VMEM)
     return pl.pallas_call(
-        product_kernel,
-        in_specs=[pl.BlockSpec(memory_space=pltpu.SMEM)] + [vmem] * 4,
+        functools.partial(product_kernel, len(adds)),
+        in_specs=[pl.BlockSpec(memory_space=pltpu.SMEM)] + [vmem] * (4 + len(adds)),
         out_specs=[vmem] * len(kinds),
         out_shape=[jax.ShapeDtypeStruct((owners, 2, owned, width), kind) for kind in kinds],
         compiler_params=params(),
         cost_estimate=cost(4 * owners * owned * width * depth * len(kinds), 5),
         name="product",
-    )(cols, mixed_near, mixed_far, near, far)
+    )(cols, mixed_near, mixed_far, near, far, *adds)
 
 
 def shards(grad_out, out_weight, query_proj, key_proj, value_proj, filter_taps, skip_gain):
@@ -459,15 +463,16 @@
     cols = [(my_x + s) % 4 for s in (2, 1, 3, 0)]
     near_cols = jnp.stack(cols + [my_core]).astype(jnp.int32)
     last_cols = jnp.stack(cols[3:] * 4 + [my_core]).astype(jnp.int32)
-    sent = product_call(near_cols, mixed, mixed_far, near, far, (bf16,) * 3)
+    sent = product_call(near_cols, mixed, mixed_far, near, far, (), (bf16,) * 3)
     sent = {s: shift(item, "x", s) for s, item in zip((2, 1, 3), sent)}
     parts = after(parts, sent[1], sent[3])
     corr = corr_call(parts, fields, total, spec, skip_rows, table)
-    grad_weight = product_call(after(last_cols, corr), mixed, mixed_far, near, far, (f32,))[0]
+    grad_weight = product_call(
+        after(last_cols, corr), mixed, mixed_far, near, far, (sent[1], sent[3]), (f32,)
+    )[0]
     corr = to_all(corr)
     grad_key, grad_value, grad_filter, grad_query = last_call(corr, key_proj, value_proj)
-    for s in (1, 3, 2):
-        grad_weight = grad_weight + sent[s].astype(f32)
+    grad_weight = grad_weight + sent[2].astype(f32)
     grad_weight = (grad_weight * norm_scale).astype(bf16).reshape(group_width, width)
     return (grad_query, grad_key, grad_value, grad_filter, grad_weight)
 

time: 186 us -> 185 us (level)
  transfers between devices with their start and end apart: 22 -> 22, of which waited for: 13 -> 12; matrix products, arithmetic and copies ran while one was open for 3% -> 3% of each run, Pallas kernels for 9% -> 9%
where the time goes in v5:
time: 185 us; the launch traced here: 184 us
  waiting for transfers between devices  73.9 us (40%)
  starting transfers between devices  65.8 us (36%)
  Pallas kernels  35.2 us (19%)
  local copies, waits for them, and re-layouts  5.3 us (3%)
  other arithmetic  2.97 us (2%)
    ppermute x18, waiting for transfers between devices, shift(): return lax.ppermute(item, axis, [(n, (n + by) % size) for n in range(size)])  57 us
    all_to_all x3, starting transfers between devices, to_all(): return lax.all_to_all(item, CTX, split_axis=0, concat_axis=0, tiled=True)  30.7 us
    ppermute x18, starting transfers between devices, shift(): return lax.ppermute(item, axis, [(n, (n + by) % size) for n in range(size)])  26.7 us
    all_to_all x3, waiting for transfers between devices, to_all(): return lax.all_to_all(item, CTX, split_axis=0, concat_axis=0, tiled=True)  16.9 us
    pallas_call x2, Pallas kernels, product_call(): pl.pallas_call(functools.partial(product_kernel, len(adds)), in_specs=[pl...  9.01 us
    all_to_all x1, starting transfers between devices, shards(): lax.all_to_all(mixed.reshape(16, owned, 8 * tok_rows), ('zh', 'x'), split...  8.37 us
    pallas_call x1, Pallas kernels, corr_call(): pl.pallas_call(corr_kernel, grid=(steps,), in_specs=[pl.BlockSpec((blocks...  7.37 us
    pallas_call x1, Pallas kernels, mix_call(): pl.pallas_call(mix_kernel, in_specs=[pl.BlockSpec(memory_space=pltpu.SMEM...  7.19 us
  transfers between devices with their start and end apart: 22, of which 12 were waited for; matrix products, arithmetic and copies ran while one was open for 3% of the time, Pallas kernels for 9%

profile of v5, /device:TPU:1, one launch (start us, length us, event | category | flops | bytes accessed | tf_op | source)
XLA Modules:
  0.0 184.0 jit_solution(5960786721640457201)
XLA Ops:
  0.6 2.2 %prep.1 = bf16[32,3,32,128]{3,2,1,0:T(8,128)(2,1)} custom-call(bf16[128,1024]{1,0:T(8,128)(2,1)} %key_ref.3, bf16[128,1024]{1,0:T(8,128)(2,1)} %value_ref.3, bf16[128,1024]{1,0:T(8,128)(2,1)} %taps_ref.1, bf16[128,1024]{1,0:T(8,128)(2,1)} %query_ref.1), custom_call_target="tpu_custom_call" | custom-call | flops 10000000 | bytes 2097152 | tf_op jit(solution)/shard_map/prep/pallas_call | solution.py:245
  2.9 12.6 %all-to-all-start = ((bf16[32,3,32,128]{3,2,1,0:T(8,128)(2,1)}), bf16[32,3,32,128]{3,2,1,0:T(8,128)(2,1)}, u32[]{:S(2)}, u32[]{:S(2)}) async-start(bf16[32,3,32,128]{3,2,1,0:T(8,128)(2,1)} %prep.1), calls=%async_computation | async-start | bytes 1572864 | tf_op jit(solution)/shard_map/all_to_all | solution.py:421
  15.5 2.7 %collective-permute-start.5 = (bf16[1024,256]{1,0:T(8,128)(2,1)}, bf16[1024,256]{1,0:T(8,128)(2,1)}, u32[]{:S(2)}, u32[]{:S(2)}) collective-permute-start(bf16[1024,256]{1,0:T(8,128)(2,1)} %refs_0_), channel_id=1, source_target_pairs={{0,48},{16,0},{32,16},{48,32},{1,49},{17,1},{33,17},{49,33},{2,50}... | collective-permute-start | bytes 1572872 | tf_op jit(solution)/shard_map/ppermute | solution.py:415
  18.2 0.0 collective-permute-start
  18.2 1.1 constant_dynamic-slice_fusion.2
  19.2 2.2 %collective-permute-start.1 = (bf16[128,512]{1,0:T(8,128)(2,1)S(1)}, bf16[128,512]{1,0:T(8,128)(2,1)S(1)}, u32[]{:S(2)}, u32[]{:S(2)}) collective-permute-start(bf16[128,512]{1,0:T(8,128)(2,1)S(1)} %get-tuple-element.51), channel_id=1, source_target_pairs={{0,64},{64,128},{128,192},{192,0},{1,65},{65,129},{129,193},{193,1... | collective-permute-start | bytes 393224 | tf_op jit(solution)/shard_map/ppermute | solution.py:415
  21.4 1.5 collective-permute-start.3
  22.9 5.1 %collective-permute-start.2 = (bf16[128,512]{1,0:T(8,128)(2,1)S(1)}, bf16[128,512]{1,0:T(8,128)(2,1)S(1)}, u32[]{:S(2)}, u32[]{:S(2)}) collective-permute-start(bf16[128,512]{1,0:T(8,128)(2,1)S(1)} %get-tuple-element.53), channel_id=1, source_target_pairs={{0,128},{64,192},{128,0},{192,64},{1,129},{65,193},{129,1},{193,65... | collective-permute-start | bytes 393224 | tf_op jit(solution)/shard_map/ppermute | solution.py:415
  28.0 0.8 dynamic_slice.15
  28.8 0.6 pad_add_fusion.place_ref
  29.4 9.4 %collective-permute-done.1 = bf16[128,512]{1,0:T(8,128)(2,1)S(1)} collective-permute-done((bf16[128,512]{1,0:T(8,128)(2,1)S(1)}, bf16[128,512]{1,0:T(8,128)(2,1)S(1)}, u32[]{:S(2)}, u32[]{:S(2)}) %collective-permute-start.1) | collective-permute-done | bytes 131104 | tf_op jit(solution)/shard_map/ppermute | solution.py:415
  38.8 6.6 %collective-permute-done.3 = bf16[128,512]{1,0:T(8,128)(2,1)S(1)} collective-permute-done((bf16[128,512]{1,0:T(8,128)(2,1)S(1)}, bf16[128,512]{1,0:T(8,128)(2,1)S(1)}, u32[]{:S(2)}, u32[]{:S(2)}) %collective-permute-start.3) | collective-permute-done | bytes 131104 | tf_op jit(solution)/shard_map/ppermute | solution.py:415
  45.4 0.0 collective-permute-done.2
  45.5 0.0 copy-start
  45.5 0.0 collective-permute-done.5.refs_3_
  45.5 0.0 collective-permute-done.refs_1_
  45.5 0.0 all-to-all-done.fields_ref
  45.5 0.7 broadcast_in_dim.2.skip_ref
  46.2 7.1 %conv.1 = (f32[32,32,128]{2,1,0:T(8,128)}, f32[4,2,528,128]{3,2,1,0:T(8,128)}, bf16[4,4,32,1024]{3,2,1,0:T(8,128)(2,1)}) custom-call(bf16[32,3,32,128]{3,2,1,0:T(8,128)(2,1)} %all-to-all-done.fields_ref, f32[32,128]{1,0:T(8,128)} %broadcast_in_dim.2.skip_ref, f32[592,128]{1,0:T(8,128)} %constant.74.clone.table_ref), custom_call_target="tpu_custom_call" | custom-call | flops 1000000000 | bytes 6291456 | tf_op jit(solution)/shard_map/conv/pallas_call | solution.py:185
  53.3 8.4 %all-to-all-start.2 = ((bf16[16,32,1024]{2,1,0:T(8,128)(2,1)}), bf16[16,32,1024]{2,1,0:T(8,128)(2,1)}, u32[]{:S(2)}, u32[]{:S(2)}) async-start(bf16[16,32,1024]{2,1,0:T(8,128)(2,1)} %bitcast.15), calls=%async_computation.2 | async-start | bytes 2097152 | tf_op jit(solution)/shard_map/all_to_all | solution.py:449
  61.7 2.9 %collective-permute-start.4 = (bf16[1024,256]{1,0:T(8,128)(2,1)S(1)}, bf16[1024,256]{1,0:T(8,128)(2,1)S(1)}, u32[]{:S(2)}, u32[]{:S(2)}) collective-permute-start(bf16[1024,256]{1,0:T(8,128)(2,1)S(1)} %copy-done.2), channel_id=1, source_target_pairs={{0,32},{16,48},{32,0},{48,16},{1,33},{17,49},{33,1},{49,17},{2,34}... | collective-permute-start | bytes 1572872 | tf_op jit(solution)/shard_map/ppermute | solution.py:415
  64.6 2.9 %collective-permute-start.8 = (bf16[3,128,512]{2,1,0:T(8,128)(2,1)S(1)}, bf16[3,128,512]{2,1,0:T(8,128)(2,1)S(1)}, u32[]{:S(2)}, u32[]{:S(2)}) collective-permute-start(bf16[3,128,512]{2,1,0:T(8,128)(2,1)S(1)} %pad_maximum_fusion.refs_8_), channel_id=1, source_target_pairs={{0,2},{1,3},{2,0},{3,1},{4,6},{5,7},{6,4},{7,5},{8,10},{9,11},{10,... | collective-permute-start | bytes 1179656 | tf_op jit(solution)/shard_map/ppermute | solution.py:415
  67.6 0.8 collective-permute-start.7
  68.3 0.7 collective-permute-start.6
  69.0 5.9 %collective-permute-done.8.refs_10_ = bf16[3,128,512]{2,1,0:T(8,128)(2,1)S(1)} collective-permute-done((bf16[3,128,512]{2,1,0:T(8,128)(2,1)S(1)}, bf16[3,128,512]{2,1,0:T(8,128)(2,1)S(1)}, u32[]{:S(2)}, u32[]{:S(2)}) %collective-permute-start.8) | collective-permute-done | bytes 393248 | tf_op jit(solution)/shard_map/ppermute | solution.py:415
  74.9 10.0 %collective-permute-done.7.refs_11_ = bf16[3,128,512]{2,1,0:T(8,128)(2,1)S(1)} collective-permute-done((bf16[3,128,512]{2,1,0:T(8,128)(2,1)S(1)}, bf16[3,128,512]{2,1,0:T(8,128)(2,1)S(1)}, u32[]{:S(2)}, u32[]{:S(2)}) %collective-permute-start.7) | collective-permute-done | bytes 393248 | tf_op jit(solution)/shard_map/ppermute | solution.py:415
  84.9 0.5 collective-permute-done.6.refs_9_
  85.5 0.0 collective-permute-done.4.refs_2_
  85.5 1.1 collective-permute-start.9
  86.6 0.1 collective-permute-start.10
  86.7 0.4 collective-permute-start.11
  87.1 0.1 collective-permute-start.12
  87.2 0.9 collective-permute-done.9.refs_4_
  88.1 2.5 %collective-permute-done.10.refs_5_ = bf16[1024,256]{1,0:T(8,128)(2,1)S(1)} collective-permute-done((bf16[1024,256]{1,0:T(8,128)(2,1)}, bf16[1024,256]{1,0:T(8,128)(2,1)S(1)}, u32[]{:S(2)}, u32[]{:S(2)}) %collective-permute-start.10) | collective-permute-done | bytes 524320 | tf_op jit(solution)/shard_map/ppermute | solution.py:415
  90.6 0.0 collective-permute-done.11.refs_6_
  90.6 0.0 copy-done.7
  90.6 0.8 copy-done.5
  91.4 0.8 copy-done.6
  92.2 0.0 collective-permute-done.12.refs_7_
  92.2 7.2 %mix.1 = (bf16[1024,512]{1,0:T(8,128)(2,1)}, bf16[4,4,128,256]{3,2,1,0:T(8,128)(2,1)}, bf16[4,4,128,256]{3,2,1,0:T(8,128)(2,1)}) custom-call(s32[4]{0:T(128)} %pad_add_fusion.place_ref, bf16[128,8192]{1,0:T(8,128)(2,1)} %grad_out_ref.1, bf16[1024,256]{1,0:T(8,128)(2,1)} %refs_0_, bf16[1024,256]{1,0:T(8,128)(2,1)} %collective-permute-done.refs_1_, ...), custom_call_target="tpu_custom_call" | custom-call | flops 2147483648 | bytes 9437184 | tf_op jit(solution)/shard_map/mix/pallas_call | solution.py:349
  99.4 0.0 copy-start.1
  99.4 0.0 all-to-all-done.2.mixed_near
  99.4 10.4 %all-to-all-start.1 = ((bf16[32,32,512]{2,1,0:T(8,128)(2,1)}), bf16[32,32,512]{2,1,0:T(8,128)(2,1)}, u32[]{:S(2)}, u32[]{:S(2)}) async-start(bf16[32,32,512]{2,1,0:T(8,128)(2,1)} %bitcast.14), calls=%async_computation.1 | async-start | bytes 2097152 | tf_op jit(solution)/shard_map/all_to_all | solution.py:421
  109.8 0.0 copy-done.1
  109.8 0.4 collective-permute-start.14
  110.2 0.2 collective-permute-start.13
  110.4 0.6 stack.64.cols_ref
  111.1 1.7 collective-permute-done.14.far
  112.7 1.7 collective-permute-done.13.mixed_far
  114.4 4.8 %product.2 = (bf16[16,2,32,256]{3,2,1,0:T(8,128)(2,1)}, bf16[16,2,32,256]{3,2,1,0:T(8,128)(2,1)}, bf16[16,2,32,256]{3,2,1,0:T(8,128)(2,1)}) custom-call(s32[5]{0:T(128)} %stack.64.cols_ref, bf16[16,32,1024]{2,1,0:T(8,128)(2,1)} %all-to-all-done.2.mixed_near, bf16[16,32,1024]{2,1,0:T(8,128)(2,1)} %collective-permute-done.13.mixed_far, ...), custom_call_target="tpu_custom_call" | custom-call | flops 1610612736 | bytes 5242880 | tf_op jit(solution)/shard_map/product/pallas_call | solution.py:391
  119.3 1.4 collective-permute-start.15
  120.7 1.3 collective-permute-start.16
  121.9 16.9 %all-to-all-done.1.parts_ref = bf16[32,32,512]{2,1,0:T(8,128)(2,1)} async-done(((bf16[32,32,512]{2,1,0:T(8,128)(2,1)}), bf16[32,32,512]{2,1,0:T(8,128)(2,1)}, u32[]{:S(2)}, u32[]{:S(2)}) %all-to-all-start.1) | async-done | bytes 1048608 | tf_op jit(solution)/shard_map/all_to_all | solution.py:421
  138.8 1.9 %collective-permute-done.15.refs_0_ = bf16[16,2,32,256]{3,2,1,0:T(8,128)(2,1)} collective-permute-done((bf16[16,2,32,256]{3,2,1,0:T(8,128)(2,1)}, bf16[16,2,32,256]{3,2,1,0:T(8,128)(2,1)}, u32[]{:S(2)}, u32[]{:S(2)}) %collective-permute-start.15) | collective-permute-done | bytes 524320 | tf_op jit(solution)/shard_map/ppermute | solution.py:415
  140.7 0.0 collective-permute-done.16.refs_1_
  140.7 7.4 %corr.1 = bf16[32,3,32,128]{3,2,1,0:T(8,128)(2,1)} custom-call(bf16[32,32,512]{2,1,0:T(8,128)(2,1)} %all-to-all-done.1.parts_ref, bf16[32,3,32,128]{3,2,1,0:T(8,128)(2,1)} %all-to-all-done.fields_ref, f32[32,32,128]{2,1,0:T(8,128)} %get-tuple-element.32.total_ref, f32[4,2,528,128]{3,2,1,0:T(8,128)} %get-tuple-element.44.spec_ref, ...), custom_call_target="tpu_custom_call" | custom-call | flops 1000000000 | bytes 6291456 | tf_op jit(solution)/shard_map/corr/pallas_call | solution.py:213
  148.1 7.7 %all-to-all-start.3 = ((bf16[32,3,32,128]{3,2,1,0:T(8,128)(2,1)}), bf16[32,3,32,128]{3,2,1,0:T(8,128)(2,1)}, u32[]{:S(2)}, u32[]{:S(2)}) async-start(bf16[32,3,32,128]{3,2,1,0:T(8,128)(2,1)} %corr.1), calls=%async_computation.3 | async-start | bytes 1572864 | tf_op jit(solution)/shard_map/all_to_all | solution.py:421
  155.8 3.0 %collective-permute-start.17 = (bf16[16,2,32,256]{3,2,1,0:T(8,128)(2,1)}, bf16[16,2,32,256]{3,2,1,0:T(8,128)(2,1)}, u32[]{:S(2)}, u32[]{:S(2)}) collective-permute-start(bf16[16,2,32,256]{3,2,1,0:T(8,128)(2,1)} %get-tuple-element.50), channel_id=1, source_target_pairs={{0,32},{16,48},{32,0},{48,16},{1,33},{17,49},{33,1},{49,17},{2,34}... | collective-permute-start | bytes 1572872 | tf_op jit(solution)/shard_map/ppermute | solution.py:415
  158.7 0.6 stack.65.cols_ref
  159.3 4.2 %product.3 = f32[16,2,32,256]{3,2,1,0:T(8,128)} custom-call(s32[5]{0:T(128)} %stack.65.cols_ref, bf16[16,32,1024]{2,1,0:T(8,128)(2,1)} %all-to-all-done.2.mixed_near, bf16[16,32,1024]{2,1,0:T(8,128)(2,1)} %collective-permute-done.13.mixed_far, bf16[4,4,128,256]{3,2,1,0:T(8,128)(2,1)} %get-tuple-element.39.near, ...), custom_call_target="tpu_custom_call" | custom-call | flops 536870912 | bytes 5242880 | tf_op jit(solution)/shard_map/product/pallas_call | solution.py:391
  163.5 15.9 %collective-permute-done.17 = bf16[16,2,32,256]{3,2,1,0:T(8,128)(2,1)} collective-permute-done((bf16[16,2,32,256]{3,2,1,0:T(8,128)(2,1)}, bf16[16,2,32,256]{3,2,1,0:T(8,128)(2,1)}, u32[]{:S(2)}, u32[]{:S(2)}) %collective-permute-start.17) | collective-permute-done | bytes 524320 | tf_op jit(solution)/shard_map/ppermute | solution.py:415
  179.4 2.3 %multiply_convert_fusion = bf16[16,2,32,256]{3,2,1,0:T(8,128)(2,1)} fusion(f32[16,2,32,256]{3,2,1,0:T(8,128)} %product.3, bf16[16,2,32,256]{3,2,1,0:T(8,128)(2,1)} %collective-permute-done.17), kind=kLoop, calls=%fused_computation | loop fusion | flops 1048576 | bytes 2097152 | tf_op jit(solution)/shard_map/convert_element_type | solution.py:476
  181.7 0.0 all-to-all-done.3.corr_ref
  181.7 2.2 %last.1 = (bf16[128,1024]{1,0:T(8,128)(2,1)}, bf16[128,1024]{1,0:T(8,128)(2,1)}, bf16[128,1024]{1,0:T(8,128)(2,1)}, bf16[128,1024]{1,0:T(8,128)(2,1)}) custom-call(bf16[32,3,32,128]{3,2,1,0:T(8,128)(2,1)} %all-to-all-done.3.corr_ref, bf16[128,1024]{1,0:T(8,128)(2,1)} %key_ref.3, bf16[128,1024]{1,0:T(8,128)(2,1)} %value_ref.3), custom_call_target="tpu_custom_call" | custom-call | flops 10000000 | bytes 3145728 | tf_op jit(solution)/shard_map/last/pallas_call | solution.py:275
  (15 shorter events, 0.1 us)
Async XLA Ops:
  2.9 42.6 %all-to-all-start = ((bf16[32,3,32,128]{3,2,1,0:T(8,128)(2,1)}), bf16[32,3,32,128]{3,2,1,0:T(8,128)(2,1)}, u32[]{:S(2)}, u32[]{:S(2)}) async-start(bf16[32,3,32,128]{3,2,1,0:T(8,128)(2,1)} %prep.1), calls=%async_computation | async-start | bytes 1572864 | tf_op jit(solution)/shard_map/all_to_all | solution.py:421
  15.5 30.0 %collective-permute-start.5 = (bf16[1024,256]{1,0:T(8,128)(2,1)}, bf16[1024,256]{1,0:T(8,128)(2,1)}, u32[]{:S(2)}, u32[]{:S(2)}) collective-permute-start(bf16[1024,256]{1,0:T(8,128)(2,1)} %refs_0_), channel_id=1, source_target_pairs={{0,48},{16,0},{32,16},{48,32},{1,49},{17,1},{33,17},{49,33},{2,50}... | collective-permute-start | bytes 1572872 | tf_op jit(solution)/shard_map/ppermute | solution.py:415
  18.2 27.3 %collective-permute-start = (bf16[1024,256]{1,0:T(8,128)(2,1)}, bf16[1024,256]{1,0:T(8,128)(2,1)}, u32[]{:S(2)}, u32[]{:S(2)}) collective-permute-start(bf16[1024,256]{1,0:T(8,128)(2,1)} %refs_0_), channel_id=1, source_target_pairs={{0,16},{16,32},{32,48},{48,0},{1,17},{17,33},{33,49},{49,1},{2,18}... | collective-permute-start | bytes 1572872 | tf_op jit(solution)/shard_map/ppermute | solution.py:415
  19.2 19.5 %collective-permute-start.1 = (bf16[128,512]{1,0:T(8,128)(2,1)S(1)}, bf16[128,512]{1,0:T(8,128)(2,1)S(1)}, u32[]{:S(2)}, u32[]{:S(2)}) collective-permute-start(bf16[128,512]{1,0:T(8,128)(2,1)S(1)} %get-tuple-element.51), channel_id=1, source_target_pairs={{0,64},{64,128},{128,192},{192,0},{1,65},{65,129},{129,193},{193,1... | collective-permute-start | bytes 393224 | tf_op jit(solution)/shard_map/ppermute | solution.py:415
  21.4 24.0 %collective-permute-start.3 = (bf16[128,512]{1,0:T(8,128)(2,1)S(1)}, bf16[128,512]{1,0:T(8,128)(2,1)S(1)}, u32[]{:S(2)}, u32[]{:S(2)}) collective-permute-start(bf16[128,512]{1,0:T(8,128)(2,1)S(1)} %get-tuple-element.52), channel_id=1, source_target_pairs={{0,192},{64,0},{128,64},{192,128},{1,193},{65,1},{129,65},{193,129... | collective-permute-start | bytes 393224 | tf_op jit(solution)/shard_map/ppermute | solution.py:415
  22.9 22.5 %collective-permute-start.2 = (bf16[128,512]{1,0:T(8,128)(2,1)S(1)}, bf16[128,512]{1,0:T(8,128)(2,1)S(1)}, u32[]{:S(2)}, u32[]{:S(2)}) collective-permute-start(bf16[128,512]{1,0:T(8,128)(2,1)S(1)} %get-tuple-element.53), channel_id=1, source_target_pairs={{0,128},{64,192},{128,0},{192,64},{1,129},{65,193},{129,1},{193,65... | collective-permute-start | bytes 393224 | tf_op jit(solution)/shard_map/ppermute | solution.py:415
  45.5 22.9 %copy-start = (bf16[3,128,512]{2,1,0:T(8,128)(2,1)}, bf16[3,128,512]{2,1,0:T(8,128)(2,1)S(1)}, u32[]{:S(2)}) copy-start(bf16[3,128,512]{2,1,0:T(8,128)(2,1)S(1)} %pad_maximum_fusion.refs_8_) | copy-start | bytes 1179652
  53.3 8.4 %copy-start.2 = (bf16[1024,256]{1,0:T(8,128)(2,1)S(1)}, bf16[1024,256]{1,0:T(8,128)(2,1)}, u32[]{:S(2)}) copy-start(bf16[1024,256]{1,0:T(8,128)(2,1)} %refs_0_) | copy-start | bytes 1572868
  53.3 46.0 %all-to-all-start.2 = ((bf16[16,32,1024]{2,1,0:T(8,128)(2,1)}), bf16[16,32,1024]{2,1,0:T(8,128)(2,1)}, u32[]{:S(2)}, u32[]{:S(2)}) async-start(bf16[16,32,1024]{2,1,0:T(8,128)(2,1)} %bitcast.15), calls=%async_computation.2 | async-start | bytes 2097152 | tf_op jit(solution)/shard_map/all_to_all | solution.py:449
  61.7 23.7 %collective-permute-start.4 = (bf16[1024,256]{1,0:T(8,128)(2,1)S(1)}, bf16[1024,256]{1,0:T(8,128)(2,1)S(1)}, u32[]{:S(2)}, u32[]{:S(2)}) collective-permute-start(bf16[1024,256]{1,0:T(8,128)(2,1)S(1)} %copy-done.2), channel_id=1, source_target_pairs={{0,32},{16,48},{32,0},{48,16},{1,33},{17,49},{33,1},{49,17},{2,34}... | collective-permute-start | bytes 1572872 | tf_op jit(solution)/shard_map/ppermute | solution.py:415
  64.6 10.3 %collective-permute-start.8 = (bf16[3,128,512]{2,1,0:T(8,128)(2,1)S(1)}, bf16[3,128,512]{2,1,0:T(8,128)(2,1)S(1)}, u32[]{:S(2)}, u32[]{:S(2)}) collective-permute-start(bf16[3,128,512]{2,1,0:T(8,128)(2,1)S(1)} %pad_maximum_fusion.refs_8_), channel_id=1, source_target_pairs={{0,2},{1,3},{2,0},{3,1},{4,6},{5,7},{6,4},{7,5},{8,10},{9,11},{10,... | collective-permute-start | bytes 1179656 | tf_op jit(solution)/shard_map/ppermute | solution.py:415
  67.6 17.4 %collective-permute-start.7 = (bf16[3,128,512]{2,1,0:T(8,128)(2,1)S(1)}, bf16[3,128,512]{2,1,0:T(8,128)(2,1)S(1)}, u32[]{:S(2)}, u32[]{:S(2)}) collective-permute-start(bf16[3,128,512]{2,1,0:T(8,128)(2,1)S(1)} %pad_maximum_fusion.refs_8_), channel_id=1, source_target_pairs={{0,3},{1,0},{2,1},{3,2},{4,7},{5,4},{6,5},{7,6},{8,11},{9,8},{10,9... | collective-permute-start | bytes 1179656 | tf_op jit(solution)/shard_map/ppermute | solution.py:415
  68.3 17.1 %collective-permute-start.6 = (bf16[3,128,512]{2,1,0:T(8,128)(2,1)S(1)}, bf16[3,128,512]{2,1,0:T(8,128)(2,1)S(1)}, u32[]{:S(2)}, u32[]{:S(2)}) collective-permute-start(bf16[3,128,512]{2,1,0:T(8,128)(2,1)S(1)} %pad_maximum_fusion.refs_8_), channel_id=1, source_target_pairs={{0,1},{1,2},{2,3},{3,0},{4,5},{5,6},{6,7},{7,4},{8,9},{9,10},{10,1... | collective-permute-start | bytes 1179656 | tf_op jit(solution)/shard_map/ppermute | solution.py:415
  74.9 15.7 %copy-start.7 = (bf16[3,128,512]{2,1,0:T(8,128)(2,1)}, bf16[3,128,512]{2,1,0:T(8,128)(2,1)S(1)}, u32[]{:S(2)}) copy-start(bf16[3,128,512]{2,1,0:T(8,128)(2,1)S(1)} %collective-permute-done.8.refs_10_) | copy-start | bytes 1179652
  84.9 5.7 %copy-start.8 = (bf16[3,128,512]{2,1,0:T(8,128)(2,1)}, bf16[3,128,512]{2,1,0:T(8,128)(2,1)S(1)}, u32[]{:S(2)}) copy-start(bf16[3,128,512]{2,1,0:T(8,128)(2,1)S(1)} %collective-permute-done.7.refs_11_) | copy-start | bytes 1179652
  85.4 5.2 %copy-start.9 = (bf16[3,128,512]{2,1,0:T(8,128)(2,1)}, bf16[3,128,512]{2,1,0:T(8,128)(2,1)S(1)}, u32[]{:S(2)}) copy-start(bf16[3,128,512]{2,1,0:T(8,128)(2,1)S(1)} %collective-permute-done.6.refs_9_) | copy-start | bytes 1179652
  85.5 2.7 %copy-start.3 = (bf16[1024,256]{1,0:T(8,128)(2,1)}, bf16[1024,256]{1,0:T(8,128)(2,1)S(1)}, u32[]{:S(2)}) copy-start(bf16[1024,256]{1,0:T(8,128)(2,1)S(1)} %collective-permute-done.4.refs_2_) | copy-start | bytes 1572868
  85.5 2.7 %collective-permute-start.9 = (bf16[1024,256]{1,0:T(8,128)(2,1)S(1)}, bf16[1024,256]{1,0:T(8,128)(2,1)S(1)}, u32[]{:S(2)}, u32[]{:S(2)}) collective-permute-start(bf16[1024,256]{1,0:T(8,128)(2,1)S(1)} %copy-done.2), channel_id=1, source_target_pairs={{0,8},{8,0},{1,9},{9,1},{2,10},{10,2},{3,11},{11,3},{4,12},{12,4},... | collective-permute-start | bytes 1572872 | tf_op jit(solution)/shard_map/ppermute | solution.py:415
  86.6 4.0 %collective-permute-start.10 = (bf16[1024,256]{1,0:T(8,128)(2,1)}, bf16[1024,256]{1,0:T(8,128)(2,1)S(1)}, u32[]{:S(2)}, u32[]{:S(2)}) collective-permute-start(bf16[1024,256]{1,0:T(8,128)(2,1)} %collective-permute-done.refs_1_), channel_id=1, source_target_pairs={{0,8},{8,0},{1,9},{9,1},{2,10},{10,2},{3,11},{11,3},{4,12},{12,4},... | collective-permute-start | bytes 1572872 | tf_op jit(solution)/shard_map/ppermute | solution.py:415
  86.7 3.9 %collective-permute-start.11 = (bf16[1024,256]{1,0:T(8,128)(2,1)S(1)}, bf16[1024,256]{1,0:T(8,128)(2,1)S(1)}, u32[]{:S(2)}, u32[]{:S(2)}) collective-permute-start(bf16[1024,256]{1,0:T(8,128)(2,1)S(1)} %collective-permute-done.4.refs_2_), channel_id=1, source_target_pairs={{0,8},{8,0},{1,9},{9,1},{2,10},{10,2},{3,11},{11,3},{4,12},{12,4},... | collective-permute-start | bytes 1572872 | tf_op jit(solution)/shard_map/ppermute | solution.py:415
  87.1 5.1 %collective-permute-start.12 = (bf16[1024,256]{1,0:T(8,128)(2,1)}, bf16[1024,256]{1,0:T(8,128)(2,1)}, u32[]{:S(2)}, u32[]{:S(2)}) collective-permute-start(bf16[1024,256]{1,0:T(8,128)(2,1)} %collective-permute-done.5.refs_3_), channel_id=1, source_target_pairs={{0,8},{8,0},{1,9},{9,1},{2,10},{10,2},{3,11},{11,3},{4,12},{12,4},... | collective-permute-start | bytes 1572872 | tf_op jit(solution)/shard_map/ppermute | solution.py:415
  88.1 2.5 %copy-start.4 = (bf16[1024,256]{1,0:T(8,128)(2,1)}, bf16[1024,256]{1,0:T(8,128)(2,1)S(1)}, u32[]{:S(2)}) copy-start(bf16[1024,256]{1,0:T(8,128)(2,1)S(1)} %collective-permute-done.9.refs_4_) | copy-start | bytes 1572868
  90.6 0.8 copy-start.5
  91.4 0.8 copy-start.6
  99.4 10.5 %copy-start.1 = (bf16[4,4,128,256]{3,2,1,0:T(8,128)(2,1)S(1)}, bf16[4,4,128,256]{3,2,1,0:T(8,128)(2,1)}, u32[]{:S(2)}) copy-start(bf16[4,4,128,256]{3,2,1,0:T(8,128)(2,1)} %get-tuple-element.40) | copy-start | bytes 3145732
  99.4 39.4 %all-to-all-start.1 = ((bf16[32,32,512]{2,1,0:T(8,128)(2,1)}), bf16[32,32,512]{2,1,0:T(8,128)(2,1)}, u32[]{:S(2)}, u32[]{:S(2)}) async-start(bf16[32,32,512]{2,1,0:T(8,128)(2,1)} %bitcast.14), calls=%async_computation.1 | async-start | bytes 2097152 | tf_op jit(solution)/shard_map/all_to_all | solution.py:421
  109.8 2.9 %collective-permute-start.14 = (bf16[4,4,128,256]{3,2,1,0:T(8,128)(2,1)S(1)}, bf16[4,4,128,256]{3,2,1,0:T(8,128)(2,1)}, u32[]{:S(2)}, u32[]{:S(2)}) collective-permute-start(bf16[4,4,128,256]{3,2,1,0:T(8,128)(2,1)S(1)} %copy-done.1), channel_id=1, source_target_pairs={{0,8},{8,0},{1,9},{9,1},{2,10},{10,2},{3,11},{11,3},{4,12},{12,4},... | collective-permute-start | bytes 3145736 | tf_op jit(solution)/shard_map/ppermute | solution.py:415
  110.2 4.2 %collective-permute-start.13 = (bf16[16,32,1024]{2,1,0:T(8,128)(2,1)}, bf16[16,32,1024]{2,1,0:T(8,128)(2,1)}, u32[]{:S(2)}, u32[]{:S(2)}) collective-permute-start(bf16[16,32,1024]{2,1,0:T(8,128)(2,1)} %all-to-all-done.2.mixed_near), channel_id=1, source_target_pairs={{0,8},{8,0},{1,9},{9,1},{2,10},{10,2},{3,11},{11,3},{4,12},{12,4},... | collective-permute-start | bytes 3145736 | tf_op jit(solution)/shard_map/ppermute | solution.py:415
  119.3 21.5 %collective-permute-start.15 = (bf16[16,2,32,256]{3,2,1,0:T(8,128)(2,1)}, bf16[16,2,32,256]{3,2,1,0:T(8,128)(2,1)}, u32[]{:S(2)}, u32[]{:S(2)}) collective-permute-start(bf16[16,2,32,256]{3,2,1,0:T(8,128)(2,1)} %get-tuple-element.41), channel_id=1, source_target_pairs={{0,16},{16,32},{32,48},{48,0},{1,17},{17,33},{33,49},{49,1},{2,18}... | collective-permute-start | bytes 1572872 | tf_op jit(solution)/shard_map/ppermute | solution.py:415
  120.7 20.1 %collective-permute-start.16 = (bf16[16,2,32,256]{3,2,1,0:T(8,128)(2,1)}, bf16[16,2,32,256]{3,2,1,0:T(8,128)(2,1)}, u32[]{:S(2)}, u32[]{:S(2)}) collective-permute-start(bf16[16,2,32,256]{3,2,1,0:T(8,128)(2,1)} %get-tuple-element.42), channel_id=1, source_target_pairs={{0,48},{16,0},{32,16},{48,32},{1,49},{17,1},{33,17},{49,33},{2,50}... | collective-permute-start | bytes 1572872 | tf_op jit(solution)/shard_map/ppermute | solution.py:415
  148.1 33.6 %all-to-all-start.3 = ((bf16[32,3,32,128]{3,2,1,0:T(8,128)(2,1)}), bf16[32,3,32,128]{3,2,1,0:T(8,128)(2,1)}, u32[]{:S(2)}, u32[]{:S(2)}) async-start(bf16[32,3,32,128]{3,2,1,0:T(8,128)(2,1)} %corr.1), calls=%async_computation.3 | async-start | bytes 1572864 | tf_op jit(solution)/shard_map/all_to_all | solution.py:421
  155.8 23.6 %collective-permute-start.17 = (bf16[16,2,32,256]{3,2,1,0:T(8,128)(2,1)}, bf16[16,2,32,256]{3,2,1,0:T(8,128)(2,1)}, u32[]{:S(2)}, u32[]{:S(2)}) collective-permute-start(bf16[16,2,32,256]{3,2,1,0:T(8,128)(2,1)} %get-tuple-element.50), channel_id=1, source_target_pairs={{0,32},{16,48},{32,0},{48,16},{1,33},{17,49},{33,1},{49,17},{2,34}... | collective-permute-start | bytes 1572872 | tf_op jit(solution)/shard_map/ppermute | solution.py:415

commit v6 on v5

--- a/solution.py
+++ b/solution.py
@@ -439,7 +439,9 @@
         passed[s] = shift(lax.dynamic_slice_in_dim(grad_late, start, 2 * width, 1), "zh", s)
         if s != 2:
             near_w[s] = shift(weight_late, "x", s)
-    passed = {0: jnp.stack([passed[s] for s in range(1, 4)])}
+    held = lax.optimization_barrier((*(passed[s] for s in range(1, 4)), skip_rows))
+    skip_rows = held[3]
+    passed = {0: jnp.stack(held[:3])}
     near_w[2] = shift(after(out_weight, passed[0]), "x", 2)
     for s in order:
         passed[s] = shift(passed[0], "y", s)

time: 185 us -> 185 us (level)
  waiting for transfers between devices: 73.9 us -> 78.3 us
  starting transfers between devices: 65.8 us -> 62.7 us
    ppermute x18, waiting for transfers between devices: 57 us -> 61.5 us  [shift(): return lax.ppermute(item, axis, [(n, (n + by) % size) for n in range(size)])]
    all_to_all x3, starting transfers between devices: 30.7 us -> 28.6 us  [to_all(): return lax.all_to_all(item, CTX, split_axis=0, concat_axis=0, tiled=True)]
  transfers between devices with their start and end apart: 22 -> 22, of which waited for: 12 -> 14; matrix products, arithmetic and copies ran while one was open for 3% -> 4% of each run, Pallas kernels for 9% -> 9%
where the time goes in v6:
time: 185 us
  waiting for transfers between devices  78.3 us (42%)
  starting transfers between devices  62.7 us (34%)
  Pallas kernels  35.3 us (19%)
  local copies, waits for them, and re-layouts  4.63 us (3%)
  other arithmetic  2.97 us (2%)
    ppermute x18, waiting for transfers between devices, shift(): return lax.ppermute(item, axis, [(n, (n + by) % size) for n in range(size)])  61.5 us
    all_to_all x3, starting transfers between devices, to_all(): return lax.all_to_all(item, CTX, split_axis=0, concat_axis=0, tiled=True)  28.6 us
    ppermute x18, starting transfers between devices, shift(): return lax.ppermute(item, axis, [(n, (n + by) % size) for n in range(size)])  26.7 us
    all_to_all x3, waiting for transfers between devices, to_all(): return lax.all_to_all(item, CTX, split_axis=0, concat_axis=0, tiled=True)  16.8 us
    pallas_call x2, Pallas kernels, product_call(): pl.pallas_call(functools.partial(product_kernel, len(adds)), in_specs=[pl...  9.01 us
    pallas_call x1, Pallas kernels, corr_call(): pl.pallas_call(corr_kernel, grid=(steps,), in_specs=[pl.BlockSpec((blocks...  7.37 us
    all_to_all x1, starting transfers between devices, shards(): lax.all_to_all(mixed.reshape(16, owned, 8 * tok_rows), ('zh', 'x'), split...  7.33 us
    pallas_call x1, Pallas kernels, conv_call(): pl.pallas_call(conv_kernel, grid=(steps,), in_specs=[pl.BlockSpec((blocks...  7.25 us
  transfers between devices with their start and end apart: 22, of which 14 were waited for; matrix products, arithmetic and copies ran while one was open for 4% of the time, Pallas kernels for 9%

profile of v6, /device:TPU:1, one launch (start us, length us, event | category | flops | bytes accessed | tf_op | source)
XLA Modules:
  0.0 184.7 jit_solution(16680606791468408873)
XLA Ops:
  0.6 2.2 %prep.1 = bf16[32,3,32,128]{3,2,1,0:T(8,128)(2,1)} custom-call(bf16[128,1024]{1,0:T(8,128)(2,1)} %key_ref.3, bf16[128,1024]{1,0:T(8,128)(2,1)} %value_ref.3, bf16[128,1024]{1,0:T(8,128)(2,1)} %taps_ref.1, bf16[128,1024]{1,0:T(8,128)(2,1)} %query_ref.1), custom_call_target="tpu_custom_call" | custom-call | flops 10000000 | bytes 2097152 | tf_op jit(solution)/shard_map/prep/pallas_call | solution.py:245
  2.9 12.6 %all-to-all-start = ((bf16[32,3,32,128]{3,2,1,0:T(8,128)(2,1)}), bf16[32,3,32,128]{3,2,1,0:T(8,128)(2,1)}, u32[]{:S(2)}, u32[]{:S(2)}) async-start(bf16[32,3,32,128]{3,2,1,0:T(8,128)(2,1)} %prep.1), calls=%async_computation | async-start | bytes 1572864 | tf_op jit(solution)/shard_map/all_to_all | solution.py:421
  15.5 2.7 %collective-permute-start.5 = (bf16[1024,256]{1,0:T(8,128)(2,1)}, bf16[1024,256]{1,0:T(8,128)(2,1)}, u32[]{:S(2)}, u32[]{:S(2)}) collective-permute-start(bf16[1024,256]{1,0:T(8,128)(2,1)} %refs_0_), channel_id=1, source_target_pairs={{0,48},{16,0},{32,16},{48,32},{1,49},{17,1},{33,17},{49,33},{2,50}... | collective-permute-start | bytes 1572872 | tf_op jit(solution)/shard_map/ppermute | solution.py:415
  18.2 0.0 collective-permute-start
  18.2 1.1 constant_dynamic-slice_fusion
  19.2 3.5 %collective-permute-start.3 = (bf16[128,512]{1,0:T(8,128)(2,1)S(1)}, bf16[128,512]{1,0:T(8,128)(2,1)S(1)}, u32[]{:S(2)}, u32[]{:S(2)}) collective-permute-start(bf16[128,512]{1,0:T(8,128)(2,1)S(1)} %get-tuple-element.59), channel_id=1, source_target_pairs={{0,192},{64,0},{128,64},{192,128},{1,193},{65,1},{129,65},{193,129... | collective-permute-start | bytes 393224 | tf_op jit(solution)/shard_map/ppermute | solution.py:415
  22.7 2.0 %collective-permute-start.2 = (bf16[128,512]{1,0:T(8,128)(2,1)S(1)}, bf16[128,512]{1,0:T(8,128)(2,1)S(1)}, u32[]{:S(2)}, u32[]{:S(2)}) collective-permute-start(bf16[128,512]{1,0:T(8,128)(2,1)S(1)} %get-tuple-element.60), channel_id=1, source_target_pairs={{0,128},{64,192},{128,0},{192,64},{1,129},{65,193},{129,1},{193,65... | collective-permute-start | bytes 393224 | tf_op jit(solution)/shard_map/ppermute | solution.py:415
  24.7 2.1 %collective-permute-start.1 = (bf16[128,512]{1,0:T(8,128)(2,1)S(1)}, bf16[128,512]{1,0:T(8,128)(2,1)S(1)}, u32[]{:S(2)}, u32[]{:S(2)}) collective-permute-start(bf16[128,512]{1,0:T(8,128)(2,1)S(1)} %get-tuple-element.61), channel_id=1, source_target_pairs={{0,64},{64,128},{128,192},{192,0},{1,65},{65,129},{129,193},{193,1... | collective-permute-start | bytes 393224 | tf_op jit(solution)/shard_map/ppermute | solution.py:415
  26.8 0.8 dynamic_slice.15
  27.6 0.6 pad_add_fusion.place_ref
  28.2 17.3 %collective-permute-done.3 = bf16[128,512]{1,0:T(8,128)(2,1)S(1)} collective-permute-done((bf16[128,512]{1,0:T(8,128)(2,1)S(1)}, bf16[128,512]{1,0:T(8,128)(2,1)S(1)}, u32[]{:S(2)}, u32[]{:S(2)}) %collective-permute-start.3) | collective-permute-done | bytes 131104 | tf_op jit(solution)/shard_map/ppermute | solution.py:415
  45.4 0.0 collective-permute-done.2
  45.4 0.8 collective-permute-done.1
  46.2 0.7 broadcast_in_dim.2.skip_ref
  47.0 0.0 copy-start
  47.0 0.0 collective-permute-done.5.refs_3_
  47.0 0.0 collective-permute-done.refs_1_
  47.0 0.0 all-to-all-done.fields_ref
  47.0 7.2 %conv.1 = (f32[32,32,128]{2,1,0:T(8,128)}, f32[4,2,528,128]{3,2,1,0:T(8,128)}, bf16[4,4,32,1024]{3,2,1,0:T(8,128)(2,1)}) custom-call(bf16[32,3,32,128]{3,2,1,0:T(8,128)(2,1)} %all-to-all-done.fields_ref, f32[32,128]{1,0:T(8,128)} %broadcast_in_dim.2.skip_ref, f32[592,128]{1,0:T(8,128)} %constant.74.clone.table_ref), custom_call_target="tpu_custom_call" | custom-call | flops 1000000000 | bytes 6291456 | tf_op jit(solution)/shard_map/conv/pallas_call | solution.py:185
  54.3 7.3 %all-to-all-start.2 = ((bf16[16,32,1024]{2,1,0:T(8,128)(2,1)}), bf16[16,32,1024]{2,1,0:T(8,128)(2,1)}, u32[]{:S(2)}, u32[]{:S(2)}) async-start(bf16[16,32,1024]{2,1,0:T(8,128)(2,1)} %bitcast.15), calls=%async_computation.2 | async-start | bytes 2097152 | tf_op jit(solution)/shard_map/all_to_all | solution.py:451
  61.6 0.0 copy-done.2
  61.6 2.9 %collective-permute-start.4 = (bf16[1024,256]{1,0:T(8,128)(2,1)S(1)}, bf16[1024,256]{1,0:T(8,128)(2,1)S(1)}, u32[]{:S(2)}, u32[]{:S(2)}) collective-permute-start(bf16[1024,256]{1,0:T(8,128)(2,1)S(1)} %copy-done.2), channel_id=1, source_target_pairs={{0,32},{16,48},{32,0},{48,16},{1,33},{17,49},{33,1},{49,17},{2,34}... | collective-permute-start | bytes 1572872 | tf_op jit(solution)/shard_map/ppermute | solution.py:415
  64.5 2.9 %collective-permute-start.8 = (bf16[3,128,512]{2,1,0:T(8,128)(2,1)S(1)}, bf16[3,128,512]{2,1,0:T(8,128)(2,1)S(1)}, u32[]{:S(2)}, u32[]{:S(2)}) collective-permute-start(bf16[3,128,512]{2,1,0:T(8,128)(2,1)S(1)} %pad_maximum_fusion.refs_8_), channel_id=1, source_target_pairs={{0,2},{1,3},{2,0},{3,1},{4,6},{5,7},{6,4},{7,5},{8,10},{9,11},{10,... | collective-permute-start | bytes 1179656 | tf_op jit(solution)/shard_map/ppermute | solution.py:415
  67.4 0.8 collective-permute-start.7
  68.2 0.0 copy-done
  68.2 0.7 collective-permute-start.6
  68.9 6.0 %collective-permute-done.8.refs_10_ = bf16[3,128,512]{2,1,0:T(8,128)(2,1)S(1)} collective-permute-done((bf16[3,128,512]{2,1,0:T(8,128)(2,1)S(1)}, bf16[3,128,512]{2,1,0:T(8,128)(2,1)S(1)}, u32[]{:S(2)}, u32[]{:S(2)}) %collective-permute-start.8) | collective-permute-done | bytes 393248 | tf_op jit(solution)/shard_map/ppermute | solution.py:415
  74.9 9.9 %collective-permute-done.7.refs_11_ = bf16[3,128,512]{2,1,0:T(8,128)(2,1)S(1)} collective-permute-done((bf16[3,128,512]{2,1,0:T(8,128)(2,1)S(1)}, bf16[3,128,512]{2,1,0:T(8,128)(2,1)S(1)}, u32[]{:S(2)}, u32[]{:S(2)}) %collective-permute-start.7) | collective-permute-done | bytes 393248 | tf_op jit(solution)/shard_map/ppermute | solution.py:415
  84.8 0.7 collective-permute-done.6.refs_9_
  85.5 1.9 %collective-permute-done.4.refs_2_ = bf16[1024,256]{1,0:T(8,128)(2,1)S(1)} collective-permute-done((bf16[1024,256]{1,0:T(8,128)(2,1)S(1)}, bf16[1024,256]{1,0:T(8,128)(2,1)S(1)}, u32[]{:S(2)}, u32[]{:S(2)}) %collective-permute-start.4) | collective-permute-done | bytes 524320 | tf_op jit(solution)/shard_map/ppermute | solution.py:415
  87.5 2.4 %collective-permute-start.9 = (bf16[1024,256]{1,0:T(8,128)(2,1)S(1)}, bf16[1024,256]{1,0:T(8,128)(2,1)S(1)}, u32[]{:S(2)}, u32[]{:S(2)}) collective-permute-start(bf16[1024,256]{1,0:T(8,128)(2,1)S(1)} %copy-done.2), channel_id=1, source_target_pairs={{0,8},{8,0},{1,9},{9,1},{2,10},{10,2},{3,11},{11,3},{4,12},{12,4},... | collective-permute-start | bytes 1572872 | tf_op jit(solution)/shard_map/ppermute | solution.py:415
  89.9 0.0 collective-permute-start.10
  89.9 0.5 collective-permute-start.11
  90.4 0.0 collective-permute-start.12
  90.4 1.7 collective-permute-done.9.refs_4_
  92.2 0.9 collective-permute-done.10.refs_5_
  93.0 0.7 collective-permute-done.11.refs_6_
  93.7 0.0 copy-done.4
  93.7 0.1 copy-done.5
  93.8 0.8 copy-done.6
  94.6 0.0 collective-permute-done.12.refs_7_
  94.6 7.2 %mix.1 = (bf16[1024,512]{1,0:T(8,128)(2,1)}, bf16[4,4,128,256]{3,2,1,0:T(8,128)(2,1)}, bf16[4,4,128,256]{3,2,1,0:T(8,128)(2,1)}) custom-call(s32[4]{0:T(128)} %pad_add_fusion.place_ref, bf16[128,8192]{1,0:T(8,128)(2,1)} %grad_out_ref.1, bf16[1024,256]{1,0:T(8,128)(2,1)} %refs_0_, bf16[1024,256]{1,0:T(8,128)(2,1)} %collective-permute-done.refs_1_, ...), custom_call_target="tpu_custom_call" | custom-call | flops 2147483648 | bytes 9437184 | tf_op jit(solution)/shard_map/mix/pallas_call | solution.py:349
  101.8 0.0 all-to-all-done.2.mixed_near
  101.8 8.1 %all-to-all-start.1 = ((bf16[32,32,512]{2,1,0:T(8,128)(2,1)}), bf16[32,32,512]{2,1,0:T(8,128)(2,1)}, u32[]{:S(2)}, u32[]{:S(2)}) async-start(bf16[32,32,512]{2,1,0:T(8,128)(2,1)} %bitcast.14), calls=%async_computation.1 | async-start | bytes 2097152 | tf_op jit(solution)/shard_map/all_to_all | solution.py:421
  109.9 0.4 collective-permute-start.14
  110.3 0.2 collective-permute-start.13
  110.5 0.6 stack.64.cols_ref
  111.1 1.7 collective-permute-done.14.far
  112.8 1.7 collective-permute-done.13.mixed_far
  114.5 4.8 %product.2 = (bf16[16,2,32,256]{3,2,1,0:T(8,128)(2,1)}, bf16[16,2,32,256]{3,2,1,0:T(8,128)(2,1)}, bf16[16,2,32,256]{3,2,1,0:T(8,128)(2,1)}) custom-call(s32[5]{0:T(128)} %stack.64.cols_ref, bf16[16,32,1024]{2,1,0:T(8,128)(2,1)} %all-to-all-done.2.mixed_near, bf16[16,32,1024]{2,1,0:T(8,128)(2,1)} %collective-permute-done.13.mixed_far, ...), custom_call_target="tpu_custom_call" | custom-call | flops 1610612736 | bytes 5242880 | tf_op jit(solution)/shard_map/product/pallas_call | solution.py:391
  119.3 1.4 collective-permute-start.15
  120.7 1.3 collective-permute-start.16
  122.0 16.8 %all-to-all-done.1.parts_ref = bf16[32,32,512]{2,1,0:T(8,128)(2,1)} async-done(((bf16[32,32,512]{2,1,0:T(8,128)(2,1)}), bf16[32,32,512]{2,1,0:T(8,128)(2,1)}, u32[]{:S(2)}, u32[]{:S(2)}) %all-to-all-start.1) | async-done | bytes 1048608 | tf_op jit(solution)/shard_map/all_to_all | solution.py:421
  138.9 2.2 %collective-permute-done.15.refs_0_ = bf16[16,2,32,256]{3,2,1,0:T(8,128)(2,1)} collective-permute-done((bf16[16,2,32,256]{3,2,1,0:T(8,128)(2,1)}, bf16[16,2,32,256]{3,2,1,0:T(8,128)(2,1)}, u32[]{:S(2)}, u32[]{:S(2)}) %collective-permute-start.15) | collective-permute-done | bytes 524320 | tf_op jit(solution)/shard_map/ppermute | solution.py:415
  141.0 0.0 collective-permute-done.16.refs_1_
  141.0 7.4 %corr.1 = bf16[32,3,32,128]{3,2,1,0:T(8,128)(2,1)} custom-call(bf16[32,32,512]{2,1,0:T(8,128)(2,1)} %all-to-all-done.1.parts_ref, bf16[32,3,32,128]{3,2,1,0:T(8,128)(2,1)} %all-to-all-done.fields_ref, f32[32,32,128]{2,1,0:T(8,128)} %get-tuple-element.40.total_ref, f32[4,2,528,128]{3,2,1,0:T(8,128)} %get-tuple-element.52.spec_ref, ...), custom_call_target="tpu_custom_call" | custom-call | flops 1000000000 | bytes 6291456 | tf_op jit(solution)/shard_map/corr/pallas_call | solution.py:213
  148.4 7.9 %all-to-all-start.3 = ((bf16[32,3,32,128]{3,2,1,0:T(8,128)(2,1)}), bf16[32,3,32,128]{3,2,1,0:T(8,128)(2,1)}, u32[]{:S(2)}, u32[]{:S(2)}) async-start(bf16[32,3,32,128]{3,2,1,0:T(8,128)(2,1)} %corr.1), calls=%async_computation.3 | async-start | bytes 1572864 | tf_op jit(solution)/shard_map/all_to_all | solution.py:421
  156.3 3.0 %collective-permute-start.17 = (bf16[16,2,32,256]{3,2,1,0:T(8,128)(2,1)}, bf16[16,2,32,256]{3,2,1,0:T(8,128)(2,1)}, u32[]{:S(2)}, u32[]{:S(2)}) collective-permute-start(bf16[16,2,32,256]{3,2,1,0:T(8,128)(2,1)} %get-tuple-element.58), channel_id=1, source_target_pairs={{0,32},{16,48},{32,0},{48,16},{1,33},{17,49},{33,1},{49,17},{2,34}... | collective-permute-start | bytes 1572872 | tf_op jit(solution)/shard_map/ppermute | solution.py:415
  159.3 0.6 stack.65.cols_ref
  159.9 4.2 %product.3 = f32[16,2,32,256]{3,2,1,0:T(8,128)} custom-call(s32[5]{0:T(128)} %stack.65.cols_ref, bf16[16,32,1024]{2,1,0:T(8,128)(2,1)} %all-to-all-done.2.mixed_near, bf16[16,32,1024]{2,1,0:T(8,128)(2,1)} %collective-permute-done.13.mixed_far, bf16[4,4,128,256]{3,2,1,0:T(8,128)(2,1)} %get-tuple-element.47.near, ...), custom_call_target="tpu_custom_call" | custom-call | flops 536870912 | bytes 5242880 | tf_op jit(solution)/shard_map/product/pallas_call | solution.py:391
  164.1 16.0 %collective-permute-done.17 = bf16[16,2,32,256]{3,2,1,0:T(8,128)(2,1)} collective-permute-done((bf16[16,2,32,256]{3,2,1,0:T(8,128)(2,1)}, bf16[16,2,32,256]{3,2,1,0:T(8,128)(2,1)}, u32[]{:S(2)}, u32[]{:S(2)}) %collective-permute-start.17) | collective-permute-done | bytes 524320 | tf_op jit(solution)/shard_map/ppermute | solution.py:415
  180.1 2.3 %multiply_convert_fusion = bf16[16,2,32,256]{3,2,1,0:T(8,128)(2,1)} fusion(f32[16,2,32,256]{3,2,1,0:T(8,128)} %product.3, bf16[16,2,32,256]{3,2,1,0:T(8,128)(2,1)} %collective-permute-done.17), kind=kLoop, calls=%fused_computation | loop fusion | flops 1048576 | bytes 2097152 | tf_op jit(solution)/shard_map/convert_element_type | solution.py:478
  182.4 0.0 all-to-all-done.3.corr_ref
  182.4 2.2 %last.1 = (bf16[128,1024]{1,0:T(8,128)(2,1)}, bf16[128,1024]{1,0:T(8,128)(2,1)}, bf16[128,1024]{1,0:T(8,128)(2,1)}, bf16[128,1024]{1,0:T(8,128)(2,1)}) custom-call(bf16[32,3,32,128]{3,2,1,0:T(8,128)(2,1)} %all-to-all-done.3.corr_ref, bf16[128,1024]{1,0:T(8,128)(2,1)} %key_ref.3, bf16[128,1024]{1,0:T(8,128)(2,1)} %value_ref.3), custom_call_target="tpu_custom_call" | custom-call | flops 10000000 | bytes 3145728 | tf_op jit(solution)/shard_map/last/pallas_call | solution.py:275
  (15 shorter events, 0.1 us)
Async XLA Ops:
  2.9 44.1 %all-to-all-start = ((bf16[32,3,32,128]{3,2,1,0:T(8,128)(2,1)}), bf16[32,3,32,128]{3,2,1,0:T(8,128)(2,1)}, u32[]{:S(2)}, u32[]{:S(2)}) async-start(bf16[32,3,32,128]{3,2,1,0:T(8,128)(2,1)} %prep.1), calls=%async_computation | async-start | bytes 1572864 | tf_op jit(solution)/shard_map/all_to_all | solution.py:421
  15.5 31.5 %collective-permute-start.5 = (bf16[1024,256]{1,0:T(8,128)(2,1)}, bf16[1024,256]{1,0:T(8,128)(2,1)}, u32[]{:S(2)}, u32[]{:S(2)}) collective-permute-start(bf16[1024,256]{1,0:T(8,128)(2,1)} %refs_0_), channel_id=1, source_target_pairs={{0,48},{16,0},{32,16},{48,32},{1,49},{17,1},{33,17},{49,33},{2,50}... | collective-permute-start | bytes 1572872 | tf_op jit(solution)/shard_map/ppermute | solution.py:415
  18.2 28.8 %collective-permute-start = (bf16[1024,256]{1,0:T(8,128)(2,1)}, bf16[1024,256]{1,0:T(8,128)(2,1)}, u32[]{:S(2)}, u32[]{:S(2)}) collective-permute-start(bf16[1024,256]{1,0:T(8,128)(2,1)} %refs_0_), channel_id=1, source_target_pairs={{0,16},{16,32},{32,48},{48,0},{1,17},{17,33},{33,49},{49,1},{2,18}... | collective-permute-start | bytes 1572872 | tf_op jit(solution)/shard_map/ppermute | solution.py:415
  19.2 26.2 %collective-permute-start.3 = (bf16[128,512]{1,0:T(8,128)(2,1)S(1)}, bf16[128,512]{1,0:T(8,128)(2,1)S(1)}, u32[]{:S(2)}, u32[]{:S(2)}) collective-permute-start(bf16[128,512]{1,0:T(8,128)(2,1)S(1)} %get-tuple-element.59), channel_id=1, source_target_pairs={{0,192},{64,0},{128,64},{192,128},{1,193},{65,1},{129,65},{193,129... | collective-permute-start | bytes 393224 | tf_op jit(solution)/shard_map/ppermute | solution.py:415
  22.7 22.7 %collective-permute-start.2 = (bf16[128,512]{1,0:T(8,128)(2,1)S(1)}, bf16[128,512]{1,0:T(8,128)(2,1)S(1)}, u32[]{:S(2)}, u32[]{:S(2)}) collective-permute-start(bf16[128,512]{1,0:T(8,128)(2,1)S(1)} %get-tuple-element.60), channel_id=1, source_target_pairs={{0,128},{64,192},{128,0},{192,64},{1,129},{65,193},{129,1},{193,65... | collective-permute-start | bytes 393224 | tf_op jit(solution)/shard_map/ppermute | solution.py:415
  24.7 21.5 %collective-permute-start.1 = (bf16[128,512]{1,0:T(8,128)(2,1)S(1)}, bf16[128,512]{1,0:T(8,128)(2,1)S(1)}, u32[]{:S(2)}, u32[]{:S(2)}) collective-permute-start(bf16[128,512]{1,0:T(8,128)(2,1)S(1)} %get-tuple-element.61), channel_id=1, source_target_pairs={{0,64},{64,128},{128,192},{192,0},{1,65},{65,129},{129,193},{193,1... | collective-permute-start | bytes 393224 | tf_op jit(solution)/shard_map/ppermute | solution.py:415
  47.0 21.2 %copy-start = (bf16[3,128,512]{2,1,0:T(8,128)(2,1)}, bf16[3,128,512]{2,1,0:T(8,128)(2,1)S(1)}, u32[]{:S(2)}) copy-start(bf16[3,128,512]{2,1,0:T(8,128)(2,1)S(1)} %pad_maximum_fusion.refs_8_) | copy-start | bytes 1179652
  54.3 7.3 %copy-start.2 = (bf16[1024,256]{1,0:T(8,128)(2,1)S(1)}, bf16[1024,256]{1,0:T(8,128)(2,1)}, u32[]{:S(2)}) copy-start(bf16[1024,256]{1,0:T(8,128)(2,1)} %refs_0_) | copy-start | bytes 1572868
  54.3 47.6 %all-to-all-start.2 = ((bf16[16,32,1024]{2,1,0:T(8,128)(2,1)}), bf16[16,32,1024]{2,1,0:T(8,128)(2,1)}, u32[]{:S(2)}, u32[]{:S(2)}) async-start(bf16[16,32,1024]{2,1,0:T(8,128)(2,1)} %bitcast.15), calls=%async_computation.2 | async-start | bytes 2097152 | tf_op jit(solution)/shard_map/all_to_all | solution.py:451
  61.6 25.9 %collective-permute-start.4 = (bf16[1024,256]{1,0:T(8,128)(2,1)S(1)}, bf16[1024,256]{1,0:T(8,128)(2,1)S(1)}, u32[]{:S(2)}, u32[]{:S(2)}) collective-permute-start(bf16[1024,256]{1,0:T(8,128)(2,1)S(1)} %copy-done.2), channel_id=1, source_target_pairs={{0,32},{16,48},{32,0},{48,16},{1,33},{17,49},{33,1},{49,17},{2,34}... | collective-permute-start | bytes 1572872 | tf_op jit(solution)/shard_map/ppermute | solution.py:415
  64.5 10.4 %collective-permute-start.8 = (bf16[3,128,512]{2,1,0:T(8,128)(2,1)S(1)}, bf16[3,128,512]{2,1,0:T(8,128)(2,1)S(1)}, u32[]{:S(2)}, u32[]{:S(2)}) collective-permute-start(bf16[3,128,512]{2,1,0:T(8,128)(2,1)S(1)} %pad_maximum_fusion.refs_8_), channel_id=1, source_target_pairs={{0,2},{1,3},{2,0},{3,1},{4,6},{5,7},{6,4},{7,5},{8,10},{9,11},{10,... | collective-permute-start | bytes 1179656 | tf_op jit(solution)/shard_map/ppermute | solution.py:415
  67.4 17.4 %collective-permute-start.7 = (bf16[3,128,512]{2,1,0:T(8,128)(2,1)S(1)}, bf16[3,128,512]{2,1,0:T(8,128)(2,1)S(1)}, u32[]{:S(2)}, u32[]{:S(2)}) collective-permute-start(bf16[3,128,512]{2,1,0:T(8,128)(2,1)S(1)} %pad_maximum_fusion.refs_8_), channel_id=1, source_target_pairs={{0,3},{1,0},{2,1},{3,2},{4,7},{5,4},{6,5},{7,6},{8,11},{9,8},{10,9... | collective-permute-start | bytes 1179656 | tf_op jit(solution)/shard_map/ppermute | solution.py:415
  68.2 17.3 %collective-permute-start.6 = (bf16[3,128,512]{2,1,0:T(8,128)(2,1)S(1)}, bf16[3,128,512]{2,1,0:T(8,128)(2,1)S(1)}, u32[]{:S(2)}, u32[]{:S(2)}) collective-permute-start(bf16[3,128,512]{2,1,0:T(8,128)(2,1)S(1)} %pad_maximum_fusion.refs_8_), channel_id=1, source_target_pairs={{0,1},{1,2},{2,3},{3,0},{4,5},{5,6},{6,7},{7,4},{8,9},{9,10},{10,1... | collective-permute-start | bytes 1179656 | tf_op jit(solution)/shard_map/ppermute | solution.py:415
  74.9 18.8 %copy-start.7 = (bf16[3,128,512]{2,1,0:T(8,128)(2,1)}, bf16[3,128,512]{2,1,0:T(8,128)(2,1)S(1)}, u32[]{:S(2)}) copy-start(bf16[3,128,512]{2,1,0:T(8,128)(2,1)S(1)} %collective-permute-done.8.refs_10_) | copy-start | bytes 1179652
  84.8 8.9 %copy-start.8 = (bf16[3,128,512]{2,1,0:T(8,128)(2,1)}, bf16[3,128,512]{2,1,0:T(8,128)(2,1)S(1)}, u32[]{:S(2)}) copy-start(bf16[3,128,512]{2,1,0:T(8,128)(2,1)S(1)} %collective-permute-done.7.refs_11_) | copy-start | bytes 1179652
  85.5 8.2 %copy-start.9 = (bf16[3,128,512]{2,1,0:T(8,128)(2,1)}, bf16[3,128,512]{2,1,0:T(8,128)(2,1)S(1)}, u32[]{:S(2)}) copy-start(bf16[3,128,512]{2,1,0:T(8,128)(2,1)S(1)} %collective-permute-done.6.refs_9_) | copy-start | bytes 1179652
  87.5 4.7 %copy-start.3 = (bf16[1024,256]{1,0:T(8,128)(2,1)}, bf16[1024,256]{1,0:T(8,128)(2,1)S(1)}, u32[]{:S(2)}) copy-start(bf16[1024,256]{1,0:T(8,128)(2,1)S(1)} %collective-permute-done.4.refs_2_) | copy-start | bytes 1572868
  87.5 4.7 %collective-permute-start.9 = (bf16[1024,256]{1,0:T(8,128)(2,1)S(1)}, bf16[1024,256]{1,0:T(8,128)(2,1)S(1)}, u32[]{:S(2)}, u32[]{:S(2)}) collective-permute-start(bf16[1024,256]{1,0:T(8,128)(2,1)S(1)} %copy-done.2), channel_id=1, source_target_pairs={{0,8},{8,0},{1,9},{9,1},{2,10},{10,2},{3,11},{11,3},{4,12},{12,4},... | collective-permute-start | bytes 1572872 | tf_op jit(solution)/shard_map/ppermute | solution.py:415
  89.9 3.1 %collective-permute-start.10 = (bf16[1024,256]{1,0:T(8,128)(2,1)}, bf16[1024,256]{1,0:T(8,128)(2,1)S(1)}, u32[]{:S(2)}, u32[]{:S(2)}) collective-permute-start(bf16[1024,256]{1,0:T(8,128)(2,1)} %collective-permute-done.refs_1_), channel_id=1, source_target_pairs={{0,8},{8,0},{1,9},{9,1},{2,10},{10,2},{3,11},{11,3},{4,12},{12,4},... | collective-permute-start | bytes 1572872 | tf_op jit(solution)/shard_map/ppermute | solution.py:415
  89.9 3.8 %collective-permute-start.11 = (bf16[1024,256]{1,0:T(8,128)(2,1)S(1)}, bf16[1024,256]{1,0:T(8,128)(2,1)S(1)}, u32[]{:S(2)}, u32[]{:S(2)}) collective-permute-start(bf16[1024,256]{1,0:T(8,128)(2,1)S(1)} %collective-permute-done.4.refs_2_), channel_id=1, source_target_pairs={{0,8},{8,0},{1,9},{9,1},{2,10},{10,2},{3,11},{11,3},{4,12},{12,4},... | collective-permute-start | bytes 1572872 | tf_op jit(solution)/shard_map/ppermute | solution.py:415
  90.4 4.2 %collective-permute-start.12 = (bf16[1024,256]{1,0:T(8,128)(2,1)}, bf16[1024,256]{1,0:T(8,128)(2,1)}, u32[]{:S(2)}, u32[]{:S(2)}) collective-permute-start(bf16[1024,256]{1,0:T(8,128)(2,1)} %collective-permute-done.5.refs_3_), channel_id=1, source_target_pairs={{0,8},{8,0},{1,9},{9,1},{2,10},{10,2},{3,11},{11,3},{4,12},{12,4},... | collective-permute-start | bytes 1572872 | tf_op jit(solution)/shard_map/ppermute | solution.py:415
  92.2 1.5 copy-start.4
  93.0 0.8 copy-start.5
  93.8 0.8 copy-start.6
  101.8 8.1 %copy-start.1 = (bf16[4,4,128,256]{3,2,1,0:T(8,128)(2,1)S(1)}, bf16[4,4,128,256]{3,2,1,0:T(8,128)(2,1)}, u32[]{:S(2)}) copy-start(bf16[4,4,128,256]{3,2,1,0:T(8,128)(2,1)} %get-tuple-element.48) | copy-start | bytes 3145732
  101.8 37.0 %all-to-all-start.1 = ((bf16[32,32,512]{2,1,0:T(8,128)(2,1)}), bf16[32,32,512]{2,1,0:T(8,128)(2,1)}, u32[]{:S(2)}, u32[]{:S(2)}) async-start(bf16[32,32,512]{2,1,0:T(8,128)(2,1)} %bitcast.14), calls=%async_computation.1 | async-start | bytes 2097152 | tf_op jit(solution)/shard_map/all_to_all | solution.py:421
  109.9 2.9 %collective-permute-start.14 = (bf16[4,4,128,256]{3,2,1,0:T(8,128)(2,1)S(1)}, bf16[4,4,128,256]{3,2,1,0:T(8,128)(2,1)}, u32[]{:S(2)}, u32[]{:S(2)}) collective-permute-start(bf16[4,4,128,256]{3,2,1,0:T(8,128)(2,1)S(1)} %copy-done.1), channel_id=1, source_target_pairs={{0,8},{8,0},{1,9},{9,1},{2,10},{10,2},{3,11},{11,3},{4,12},{12,4},... | collective-permute-start | bytes 3145736 | tf_op jit(solution)/shard_map/ppermute | solution.py:415
  110.3 4.2 %collective-permute-start.13 = (bf16[16,32,1024]{2,1,0:T(8,128)(2,1)}, bf16[16,32,1024]{2,1,0:T(8,128)(2,1)}, u32[]{:S(2)}, u32[]{:S(2)}) collective-permute-start(bf16[16,32,1024]{2,1,0:T(8,128)(2,1)} %all-to-all-done.2.mixed_near), channel_id=1, source_target_pairs={{0,8},{8,0},{1,9},{9,1},{2,10},{10,2},{3,11},{11,3},{4,12},{12,4},... | collective-permute-start | bytes 3145736 | tf_op jit(solution)/shard_map/ppermute | solution.py:415
  119.3 21.7 %collective-permute-start.15 = (bf16[16,2,32,256]{3,2,1,0:T(8,128)(2,1)}, bf16[16,2,32,256]{3,2,1,0:T(8,128)(2,1)}, u32[]{:S(2)}, u32[]{:S(2)}) collective-permute-start(bf16[16,2,32,256]{3,2,1,0:T(8,128)(2,1)} %get-tuple-element.49), channel_id=1, source_target_pairs={{0,16},{16,32},{32,48},{48,0},{1,17},{17,33},{33,49},{49,1},{2,18}... | collective-permute-start | bytes 1572872 | tf_op jit(solution)/shard_map/ppermute | solution.py:415
  120.7 20.3 %collective-permute-start.16 = (bf16[16,2,32,256]{3,2,1,0:T(8,128)(2,1)}, bf16[16,2,32,256]{3,2,1,0:T(8,128)(2,1)}, u32[]{:S(2)}, u32[]{:S(2)}) collective-permute-start(bf16[16,2,32,256]{3,2,1,0:T(8,128)(2,1)} %get-tuple-element.50), channel_id=1, source_target_pairs={{0,48},{16,0},{32,16},{48,32},{1,49},{17,1},{33,17},{49,33},{2,50}... | collective-permute-start | bytes 1572872 | tf_op jit(solution)/shard_map/ppermute | solution.py:415
  148.4 34.1 %all-to-all-start.3 = ((bf16[32,3,32,128]{3,2,1,0:T(8,128)(2,1)}), bf16[32,3,32,128]{3,2,1,0:T(8,128)(2,1)}, u32[]{:S(2)}, u32[]{:S(2)}) async-start(bf16[32,3,32,128]{3,2,1,0:T(8,128)(2,1)} %corr.1), calls=%async_computation.3 | async-start | bytes 1572864 | tf_op jit(solution)/shard_map/all_to_all | solution.py:421
  156.3 23.8 %collective-permute-start.17 = (bf16[16,2,32,256]{3,2,1,0:T(8,128)(2,1)}, bf16[16,2,32,256]{3,2,1,0:T(8,128)(2,1)}, u32[]{:S(2)}, u32[]{:S(2)}) collective-permute-start(bf16[16,2,32,256]{3,2,1,0:T(8,128)(2,1)} %get-tuple-element.58), channel_id=1, source_target_pairs={{0,32},{16,48},{32,0},{48,16},{1,33},{17,49},{33,1},{49,17},{2,34}... | collective-permute-start | bytes 1572872 | tf_op jit(solution)/shard_map/ppermute | solution.py:415
